TPU v7x, 768 devices: a whole 4x8x12 slice. The times are simulated.
768 devices in a mesh: gx: 96 (over x, z, core), gy: 8 (over y).
Axes of the slice: x: 4, y: 8, z: 12, core: 2. Of those that a mesh axis runs over, the one named last changes fastest.
Arguments:
- depth: float32 [3072, 4096], P('gx', 'gy'), may hold values from 0.5 to 2
- discharge: float32 [2, 3072, 4096], P(None, 'gx', 'gy'), may hold values from -1.5 to 1.5
- roughness: float32 [3072, 4096], P('gx', 'gy'), may hold values from 0.03 to 0.15
- reach_state: float32 [768, 1024], P('gx'), may hold values from 0.5 to 2.5
- celerity: float32 [768, 8], P('gx'), may hold values from 0.05 to 0.75
- base_inflow: float32 [768, 8], P('gx'), may hold values from 0.5 to 2
- upstream: int32 [768, 2], P('gx'), may hold values from -1 to 759, as said below
- bank_cell: int32 [2304, 1024], P('gx', 'gy'), may hold values from -1 to 16383, as said below
- bank_site: int32 [2304, 1024], P('gx', 'gy'), may hold values from 0 to 1023
- bank_coeff: float32 [2304, 1024], P('gx', 'gy'), may hold values from 0.02 to 0.2
Outputs:
- plain_state: float32 [3, 3072, 4096], P(None, 'gx', 'gy')
- reach_final: float32 [768, 1024], P('gx')
Inputs may be any that keep to these rules, and one draw needn't show every extreme that they name: `upstream`: of the basins of each gx index g >= 1, a half lists two basins of gx index g - 1 each and the others list -1 twice; the basins of gx index 0 list -1 twice; every basin other than those of the last gx index is listed exactly once. `bank_cell`: in every block of 128 slots the occupied ones come first; the blocks of basins outside the grid are empty.
All inputs are finite; a program needn't handle non-finite values.
Results may differ from a plain program's by a relative error of at most 0.0001.
Values sent between devices are 32-bit elements; how exact they have to be, the bound alone decides.
No kernel may reach another device: no remote copies, remote signals or barrier semaphores. Data moves between devices by JAX's collectives and lax.ppermute only.
A program may use at most 32 MiB of HBM per device.

v0:
```python
import jax
import jax.numpy as jnp
from jax import lax
from jax.sharding import PartitionSpec as P

STEPS = 4


GRAV = 9.81
DT = 0.5
DX = 10.0
NU = 0.1
RATIO = 0.25


def with_halo(cells, sides, width):
    for axis, dim in sides:
        count = lax.axis_size(axis)
        ends = count - 1
        head = lax.slice_in_dim(cells, 0, width, axis=dim)
        tail = lax.slice_in_dim(cells, cells.shape[dim] - width, cells.shape[dim], axis=dim)
        cells = jnp.concatenate(
            [
                lax.ppermute(tail, axis, [(i, (i + 1) % count) for i in range(ends)]),
                cells,
                lax.ppermute(head, axis, [((i + 1) % count, i) for i in range(ends)]),
            ],
            axis=dim,
        )
    return cells


def fluxes(state_cells):
    height = state_cells[0]
    velocity_x = state_cells[1] / height
    velocity_y = state_cells[2] / height
    pressure = 0.5 * GRAV * height * height
    flux_x = jnp.stack(
        [state_cells[1], state_cells[1] * velocity_x + pressure, state_cells[2] * velocity_x]
    )
    flux_y = jnp.stack(
        [state_cells[2], state_cells[1] * velocity_y, state_cells[2] * velocity_y + pressure]
    )
    return (flux_x, flux_y)


def flood_update(plain, roughness, source):
    padded = with_halo(plain, (("gx", 1), ("gy", 2)), 1)
    row_index = lax.axis_index("gx")
    col_index = lax.axis_index("gy")
    top_rows = jnp.where(row_index == 0, padded[:, 1:2, :], padded[:, 0:1, :])
    low_rows = jnp.where(
        row_index == lax.axis_size("gx") - 1, padded[:, -2:-1, :], padded[:, -1:, :]
    )
    padded = jnp.concatenate([top_rows, padded[:, 1:-1, :], low_rows], axis=1)
    left_cols = jnp.where(col_index == 0, padded[:, :, 1:2], padded[:, :, 0:1])
    right_cols = jnp.where(
        col_index == lax.axis_size("gy") - 1, padded[:, :, -2:-1], padded[:, :, -1:]
    )
    padded = jnp.concatenate([left_cols, padded[:, :, 1:-1], right_cols], axis=2)
    flux_x, flux_y = fluxes(padded)
    centre = padded[:, 1:-1, 1:-1]
    average = 0.25 * (
        padded[:, 2:, 1:-1] + padded[:, :-2, 1:-1] + padded[:, 1:-1, 2:] + padded[:, 1:-1, :-2]
    )
    factor = DT / (2.0 * DX)
    updated = (
        average
        - factor * (flux_x[:, 2:, 1:-1] - flux_x[:, :-2, 1:-1])
        - factor * (flux_y[:, 1:-1, 2:] - flux_y[:, 1:-1, :-2])
    )
    height = centre[0]
    velocity_x = centre[1] / height
    velocity_y = centre[2] / height
    flow_speed = jnp.sqrt(velocity_x * velocity_x + velocity_y * velocity_y)
    drag_rate = GRAV * roughness * roughness * flow_speed / jnp.cbrt(height)
    return updated + DT * jnp.stack([source, -drag_rate * velocity_x, -drag_rate * velocity_y])


def river_update(reach_now, prev_block, linked, celerity, base_inflow, lateral):
    per_row = reach_now.shape[0]
    fields = celerity.shape[1]
    stations = reach_now.shape[1] // fields
    current = reach_now.reshape(per_row, fields, stations)
    prev_last = prev_block.reshape(per_row, fields, stations)[:, :, -1]
    inflow = base_inflow + jnp.einsum(
        "bmu,uf->bf", linked, prev_last, precision=lax.Precision.HIGHEST
    )
    behind = jnp.concatenate([inflow[:, :, None], current[:, :, :-1]], axis=2)
    sides = jnp.concatenate([current[:, :1], current, current[:, -1:]], axis=1)
    mixing = sides[:, 2:] - 2.0 * current + sides[:, :-2]
    updated = (
        current
        - celerity[:, :, None] * (current - behind)
        + NU * mixing
        - DT * RATIO * lateral.reshape(per_row, fields, stations)
    )
    return updated.reshape(per_row, fields * stations)


def per_device(
    depth,
    discharge,
    roughness,
    reach_state,
    celerity,
    base_inflow,
    upstream,
    bank_cell,
    bank_site,
    bank_coeff,
):
    rows_dev, cols_dev = depth.shape
    cell_total = rows_dev * cols_dev
    per_row = reach_state.shape[0]
    site_count = reach_state.shape[1]
    row_index = lax.axis_index("gx")
    plain = jnp.concatenate([depth[None], discharge], axis=0)
    reach_now = reach_state
    prev_ids = (row_index - 1) * per_row + jnp.arange(per_row, dtype=jnp.int32)
    linked = (upstream[:, :, None] == prev_ids[None, None, :]).astype(jnp.float32)
    occupied = bank_cell >= 0
    cell_flat = jnp.where(occupied, bank_cell, cell_total)
    cell_read = jnp.minimum(cell_flat, cell_total - 1)
    block_ids = jnp.broadcast_to(jnp.arange(3 * per_row, dtype=jnp.int32)[:, None], bank_site.shape)
    for step_index in range(STEPS):
        reach_all = with_halo(reach_now, (("gx", 0),), per_row)
        river_segment = jnp.take_along_axis(reach_all, bank_site, axis=1)
        cell_depth = plain[0].reshape(-1)[cell_read]
        rates = jnp.where(occupied, bank_coeff * (river_segment - cell_depth), 0.0)
        source = (
            jnp.zeros((cell_total,), jnp.float32)
            .at[cell_flat.reshape(-1)]
            .add(rates.reshape(-1), mode="drop")
            .reshape(rows_dev, cols_dev)
        )
        partial_value = (
            jnp.zeros((3 * per_row, site_count), jnp.float32).at[block_ids, bank_site].add(rates)
        )
        totals = lax.psum(partial_value, "gy")
        edges = jnp.concatenate([totals[:per_row], totals[2 * per_row :]], axis=0)
        widened = with_halo(edges, (("gx", 0),), per_row)
        lateral = totals[per_row : 2 * per_row] + widened[:per_row] + widened[-per_row:]
        plain_next = flood_update(plain, roughness, source)
        reach_now = river_update(
            reach_now, reach_all[:per_row], linked, celerity, base_inflow, lateral
        )
        plain = plain_next
    return (plain, reach_now)


def solution(mesh):
    return jax.shard_map(
        per_device,
        mesh=mesh,
        in_specs=(
            P("gx", "gy"),
            P(None, "gx", "gy"),
            P("gx", "gy"),
            P("gx", None),
            P("gx", None),
            P("gx", None),
            P("gx", None),
            P("gx", "gy"),
            P("gx", "gy"),
            P("gx", "gy"),
        ),
        out_specs=(P(None, "gx", "gy"), P("gx", None)),
        check_vma=False,
    )
```

profile of v0, /device:TPU:6, one launch (start us, length us, event | category | flops | bytes accessed | tf_op | source)
XLA Modules:
  0.0 778.8 jit_solution(10998246891515317064)
XLA Ops:
  7.2 14.4 %collective-permute-start.5 = (f32[8,1024]{1,0:T(8,128)}, f32[8,1024]{1,0:T(8,128)S(1)}, u32[]{:S(2)}, u32[]{:S(2)}) collective-permute-start(f32[8,1024]{1,0:T(8,128)} %param.15), channel_id=1, source_target_pairs={{8,0},{16,8},{24,16},{32,24},{40,32},{48,40},{56,48},{64,56},{72,6... | collective-permute-start | bytes 98312 | tf_op jit(solution)/shard_map/ppermute | solution.py:26
  24.4 5.8 collective-permute-start.1
  38.6 4.5 collective-permute-start.2
  43.3 17.4 %gather_fusion = f32[3072]{0:T(1024)S(1)} fusion(f32[16384]{0:T(1024)S(1)} %bitcast.238, s32[3072]{0:T(1024)S(1)} %get-tuple-element.11), kind=kCustom, calls=%fused_computation.4 | custom fusion | bytes 36864 | tf_op jit(solution)/shard_map/gather | solution.py:129
  61.8 24.7 %gather_fusion.4 = f32[3072]{0:T(1024)S(1)} fusion(f32[24,1024]{1,0:T(8,128)S(1)} %pad_maximum_fusion.36, s32[3072]{0:T(1024)S(1)} %fusion.128), kind=kCustom, calls=%fused_computation.clone | custom fusion | bytes 49152 | tf_op jit(solution)/shard_map/jit(take_along_axis)/gather | solution.py:128
  86.6 16.6 %scatter_custom_fusion = f32[16384]{0:T(1024)S(1)} fusion(s32[3072]{0:T(1024)S(1)} %bitcast.271, f32[3072]{0:T(1024)S(1)} %get-tuple-element.9, f32[]{:T(128)} %constant.8.clone.1), kind=kCustom, calls=%fused_computation.276 | custom fusion | flops 3072 | bytes 65540 | tf_op jit(solution)/shard_map/scatter-add | solution.py:134
  108.4 17.4 %gather_fusion.1 = f32[3072]{0:T(1024)S(1)} fusion(f32[16384]{0:T(1024)S(1)} %bitcast.239, s32[3072]{0:T(1024)S(1)} %get-tuple-element.11), kind=kCustom, calls=%fused_computation.5 | custom fusion | bytes 36864 | tf_op jit(solution)/shard_map/gather | solution.py:129
  125.8 21.7 %scatter_custom_fusion.4 = f32[24576]{0:T(1024)S(1)} fusion(s32[3072]{0:T(1024)S(1)} %select_bitcast_fusion, f32[3072]{0:T(1024)S(1)} %get-tuple-element.9, f32[]{:T(128)} %constant.8.clone.1), kind=kCustom, calls=%fused_computation.193 | custom fusion | flops 3072 | bytes 98308
  149.9 4.5 collective-permute-start.8
  157.3 70.0 %all-reduce.5.cloned.1.call-done = f32[24,1024]{1,0:T(8,128)} async-done(((f32[24,1024]{1,0:T(8,128)}), f32[24,1024]{1,0:T(8,128)}) %all-reduce.5.cloned.1.call-update) | async-done | bytes 98320 | tf_op jit(solution)/shard_map/psum | solution.py:140
  232.5 6.1 collective-permute-done.10
  243.8 4.9 collective-permute-done.12
  248.8 24.7 %gather_fusion.5 = f32[3072]{0:T(1024)S(1)} fusion(f32[24,1024]{1,0:T(8,128)S(1)} %pad_maximum_fusion.37, s32[3072]{0:T(1024)S(1)} %fusion.128), kind=kCustom, calls=%fused_computation.1.clone | custom fusion | bytes 49152 | tf_op jit(solution)/shard_map/jit(take_along_axis)/gather | solution.py:128
  273.5 16.6 %scatter_custom_fusion.1 = f32[16384]{0:T(1024)S(1)} fusion(s32[3072]{0:T(1024)S(1)} %bitcast.272, f32[3072]{0:T(1024)S(1)} %fusion.124, f32[]{:T(128)} %constant.8.clone.1), kind=kCustom, calls=%fused_computation.274 | custom fusion | flops 3072 | bytes 65540 | tf_op jit(solution)/shard_map/scatter-add | solution.py:134
  290.8 21.7 %scatter_custom_fusion.5 = f32[24576]{0:T(1024)S(1)} fusion(s32[3072]{0:T(1024)S(1)} %select_bitcast_fusion, f32[3072]{0:T(1024)S(1)} %fusion.124, f32[]{:T(128)} %constant.8.clone.1), kind=kCustom, calls=%fused_computation.191 | custom fusion | flops 3072 | bytes 98308
  316.9 17.4 %gather_fusion.2 = f32[3072]{0:T(1024)S(1)} fusion(f32[16384]{0:T(1024)S(1)} %bitcast.240, s32[3072]{0:T(1024)S(1)} %get-tuple-element.11), kind=kCustom, calls=%fused_computation.6 | custom fusion | bytes 36864 | tf_op jit(solution)/shard_map/gather | solution.py:129
  336.8 4.5 collective-permute-start.16
  344.3 68.6 %all-reduce.7.cloned.1.call-done = f32[24,1024]{1,0:T(8,128)} async-done(((f32[24,1024]{1,0:T(8,128)}), f32[24,1024]{1,0:T(8,128)}) %all-reduce.7.cloned.1.call-update) | async-done | bytes 98320 | tf_op jit(solution)/shard_map/psum | solution.py:140
  418.0 6.1 collective-permute-done.18
  429.4 4.9 collective-permute-done.20
  434.3 24.7 %gather_fusion.6 = f32[3072]{0:T(1024)S(1)} fusion(f32[24,1024]{1,0:T(8,128)S(1)} %pad_maximum_fusion.38, s32[3072]{0:T(1024)S(1)} %fusion.128), kind=kCustom, calls=%fused_computation.2.clone | custom fusion | bytes 49152 | tf_op jit(solution)/shard_map/jit(take_along_axis)/gather | solution.py:128
  459.0 16.6 %scatter_custom_fusion.2 = f32[16384]{0:T(1024)S(1)} fusion(s32[3072]{0:T(1024)S(1)} %bitcast.273, f32[3072]{0:T(1024)S(1)} %fusion.121, f32[]{:T(128)} %constant.8.clone.1), kind=kCustom, calls=%fused_computation.272 | custom fusion | flops 3072 | bytes 65540 | tf_op jit(solution)/shard_map/scatter-add | solution.py:134
  476.3 21.7 %scatter_custom_fusion.6 = f32[24576]{0:T(1024)S(1)} fusion(s32[3072]{0:T(1024)S(1)} %select_bitcast_fusion, f32[3072]{0:T(1024)S(1)} %fusion.121, f32[]{:T(128)} %constant.8.clone.1), kind=kCustom, calls=%fused_computation.189 | custom fusion | flops 3072 | bytes 98308
  502.5 17.4 %gather_fusion.3 = f32[3072]{0:T(1024)S(1)} fusion(f32[16384]{0:T(1024)S(1)} %bitcast.237, s32[3072]{0:T(1024)S(1)} %get-tuple-element.11), kind=kCustom, calls=%fused_computation.7 | custom fusion | bytes 36864 | tf_op jit(solution)/shard_map/gather | solution.py:129
  529.6 68.8 %all-reduce.9.cloned.1.call-done = f32[24,1024]{1,0:T(8,128)} async-done(((f32[24,1024]{1,0:T(8,128)}), f32[24,1024]{1,0:T(8,128)}) %all-reduce.9.cloned.1.call-update) | async-done | bytes 98320 | tf_op jit(solution)/shard_map/psum | solution.py:140
  603.6 6.1 collective-permute-done.26
  614.9 4.9 collective-permute-done.28
  619.8 24.7 %gather_fusion.7 = f32[3072]{0:T(1024)S(1)} fusion(f32[24,1024]{1,0:T(8,128)S(1)} %pad_maximum_fusion.39, s32[3072]{0:T(1024)S(1)} %fusion.128), kind=kCustom, calls=%fused_computation.3.clone | custom fusion | bytes 49152 | tf_op jit(solution)/shard_map/jit(take_along_axis)/gather | solution.py:128
  644.6 16.6 %scatter_custom_fusion.3 = f32[16384]{0:T(1024)S(1)} fusion(s32[3072]{0:T(1024)S(1)} %bitcast.274, f32[3072]{0:T(1024)S(1)} %fusion.118, f32[]{:T(128)} %constant.8.clone.1), kind=kCustom, calls=%fused_computation.270 | custom fusion | flops 3072 | bytes 65540 | tf_op jit(solution)/shard_map/scatter-add | solution.py:134
  661.2 21.7 %scatter_custom_fusion.7 = f32[24576]{0:T(1024)S(1)} fusion(s32[3072]{0:T(1024)S(1)} %select_bitcast_fusion, f32[3072]{0:T(1024)S(1)} %fusion.118, f32[]{:T(128)} %constant.8.clone.1), kind=kCustom, calls=%fused_computation.187 | custom fusion | flops 3072 | bytes 98308
  685.0 74.5 %all-reduce.11.cloned.1.call-done = f32[24,1024]{1,0:T(8,128)} async-done(((f32[24,1024]{1,0:T(8,128)}), f32[24,1024]{1,0:T(8,128)}) %all-reduce.11.cloned.1.call-update) | async-done | bytes 98320 | tf_op jit(solution)/shard_map/psum | solution.py:140
  764.9 5.9 collective-permute-done.30
  (209 shorter events, 87.2 us)
Async XLA Ops:
  7.2 220.1 %all-reduce.5.cloned.1.call-start = ((), (), s32[]{:S(2)}) async-start(), calls=%async_computation | async-start | bytes 196608 | tf_op jit(solution)/shard_map/psum | solution.py:140
  7.2 54.5 %collective-permute-start.5 = (f32[8,1024]{1,0:T(8,128)}, f32[8,1024]{1,0:T(8,128)S(1)}, u32[]{:S(2)}, u32[]{:S(2)}) collective-permute-start(f32[8,1024]{1,0:T(8,128)} %param.15), channel_id=1, source_target_pairs={{8,0},{16,8},{24,16},{32,24},{40,32},{48,40},{56,48},{64,56},{72,6... | collective-permute-start | bytes 98312 | tf_op jit(solution)/shard_map/ppermute | solution.py:26
  21.7 40.1 %collective-permute-start.4 = (f32[8,1024]{1,0:T(8,128)}, f32[8,1024]{1,0:T(8,128)S(1)}, u32[]{:S(2)}, u32[]{:S(2)}) collective-permute-start(f32[8,1024]{1,0:T(8,128)} %param.15), channel_id=1, source_target_pairs={{0,8},{8,16},{16,24},{24,32},{32,40},{40,48},{48,56},{56,64},{64,7... | collective-permute-start | bytes 98312 | tf_op jit(solution)/shard_map/ppermute | solution.py:24
  24.4 10.2 %collective-permute-start.1 = (f32[3,1,512]{2,1,0:T(1,128)S(1)}, f32[3,1,512]{2,1,0:T(1,128)S(1)}, u32[]{:S(2)}, u32[]{:S(2)}) collective-permute-start(f32[3,1,512]{2,1,0:T(1,128)S(1)} %get-tuple-element.63), channel_id=1, source_target_pairs={{8,0},{16,8},{24,16},{32,24},{40,32},{48,40},{56,48},{64,56},{72,6... | collective-permute-start | bytes 18440 | tf_op jit(solution)/shard_map/ppermute | solution.py:26
  30.2 7.1 collective-permute-start
  37.3 23.4 %collective-permute-start.3 = (f32[3,34,1]{2,1,0:T(8,128)S(1)}, f32[3,34,1]{2,1,0:T(8,128)S(1)}, u32[]{:S(2)}, u32[]{:S(2)}) collective-permute-start(f32[3,34,1]{2,1,0:T(8,128)S(1)} %get-tuple-element.55), channel_id=1, source_target_pairs={{1,0},{2,1},{3,2},{4,3},{5,4},{6,5},{7,6},{9,8},{10,9},{11,10},{12... | collective-permute-start | bytes 1232 | tf_op jit(solution)/shard_map/ppermute | solution.py:26
  38.6 22.1 %collective-permute-start.2 = (f32[3,34,1]{2,1,0:T(8,128)S(1)}, f32[3,34,1]{2,1,0:T(8,128)S(1)}, u32[]{:S(2)}, u32[]{:S(2)}) collective-permute-start(f32[3,34,1]{2,1,0:T(8,128)S(1)} %get-tuple-element.54), channel_id=1, source_target_pairs={{0,1},{1,2},{2,3},{3,4},{4,5},{5,6},{6,7},{8,9},{9,10},{10,11},{11... | collective-permute-start | bytes 1232 | tf_op jit(solution)/shard_map/ppermute | solution.py:24
  103.9 44.6 %collective-permute-start.7 = (f32[3,1,512]{2,1,0:T(1,128)S(1)}, f32[3,1,512]{2,1,0:T(1,128)S(1)}, u32[]{:S(2)}, u32[]{:S(2)}) collective-permute-start(f32[3,1,512]{2,1,0:T(1,128)S(1)} %get-tuple-element.61), channel_id=1, source_target_pairs={{8,0},{16,8},{24,16},{32,24},{40,32},{48,40},{56,48},{64,56},{72,6... | collective-permute-start | bytes 18440 | tf_op jit(solution)/shard_map/ppermute | solution.py:26
  106.4 42.1 %collective-permute-start.6 = (f32[3,1,512]{2,1,0:T(1,128)S(1)}, f32[3,1,512]{2,1,0:T(1,128)S(1)}, u32[]{:S(2)}, u32[]{:S(2)}) collective-permute-start(f32[3,1,512]{2,1,0:T(1,128)S(1)} %get-tuple-element.60), channel_id=1, source_target_pairs={{0,8},{8,16},{16,24},{24,32},{32,40},{40,48},{48,56},{56,64},{64,7... | collective-permute-start | bytes 18440 | tf_op jit(solution)/shard_map/ppermute | solution.py:24
  148.3 264.6 %all-reduce.7.cloned.1.call-start = ((), (), s32[]{:S(2)}) async-start(), calls=%async_computation.1 | async-start | bytes 196608 | tf_op jit(solution)/shard_map/psum | solution.py:140
  148.6 6.1 collective-permute-start.9
  149.9 6.4 collective-permute-start.8
  228.1 4.4 collective-permute-start.11
  230.0 8.6 %collective-permute-start.10 = (f32[8,1024]{1,0:T(8,128)S(1)}, f32[8,1024]{1,0:T(8,128)S(1)}, u32[]{:S(2)}, u32[]{:S(2)}) collective-permute-start(f32[8,1024]{1,0:T(8,128)S(1)} %get-tuple-element.70), channel_id=1, source_target_pairs={{0,8},{8,16},{16,24},{24,32},{32,40},{40,48},{48,56},{56,64},{64,7... | collective-permute-start | bytes 98312 | tf_op jit(solution)/shard_map/ppermute | solution.py:24
  241.4 7.3 collective-permute-start.12
  312.5 22.9 %collective-permute-start.15 = (f32[3,1,512]{2,1,0:T(1,128)S(1)}, f32[3,1,512]{2,1,0:T(1,128)S(1)}, u32[]{:S(2)}, u32[]{:S(2)}) collective-permute-start(f32[3,1,512]{2,1,0:T(1,128)S(1)} %get-tuple-element.59), channel_id=1, source_target_pairs={{8,0},{16,8},{24,16},{32,24},{40,32},{48,40},{56,48},{64,56},{72,6... | collective-permute-start | bytes 18440 | tf_op jit(solution)/shard_map/ppermute | solution.py:26
  314.5 21.0 %collective-permute-start.14 = (f32[3,1,512]{2,1,0:T(1,128)S(1)}, f32[3,1,512]{2,1,0:T(1,128)S(1)}, u32[]{:S(2)}, u32[]{:S(2)}) collective-permute-start(f32[3,1,512]{2,1,0:T(1,128)S(1)} %get-tuple-element.58), channel_id=1, source_target_pairs={{0,8},{8,16},{16,24},{24,32},{32,40},{40,48},{48,56},{56,64},{64,7... | collective-permute-start | bytes 18440 | tf_op jit(solution)/shard_map/ppermute | solution.py:24
  335.0 263.4 %all-reduce.9.cloned.1.call-start = ((), (), s32[]{:S(2)}) async-start(), calls=%async_computation.2 | async-start | bytes 196608 | tf_op jit(solution)/shard_map/psum | solution.py:140
  335.5 6.1 collective-permute-start.17
  336.8 6.4 collective-permute-start.16
  415.6 8.6 %collective-permute-start.18 = (f32[8,1024]{1,0:T(8,128)S(1)}, f32[8,1024]{1,0:T(8,128)S(1)}, u32[]{:S(2)}, u32[]{:S(2)}) collective-permute-start(f32[8,1024]{1,0:T(8,128)S(1)} %get-tuple-element.68), channel_id=1, source_target_pairs={{0,8},{8,16},{16,24},{24,32},{32,40},{40,48},{48,56},{56,64},{64,7... | collective-permute-start | bytes 98312 | tf_op jit(solution)/shard_map/ppermute | solution.py:24
  426.9 7.3 collective-permute-start.20
  498.1 22.7 %collective-permute-start.23 = (f32[3,1,512]{2,1,0:T(1,128)S(1)}, f32[3,1,512]{2,1,0:T(1,128)S(1)}, u32[]{:S(2)}, u32[]{:S(2)}) collective-permute-start(f32[3,1,512]{2,1,0:T(1,128)S(1)} %get-tuple-element.57), channel_id=1, source_target_pairs={{8,0},{16,8},{24,16},{32,24},{40,32},{48,40},{56,48},{64,56},{72,6... | collective-permute-start | bytes 18440 | tf_op jit(solution)/shard_map/ppermute | solution.py:26
  500.0 20.8 %collective-permute-start.22 = (f32[3,1,512]{2,1,0:T(1,128)S(1)}, f32[3,1,512]{2,1,0:T(1,128)S(1)}, u32[]{:S(2)}, u32[]{:S(2)}) collective-permute-start(f32[3,1,512]{2,1,0:T(1,128)S(1)} %get-tuple-element.56), channel_id=1, source_target_pairs={{0,8},{8,16},{16,24},{24,32},{32,40},{40,48},{48,56},{56,64},{64,7... | collective-permute-start | bytes 18440 | tf_op jit(solution)/shard_map/ppermute | solution.py:24
  520.6 239.0 %all-reduce.11.cloned.1.call-start = ((), (), s32[]{:S(2)}) async-start(), calls=%async_computation.3 | async-start | bytes 196608 | tf_op jit(solution)/shard_map/psum | solution.py:140
  520.9 6.1 collective-permute-start.25
  522.2 6.4 collective-permute-start.24
  599.2 4.4 collective-permute-start.27
  601.1 8.6 %collective-permute-start.26 = (f32[8,1024]{1,0:T(8,128)S(1)}, f32[8,1024]{1,0:T(8,128)S(1)}, u32[]{:S(2)}, u32[]{:S(2)}) collective-permute-start(f32[8,1024]{1,0:T(8,128)S(1)} %get-tuple-element.66), channel_id=1, source_target_pairs={{0,8},{8,16},{16,24},{24,32},{32,40},{40,48},{48,56},{56,64},{64,7... | collective-permute-start | bytes 98312 | tf_op jit(solution)/shard_map/ppermute | solution.py:24
  612.5 7.3 collective-permute-start.28
  760.3 4.6 collective-permute-start.31
  762.2 8.6 %collective-permute-start.30 = (f32[8,1024]{1,0:T(8,128)S(1)}, f32[8,1024]{1,0:T(8,128)S(1)}, u32[]{:S(2)}, u32[]{:S(2)}) collective-permute-start(f32[8,1024]{1,0:T(8,128)S(1)} %get-tuple-element.64), channel_id=1, source_target_pairs={{0,8},{8,16},{16,24},{24,32},{32,40},{40,48},{48,56},{56,64},{64,7... | collective-permute-start | bytes 98312 | tf_op jit(solution)/shard_map/ppermute | solution.py:24
  (16 other events, 165.1 us)
Sparse Core Ops, SparseCore 0:
  148.4 78.9 all-reduce.4
  335.1 77.6 all-reduce.6
  520.7 77.7 all-reduce.8
  683.7 75.7 all-reduce.10
where the time goes:
time: 781 us; the launch traced here: 779 us
  waiting for transfers between devices  328 us (42%)
  local copies, waits for them, and re-layouts  177 us (23%)
  other arithmetic  167 us (21%)
  starting transfers between devices  91.1 us (12%)
  between operations  15.1 us (2%)
    psum x4, waiting for transfers between devices, per_device(): totals = lax.psum(partial_value, 'gy')  282 us
    gather x4, local copies, waits for them, and re-layouts, per_device(): river_segment = jnp.take_along_axis(reach_all, bank_site, axis=1)  98.8 us
    unnamed x7, other arithmetic  87.1 us
    gather x4, local copies, waits for them, and re-layouts, per_device(): cell_depth = plain[0].reshape(-1)[cell_read]  69.6 us
    scatter-add x4, other arithmetic, per_device(): source = jnp.zeros((cell_total,), jnp.float32).at[cell_flat.reshape(-1)]....  66.4 us
    ppermute x16, waiting for transfers between devices, with_halo(): lax.ppermute(tail, axis, [(i, (i + 1) % count) for i in range(ends)])  46.3 us
    ppermute x16, starting transfers between devices, with_halo(): lax.ppermute(tail, axis, [(i, (i + 1) % count) for i in range(ends)])  45.6 us
    ppermute x16, starting transfers between devices, with_halo(): lax.ppermute(head, axis, [((i + 1) % count, i) for i in range(ends)])  45.2 us
  transfers between devices with their start and end apart: 36, of which 15 were waited for; matrix products, arithmetic and copies ran while one was open for 13% of the time, Pallas kernels for 0%

commit v1 on v0

v1 whole, which is shorter than its diff:
```python
import functools

import jax
import jax.numpy as jnp
from jax import lax
from jax.experimental import pallas as pl
from jax.experimental.pallas import tpu as pltpu
from jax.sharding import PartitionSpec as P

STEPS = 4


GRAV = 9.81
DT = 0.5
DX = 10.0
NU = 0.1
RATIO = 0.25
FACTOR = DT / (2.0 * DX)

LANES = 128
ROWS = 32
QUADS = 4
COLS = QUADS * LANES
FIELDS = 8
BASINS = 8
SLOT_ROWS = 3 * BASINS
FIRST_ROWS = 24
STEP_ROWS = 16
INTERPRET = False


def iota(shape, dim):
    return lax.broadcasted_iota(jnp.int32, shape, dim)


def lane_gather(rows, index):
    return jnp.take_along_axis(rows, index, axis=1, mode="promise_in_bounds")


def lane_to_column(row, count, offset):
    wide = jnp.broadcast_to(row, (count, LANES))
    hit = iota((count, LANES), 1) == iota((count, LANES), 0) + offset
    return jnp.sum(jnp.where(hit, wide, 0.0), axis=1, keepdims=True)


def column_to_lane(column, offset):
    count = column.shape[0]
    wide = jnp.broadcast_to(column, (count, LANES))
    hit = iota((count, LANES), 1) == iota((count, LANES), 0) + offset
    return jnp.sum(jnp.where(hit, wide, 0.0), axis=0, keepdims=True)


def own_row(block, y):
    return jnp.sum(jnp.where(iota(block.shape, 0) == y, block, 0.0), axis=0, keepdims=True)


def flux_terms(cells):
    h, p, q = cells
    inverse = 1.0 / h
    u = p * inverse
    v = q * inverse
    pressure = 0.5 * GRAV * h * h
    return (p, p * u + pressure, q * u), (q, p * v, q * v + pressure), u, v


def flood_update(cells, top, low, left, right, rough, source):
    flux_x, flux_y, u, v = flux_terms(cells)
    top_x = flux_terms(top)[0]
    low_x = flux_terms(low)[0]
    left_y = flux_terms(left)[1]
    right_y = flux_terms(right)[1]
    row = iota((ROWS, COLS), 0)
    col = iota((ROWS, COLS), 1)
    out = []
    for k in range(3):
        quarter = 0.25 * cells[k]
        from_top = jnp.where(
            row == 0, 0.25 * top[k] + FACTOR * top_x[k], pltpu.roll(quarter + FACTOR * flux_x[k], 1, 0)
        )
        from_low = jnp.where(
            row == ROWS - 1,
            0.25 * low[k] - FACTOR * low_x[k],
            pltpu.roll(quarter - FACTOR * flux_x[k], ROWS - 1, 0),
        )
        from_left = jnp.where(
            col == 0, 0.25 * left[k] + FACTOR * left_y[k], pltpu.roll(quarter + FACTOR * flux_y[k], 1, 1)
        )
        from_right = jnp.where(
            col == COLS - 1,
            0.25 * right[k] - FACTOR * right_y[k],
            pltpu.roll(quarter - FACTOR * flux_y[k], COLS - 1, 1),
        )
        out.append((from_top + from_low) + (from_left + from_right))
    h = cells[0]
    size = jnp.abs(h)
    root = jnp.exp(jnp.log(size) * (-1.0 / 3.0))
    root = root * (4.0 - size * (root * root * root)) * (1.0 / 3.0)
    root = jnp.where(h < 0.0, -root, root)
    drag = (GRAV * DT) * rough * rough * jnp.sqrt(u * u + v * v) * root
    return [out[0] + DT * source, out[1] - drag * u, out[2] - drag * v]


def halves(values):
    high = values.astype(jnp.bfloat16).astype(jnp.float32)
    return high, values - high


def spread(rates, major, minor, count):
    total = None
    rows = rates.shape[0]
    group = 4
    high, low = halves(rates)
    for start in range(0, rows, group):
        left, right = [], []
        for r in range(start, start + group):
            at = iota((count, LANES), 0) == major[r : r + 1]
            left.append(
                jnp.concatenate(
                    [
                        jnp.where(at, high[r : r + 1], 0.0),
                        jnp.where(at, low[r : r + 1], 0.0),
                    ],
                    axis=0,
                ).astype(jnp.bfloat16)
            )
            right.append(
                jnp.where(iota((LANES, LANES), 0) == minor[r : r + 1], 1.0, 0.0).astype(jnp.bfloat16)
            )
        part = lax.dot_general(
            jnp.concatenate(left, axis=1),
            jnp.concatenate(right, axis=1),
            (((1,), (1,)), ((), ())),
            preferred_element_type=jnp.float32,
        )
        total = part if total is None else total + part
    return total[:count] + total[count:]


def cell_parts(cell):
    col = cell & (COLS - 1)
    return (col >> 7) * ROWS + (cell >> 9), col & (LANES - 1)


def depth_at_slots(h_ref, index, cell):
    major, minor = cell_parts(cell)
    index_rows = [minor[8 * v : 8 * v + 8] for v in range(3)]
    key_rows = [major[8 * v : 8 * v + 8] for v in range(3)]
    found = [jnp.zeros((8, LANES), jnp.float32) for _ in range(3)]
    for quad in range(QUADS):
        for row in range(ROWS):
            values = h_ref[index + (slice(row, row + 1), slice(quad * LANES, (quad + 1) * LANES))]
            values = jnp.broadcast_to(values, (8, LANES))
            for v in range(3):
                found[v] = jnp.where(
                    key_rows[v] == quad * ROWS + row, lane_gather(values, index_rows[v]), found[v]
                )
    return jnp.concatenate(found, axis=0)


def level_at_sites(reach_rows, site):
    found = []
    for v in range(3):
        sites = site[8 * v : 8 * v + 8]
        field = sites >> 7
        station = sites & (LANES - 1)
        level = jnp.zeros((8, LANES), jnp.float32)
        for f in range(FIELDS):
            level = jnp.where(field == f, lane_gather(reach_rows(f, v), station), level)
        found.append(level)
    return jnp.concatenate(found, axis=0)


def put_edges(send_ref, across_ref, cells, even, mine, other, y, col_row, edge_row):
    lane_left = column_to_lane(cells[0][:, 0:1], 0)
    lane_right = column_to_lane(cells[0][:, COLS - 1 : COLS], 0)
    for k in (1, 2):
        lane_left = lane_left + column_to_lane(cells[k][:, 0:1], k * ROWS)
        lane_right = lane_right + column_to_lane(cells[k][:, COLS - 1 : COLS], k * ROWS)
    send_ref[mine, jnp.maximum(y - 1, 0), col_row : col_row + 1, :] = lane_left
    send_ref[mine, jnp.minimum(y + 1, BASINS - 1), col_row : col_row + 1, :] = lane_right
    for k in range(3):
        first = cells[k][0:1]
        last = cells[k][ROWS - 1 : ROWS]
        inner = jnp.where(even, last, first)
        outer = jnp.where(even, first, last)
        for quad in range(QUADS):
            at = k * QUADS + quad
            lanes = slice(quad * LANES, (quad + 1) * LANES)
            send_ref[other, y, edge_row + at : edge_row + at + 1, :] = inner[:, lanes]
            across_ref[at : at + 1, :] = outer[:, lanes]


def get_edges(got_ref, over_ref, cells, scal, mine, other, y, col_row, edge_row, over_edge):
    even = scal[0] == 0
    is_first, is_last = scal[2] == 1, scal[3] == 1
    before = got_ref[mine, jnp.maximum(y - 1, 0), col_row : col_row + 1, :]
    after = got_ref[mine, jnp.minimum(y + 1, BASINS - 1), col_row : col_row + 1, :]
    top, low, left, right = [], [], [], []
    for k in range(3):
        inner = jnp.concatenate(
            [
                got_ref[other, y, edge_row + k * QUADS + quad : edge_row + k * QUADS + quad + 1, :]
                for quad in range(QUADS)
            ],
            axis=1,
        )
        outer = jnp.concatenate(
            [
                over_ref[over_edge + k * QUADS + quad : over_edge + k * QUADS + quad + 1, :]
                for quad in range(QUADS)
            ],
            axis=1,
        )
        top.append(jnp.where(is_first, cells[k][0:1], jnp.where(even, outer, inner)))
        low.append(jnp.where(is_last, cells[k][ROWS - 1 : ROWS], jnp.where(even, inner, outer)))
        left.append(jnp.where(y == 0, cells[k][:, 0:1], lane_to_column(before, ROWS, k * ROWS)))
        right.append(
            jnp.where(
                y == BASINS - 1, cells[k][:, COLS - 1 : COLS], lane_to_column(after, ROWS, k * ROWS)
            )
        )
    return top, low, left, right


def river_update(current, outlets, own, lateral):
    rate = own[0:8]
    base = own[8:16, 0:1]
    weight = own[16:24]
    inflow_row = jnp.sum(weight * outlets, axis=0, keepdims=True)
    inflow = base + lane_to_column(inflow_row, FIELDS, 0)
    lane = iota((FIELDS, LANES), 1)
    sub = iota((FIELDS, LANES), 0)
    behind = jnp.where(lane == 0, inflow, pltpu.roll(current, 1, 1))
    above = jnp.where(sub == FIELDS - 1, current, pltpu.roll(current, FIELDS - 1, 0))
    below = jnp.where(sub == 0, current, pltpu.roll(current, 1, 0))
    mixing = above - 2.0 * current + below
    return current - rate * (current - behind) + NU * mixing - (DT * RATIO) * lateral


def first_kernel(
    scal, depth, discharge, cell_in, site_in, coeff_in, reach, send_ref, across_ref, cell_ref, site_ref, coeff_ref, slots_ref
):
    even = scal[0] == 0
    mine, other, y = scal[0], 1 - scal[0], scal[1]
    send_ref[...] = jnp.zeros_like(send_ref)
    across_ref[...] = jnp.zeros_like(across_ref)

    def arranged(ref):
        low, own, high = ref[0:8], ref[8:16], ref[16:24]
        return jnp.concatenate([own, jnp.where(even, high, low), jnp.where(even, low, high)], axis=0)

    cell = arranged(cell_in)
    site = arranged(site_in)
    coeff = jnp.where(cell >= 0, arranged(coeff_in), 0.0)
    cell = jnp.maximum(cell, 0)
    cell_ref[...] = cell
    site_ref[...] = site
    coeff_ref[...] = coeff
    slots = depth_at_slots(depth, (), cell)
    slots_ref[...] = slots
    site_value = site.astype(jnp.float32)
    level_rows = [own_row(reach[:, f * LANES : (f + 1) * LANES], y) for f in range(FIELDS)]
    for b in range(BASINS):
        for at, value in enumerate((slots, site_value, coeff)):
            send_ref[mine, b, at : at + 1, :] = value[b : b + 1]
            send_ref[other, b, at : at + 1, :] = value[8 + b : 9 + b]
            send_ref[mine, b, 3 + at : 4 + at, :] = value[16 + b : 17 + b]
        for f in range(FIELDS):
            send_ref[other, b, 15 + f : 16 + f, :] = level_rows[f]
    cells = [depth[...], discharge[0], discharge[1]]
    put_edges(send_ref, across_ref, cells, even, mine, other, y, 6, 3)


def step_kernel(first, last, *refs):
    refs = list(refs)

    def take(n):
        taken = refs[:n]
        del refs[:n]
        return taken

    (scal,) = take(1)
    if first:
        depth, discharge, reach = take(3)
    else:
        state, levels, owner_levels, owner_site, owner_coeff = take(5)
    got, over, rough, own, cell_ref, coeff_ref, slots_ref = take(7)
    if first:
        (site_ref,) = take(1)
    (state_out,) = take(1)
    if last:
        (all_levels,) = take(1)
    else:
        levels_out, owner_levels_out, slots_out, send_ref, across_ref = take(5)
        if first:
            owner_site_out, owner_coeff_out = take(2)
    even = scal[0] == 0
    mine, other, y = scal[0], 1 - scal[0], scal[1]
    cell = cell_ref[...]

    def gathered(row, across_row):
        return jnp.concatenate(
            [got[mine, :, row, :], got[other, :, row, :], over[pl.ds(across_row, 8, stride=8), :]],
            axis=0,
        )

    if first:
        cells = [depth[...], discharge[0], discharge[1]]
        current = jnp.concatenate(
            [own_row(reach[:, f * LANES : (f + 1) * LANES], y) for f in range(FIELDS)], axis=0
        )
        over_edge = 64

        def tile_rows(f, v):
            if v == 0:
                return reach[:, f * LANES : (f + 1) * LANES]
            if v == 1:
                return got[other, :, 15 + f, :]
            return over[80 + 8 * f : 88 + 8 * f, :]

        segment = level_at_sites(tile_rows, site_ref[...])
        site_owner = gathered(1, 4).astype(jnp.int32)
        coeff_owner = gathered(2, 5)
        slots_owner = gathered(0, 3)
        outlets = jnp.zeros((BASINS, LANES), jnp.float32)
        for f in range(FIELDS):
            source_rows = jnp.where(even, tile_rows(f, 2), tile_rows(f, 1))
            outlets = jnp.where(
                iota((BASINS, LANES), 1) == f, source_rows[:, LANES - 1 : LANES], outlets
            )
        segment_owner = level_at_sites(
            lambda f, v: jnp.broadcast_to(current[f : f + 1], (8, LANES)), site_owner
        )
        edge_rows = (6, 3)
    else:
        cells = [state[0], state[1], state[2]]
        current = levels[...]
        over_edge = 64
        segment = gathered(1, 4)
        slots_owner = gathered(0, 3)
        site_owner = owner_site[...]
        coeff_owner = owner_coeff[...]
        segment_owner = owner_levels[...]
        outlets = jnp.where(even, over[pl.ds(2, 8, stride=8), :], got[other, :, 2, :])
        edge_rows = (5, 3)

    rates_owner = coeff_owner * (segment_owner - slots_owner)
    lateral = spread(rates_owner, site_owner >> 7, site_owner & (LANES - 1), FIELDS)
    levels_next = river_update(current, outlets, own[...], lateral)

    major, minor = cell_parts(cell)
    rates = coeff_ref[...] * (segment - slots_ref[...])
    blocks = spread(rates, major, minor, QUADS * ROWS)
    source = jnp.concatenate([blocks[q * ROWS : (q + 1) * ROWS] for q in range(QUADS)], axis=1)
    top, low, left, right = get_edges(
        got, over, cells, scal, mine, other, y, edge_rows[0], edge_rows[1], over_edge
    )
    new = flood_update(cells, top, low, left, right, rough[...], source)
    for k in range(3):
        state_out[k] = new[k]

    if last:
        for b in range(BASINS):
            all_levels[b] = levels_next
        return

    if first:
        owner_site_out[...] = site_owner
        owner_coeff_out[...] = coeff_owner
    send_ref[...] = jnp.zeros_like(send_ref)
    across_ref[...] = jnp.zeros_like(across_ref)
    levels_out[...] = levels_next
    owned = level_at_sites(
        lambda f, v: jnp.broadcast_to(levels_next[f : f + 1], (8, LANES)), site_owner
    )
    owner_levels_out[...] = owned
    slots = depth_at_slots(state_out, (0,), cell)
    slots_out[...] = slots
    outlet_row = column_to_lane(levels_next[:, LANES - 1 : LANES], 0)
    for b in range(BASINS):
        for at, value in enumerate((slots, owned)):
            send_ref[mine, b, at : at + 1, :] = value[b : b + 1]
            send_ref[other, b, at : at + 1, :] = value[8 + b : 9 + b]
            send_ref[mine, b, 3 + at : 4 + at, :] = value[16 + b : 17 + b]
        send_ref[mine, b, 2:3, :] = outlet_row
        send_ref[other, b, 2:3, :] = outlet_row
    put_edges(send_ref, across_ref, new, even, mine, other, y, 5, 3)


def call(kernel, outs, args):
    specs = [pl.BlockSpec(memory_space=pltpu.SMEM)]
    specs += [pl.BlockSpec(memory_space=pltpu.VMEM) for _ in args[1:]]
    return pl.pallas_call(
        kernel,
        out_shape=outs,
        in_specs=specs,
        out_specs=[pl.BlockSpec(memory_space=pltpu.VMEM) for _ in outs],
        compiler_params=None if INTERPRET else pltpu.CompilerParams(vmem_limit_bytes=16 << 20),
        interpret=INTERPRET,
    )(*args)


def f32(*shape):
    return jax.ShapeDtypeStruct(shape, jnp.float32)


def i32(*shape):
    return jax.ShapeDtypeStruct(shape, jnp.int32)


def per_device(
    depth,
    discharge,
    roughness,
    reach_state,
    celerity,
    base_inflow,
    upstream,
    bank_cell,
    bank_site,
    bank_coeff,
):
    count_x = lax.axis_size("gx")
    count_y = lax.axis_size("gy")
    gx = lax.axis_index("gx")
    gy = lax.axis_index("gy")
    core = gx % 2
    pairs = [list(range(c * 2 * count_y, (c + 1) * 2 * count_y)) for c in range(count_x // 2)]
    border = [(i, i + 1) for i in range(1, count_x - 1, 2)]
    border = border + [(b, a) for a, b in border]
    scal = jnp.stack(
        [core, gy, (gx == 0).astype(jnp.int32), (gx == count_x - 1).astype(jnp.int32)]
    ).astype(jnp.int32)

    def mine_of(array):
        return lax.dynamic_slice_in_dim(array, gy, 1, axis=0)

    ids = (gx - 1) * BASINS + jnp.arange(BASINS, dtype=jnp.int32)
    weight = jnp.sum((mine_of(upstream) == ids[:, None]).astype(jnp.float32), axis=1, keepdims=True)
    own = jnp.concatenate(
        [
            jnp.broadcast_to(mine_of(celerity).reshape(FIELDS, 1), (FIELDS, LANES)),
            jnp.broadcast_to(mine_of(base_inflow).reshape(FIELDS, 1), (FIELDS, LANES)),
            jnp.broadcast_to(weight, (BASINS, LANES)),
        ],
        axis=0,
    )

    def exchange(send, across, extra):
        rows = send.shape[2]
        got = lax.all_to_all(
            send.reshape(2 * BASINS, rows, LANES), ("gx", "gy"), 0, 0, axis_index_groups=pairs
        )
        part = lax.dynamic_slice(got, (core * BASINS, 0, 0), (BASINS, 8, LANES))
        packed = jnp.concatenate([part.reshape(BASINS * 8, LANES), across] + extra, axis=0)
        over = lax.ppermute(packed, "gx", border)
        return got.reshape(2, BASINS, rows, LANES), over

    send, across, cell, site, coeff, slots = call(
        first_kernel,
        [
            f32(2, BASINS, FIRST_ROWS, LANES),
            f32(16, LANES),
            i32(SLOT_ROWS, LANES),
            i32(SLOT_ROWS, LANES),
            f32(SLOT_ROWS, LANES),
            f32(SLOT_ROWS, LANES),
        ],
        [scal, depth, discharge, bank_cell, bank_site, bank_coeff, reach_state],
    )
    fields_major = [reach_state[:, f * LANES : (f + 1) * LANES] for f in range(FIELDS)]
    got, over = exchange(send, across, fields_major)
    for step in range(STEPS):
        first, last = step == 0, step == STEPS - 1
        outs = [f32(3, ROWS, COLS)]
        if last:
            outs += [f32(BASINS, FIELDS, LANES)]
        else:
            outs += [
                f32(FIELDS, LANES),
                f32(SLOT_ROWS, LANES),
                f32(SLOT_ROWS, LANES),
                f32(2, BASINS, STEP_ROWS, LANES),
                f32(16, LANES),
            ]
        if first:
            outs += [i32(SLOT_ROWS, LANES), f32(SLOT_ROWS, LANES)]
            args = [scal, depth, discharge, reach_state]
        else:
            args = [scal, state, levels, owner_levels, owner_site, owner_coeff]
        args += [got, over, roughness, own, cell, coeff, slots]
        if first:
            args += [site]
        result = call(functools.partial(step_kernel, first, last), outs, args)
        state = result[0]
        if last:
            break
        levels, owner_levels, slots, send, across = result[1:6]
        if first:
            owner_site, owner_coeff = result[6:8]
        got, over = exchange(send, across, [])
    final = lax.all_to_all(result[1], "gy", 0, 0)
    return state, final.reshape(BASINS, FIELDS * LANES)


def solution(mesh):
    return jax.shard_map(
        per_device,
        mesh=mesh,
        in_specs=(
            P("gx", "gy"),
            P(None, "gx", "gy"),
            P("gx", "gy"),
            P("gx", None),
            P("gx", None),
            P("gx", None),
            P("gx", None),
            P("gx", "gy"),
            P("gx", "gy"),
            P("gx", "gy"),
        ),
        out_specs=(P(None, "gx", "gy"), P("gx", None)),
        check_vma=False,
    )
```

time: 781 us -> 120 us (0.15)
  waiting for transfers between devices: 328 us -> 20.2 us
  local copies, waits for them, and re-layouts: 177 us -> 5.46 us
  other arithmetic: 167 us -> 0.26 us
  starting transfers between devices: 91.1 us -> 33.5 us
  blocking collectives: 0 us -> 46.8 us
  between operations: 15.1 us -> 0.86 us
  Pallas kernels: 0 us -> 12.4 us
    psum x4 -> x0, waiting for transfers between devices: 282 us -> none  [per_device(): totals = lax.psum(partial_value, 'gy')]
    gather x8 -> x0, local copies, waits for them, and re-layouts: 168 us -> none  [the longest x4 98.8 us: per_device(): river_segment = jnp.take_along_axis(reach_all, bank_site, axis=1)]
    unnamed x7 -> x0, other arithmetic: 87.1 us -> none
    scatter-add x4 -> x0, other arithmetic: 66.4 us -> none  [per_device(): source = jnp.zeros((cell_total,), jnp.float32).at[cell_flat.reshape(-1)]....]
    ppermute x32 -> x4, starting transfers between devices: 90.8 us -> 26.1 us  [exchange(): over = lax.ppermute(packed, 'gx', border)]
    all_to_all x0 -> x4, blocking collectives: none -> 46.8 us  [the longest x3 35.8 us: exchange(): lax.all_to_all(send.reshape(2 * BASINS, rows, LANES), ('gx', 'gy'), 0, 0,...]
    ppermute x32 -> x4, waiting for transfers between devices: 46.4 us -> 12.1 us  [exchange(): over = lax.ppermute(packed, 'gx', border)]
    pallas_call x0 -> x5, Pallas kernels: none -> 12.4 us  [call(): pl.pallas_call(kernel, out_shape=outs, in_specs=specs, out_specs=[pl.Bloc...]
  transfers between devices with their start and end apart: 36 -> 5, of which waited for: 15 -> 5; matrix products, arithmetic and copies ran while one was open for 13% -> 1% of each run, Pallas kernels for 0% -> 0%
where the time goes in v1:
time: 120 us; the launch traced here: 119 us
  blocking collectives  46.8 us (39%)
  starting transfers between devices  33.5 us (28%)
  waiting for transfers between devices  20.2 us (17%)
  Pallas kernels  12.4 us (10%)
  local copies, waits for them, and re-layouts  5.46 us (5%)
    all_to_all x3, blocking collectives, exchange(): lax.all_to_all(send.reshape(2 * BASINS, rows, LANES), ('gx', 'gy'), 0, 0,...  35.8 us
    ppermute x4, starting transfers between devices, exchange(): over = lax.ppermute(packed, 'gx', border)  26.1 us
    pallas_call x5, Pallas kernels, call(): pl.pallas_call(kernel, out_shape=outs, in_specs=specs, out_specs=[pl.Bloc...  12.4 us
    ppermute x4, waiting for transfers between devices, exchange(): over = lax.ppermute(packed, 'gx', border)  12.1 us
    all_to_all x1, blocking collectives, per_device(): final = lax.all_to_all(result[1], 'gy', 0, 0)  11 us
    all_to_all x1, waiting for transfers between devices, exchange(): lax.all_to_all(send.reshape(2 * BASINS, rows, LANES), ('gx', 'gy'), 0, 0,...  8.14 us
    all_to_all x1, starting transfers between devices, exchange(): lax.all_to_all(send.reshape(2 * BASINS, rows, LANES), ('gx', 'gy'), 0, 0,...  7.34 us
    unnamed x30, local copies, waits for them, and re-layouts  4.48 us
  transfers between devices with their start and end apart: 5, of which 5 were waited for; matrix products, arithmetic and copies ran while one was open for 1% of the time, Pallas kernels for 0%

profile of v1, /device:TPU:6, one launch (start us, length us, event | category | flops | bytes accessed | tf_op | source)
XLA Modules:
  0.0 119.5 jit_solution(8703946508964857820)
XLA Ops:
  0.6 0.0 copy-start
  0.7 0.1 pad_add_fusion.scal.refs_0_
  0.8 0.6 copy-done.4
  1.4 0.9 copy-done.2
  2.3 0.8 copy-done.5
  3.2 0.7 copy-done.8
  3.9 0.7 copy-done.9
  4.6 2.3 %shard_map.113 = (f32[2,8,24,128]{3,2,1,0:T(8,128)}, f32[16,128]{1,0:T(8,128)S(1)}, s32[24,128]{1,0:T(8,128)S(1)}, s32[24,128]{1,0:T(8,128)S(1)}, f32[24,128]{1,0:T(8,128)S(1)}, /*index=5*/f32[24,128]{1,0:T(8,128)S(1)}) custom-call(s32[4]{0:T(128)S(1)} %pad_add_fusion.scal.refs_0_, f32[32,512]{1,0:T(8,128)S(1)} %copy-done.5, f32[2,32,512]{2,1,0:T(8,128)S(1)} %copy-done.2, ...), custom_call_target="tpu_custom_call" | custom-call | tf_op jit(solution)/shard_map/pallas_call | solution.py:393
  6.9 7.3 %all-to-all-start = ((f32[16,24,128]{2,1,0:T(8,128)}), f32[16,24,128]{2,1,0:T(8,128)S(1)}, u32[]{:S(2)}, u32[]{:S(2)}) async-start(f32[16,24,128]{2,1,0:T(8,128)} %bitcast.4), calls=%async_computation | async-start | bytes 393216 | tf_op jit(solution)/shard_map/all_to_all | solution.py:451
  14.3 0.2 fusion
  14.5 0.7 fusion.2
  15.2 0.1 fusion.1
  15.3 8.1 %all-to-all-done = f32[16,24,128]{2,1,0:T(8,128)S(1)} async-done(((f32[16,24,128]{2,1,0:T(8,128)}), f32[16,24,128]{2,1,0:T(8,128)S(1)}, u32[]{:S(2)}, u32[]{:S(2)}) %all-to-all-start) | async-done | bytes 196640 | tf_op jit(solution)/shard_map/all_to_all | solution.py:451
  23.5 14.0 %collective-permute-start = (f32[144,128]{1,0:T(8,128)S(1)}, f32[144,128]{1,0:T(8,128)S(1)}, u32[]{:S(2)}, u32[]{:S(2)}) collective-permute-start(f32[144,128]{1,0:T(8,128)S(1)} %constant_dynamic-update-slice_fusion), channel_id=1, source_target_pairs={{8,16},{24,32},{40,48},{56,64},{72,80},{88,96},{104,112},{120,128}... | collective-permute-start | bytes 221192 | tf_op jit(solution)/shard_map/ppermute | solution.py:456
  37.5 0.1 maximum_maximum_fusion
  37.6 1.9 %collective-permute-done.refs_5_ = f32[144,128]{1,0:T(8,128)S(1)} collective-permute-done((f32[144,128]{1,0:T(8,128)S(1)}, f32[144,128]{1,0:T(8,128)S(1)}, u32[]{:S(2)}, u32[]{:S(2)}) %collective-permute-start) | collective-permute-done | bytes 73760 | tf_op jit(solution)/shard_map/ppermute | solution.py:456
  39.5 0.1 broadcast.11.refs_7_.refs_9_
  39.6 2.7 %shard_map.114 = (f32[3,32,512]{2,1,0:T(8,128)S(1)}, f32[8,128]{1,0:T(8,128)S(1)}, f32[24,128]{1,0:T(8,128)S(1)}, f32[24,128]{1,0:T(8,128)S(1)}, f32[2,8,16,128]...) custom-call(s32[4]{0:T(128)S(1)} %pad_add_fusion.scal.refs_0_, ...), custom_call_target="tpu_custom_call" | custom-call | tf_op jit(solution)/shard_map/pallas_call | solution.py:393
  42.3 12.6 %all_to_all.25 = f32[16,16,128]{2,1,0:T(8,128)S(1)} all-to-all(f32[16,16,128]{2,1,0:T(8,128)S(1)} %bitcast.32), channel_id=1, replica_groups={{0,1,2,3,4,5,6,7,8,9,10,11,12,13,14,15},{16,17,18,19,20,21,22,23,24,25,..., dimensions={0} | all-to-all | bytes 262144 | tf_op jit(solution)/shard_map/all_to_all | solution.py:451
  54.9 4.6 %collective-permute-start.1 = (f32[80,128]{1,0:T(8,128)S(1)}, f32[80,128]{1,0:T(8,128)S(1)}, u32[]{:S(2)}, u32[]{:S(2)}) collective-permute-start(f32[80,128]{1,0:T(8,128)S(1)} %pad_maximum_fusion), channel_id=1, source_target_pairs={{8,16},{24,32},{40,48},{56,64},{72,80},{88,96},{104,112},{120,128}... | collective-permute-start | bytes 122888 | tf_op jit(solution)/shard_map/ppermute | solution.py:456
  59.5 2.8 %collective-permute-done.1.refs_7_ = f32[80,128]{1,0:T(8,128)S(1)} collective-permute-done((f32[80,128]{1,0:T(8,128)S(1)}, f32[80,128]{1,0:T(8,128)S(1)}, u32[]{:S(2)}, u32[]{:S(2)}) %collective-permute-start.1) | collective-permute-done | bytes 40992 | tf_op jit(solution)/shard_map/ppermute | solution.py:456
  62.3 2.6 %shard_map.115 = (f32[3,32,512]{2,1,0:T(8,128)S(1)}, f32[8,128]{1,0:T(8,128)S(1)}, f32[24,128]{1,0:T(8,128)S(1)}, f32[24,128]{1,0:T(8,128)S(1)}, f32[2,8,16,128]{3,2,1,0:T(8,128)S(1)}, /*index=5*/f32[16,128]{1,0:T(8,128)S(1)}) custom-call(s32[4]{0:T(128)S(1)} %pad_add_fusion.scal.refs_0_, f32[3,32,512]{2,1,0:T(8,128)S(1)} %get-tuple-element.36.refs_1_, ...), custom_call_target="tpu_custom_call" | custom-call | tf_op jit(solution)/shard_map/pallas_call | solution.py:393
  64.9 11.6 %all_to_all.26 = f32[16,16,128]{2,1,0:T(8,128)S(1)} all-to-all(f32[16,16,128]{2,1,0:T(8,128)S(1)} %bitcast.33), channel_id=1, replica_groups={{0,1,2,3,4,5,6,7,8,9,10,11,12,13,14,15},{16,17,18,19,20,21,22,23,24,25,..., dimensions={0} | all-to-all | bytes 262144 | tf_op jit(solution)/shard_map/all_to_all | solution.py:451
  76.5 4.0 %collective-permute-start.2 = (f32[80,128]{1,0:T(8,128)S(1)}, f32[80,128]{1,0:T(8,128)S(1)}, u32[]{:S(2)}, u32[]{:S(2)}) collective-permute-start(f32[80,128]{1,0:T(8,128)S(1)} %pad_maximum_fusion.1), channel_id=1, source_target_pairs={{8,16},{24,32},{40,48},{56,64},{72,80},{88,96},{104,112},{120,128}... | collective-permute-start | bytes 122888 | tf_op jit(solution)/shard_map/ppermute | solution.py:456
  80.6 3.4 %collective-permute-done.2.refs_7_ = f32[80,128]{1,0:T(8,128)S(1)} collective-permute-done((f32[80,128]{1,0:T(8,128)S(1)}, f32[80,128]{1,0:T(8,128)S(1)}, u32[]{:S(2)}, u32[]{:S(2)}) %collective-permute-start.2) | collective-permute-done | bytes 40992 | tf_op jit(solution)/shard_map/ppermute | solution.py:456
  84.0 2.6 %shard_map.116 = (f32[3,32,512]{2,1,0:T(8,128)S(1)}, f32[8,128]{1,0:T(8,128)S(1)}, f32[24,128]{1,0:T(8,128)S(1)}, f32[24,128]{1,0:T(8,128)S(1)}, f32[2,8,16,128]{3,2,1,0:T(8,128)S(1)}, /*index=5*/f32[16,128]{1,0:T(8,128)S(1)}) custom-call(s32[4]{0:T(128)S(1)} %pad_add_fusion.scal.refs_0_, f32[3,32,512]{2,1,0:T(8,128)S(1)} %get-tuple-element.44.refs_1_, ...), custom_call_target="tpu_custom_call" | custom-call | tf_op jit(solution)/shard_map/pallas_call | solution.py:393
  86.6 11.6 %all_to_all.27 = f32[16,16,128]{2,1,0:T(8,128)S(1)} all-to-all(f32[16,16,128]{2,1,0:T(8,128)S(1)} %bitcast.34), channel_id=1, replica_groups={{0,1,2,3,4,5,6,7,8,9,10,11,12,13,14,15},{16,17,18,19,20,21,22,23,24,25,..., dimensions={0} | all-to-all | bytes 262144 | tf_op jit(solution)/shard_map/all_to_all | solution.py:451
  98.2 3.5 %collective-permute-start.3 = (f32[80,128]{1,0:T(8,128)S(1)}, f32[80,128]{1,0:T(8,128)S(1)}, u32[]{:S(2)}, u32[]{:S(2)}) collective-permute-start(f32[80,128]{1,0:T(8,128)S(1)} %pad_maximum_fusion.2), channel_id=1, source_target_pairs={{8,16},{24,32},{40,48},{56,64},{72,80},{88,96},{104,112},{120,128}... | collective-permute-start | bytes 122888 | tf_op jit(solution)/shard_map/ppermute | solution.py:456
  101.7 3.9 %collective-permute-done.3.refs_7_ = f32[80,128]{1,0:T(8,128)S(1)} collective-permute-done((f32[80,128]{1,0:T(8,128)S(1)}, f32[80,128]{1,0:T(8,128)S(1)}, u32[]{:S(2)}, u32[]{:S(2)}) %collective-permute-start.3) | collective-permute-done | bytes 40992 | tf_op jit(solution)/shard_map/ppermute | solution.py:456
  105.6 2.2 %shard_map.117 = (f32[3,32,512]{2,1,0:T(8,128)}, f32[8,8,128]{2,1,0:T(8,128)S(1)}) custom-call(s32[4]{0:T(128)S(1)} %pad_add_fusion.scal.refs_0_, f32[3,32,512]{2,1,0:T(8,128)S(1)} %get-tuple-element.50.refs_1_, f32[8,128]{1,0:T(8,128)S(1)} %get-tuple-element.51.refs_2_, f32[24,128]{1,0:T(8,128)S(1)} %get-tuple-element.52.refs_3_, ...), custom_call_target="tpu_custom_call" | custom-call | tf_op jit(solution)/shard_map/pallas_call | solution.py:393
  107.8 11.0 %all_to_all.28 = f32[8,8,128]{2,1,0:T(8,128)S(1)} all-to-all(f32[8,8,128]{2,1,0:T(8,128)S(1)} %get-tuple-element.57), channel_id=1, replica_groups=mesh['gx'=96,'gy'=8] {'gy'}, dimensions={0} | all-to-all | bytes 65536 | tf_op jit(solution)/shard_map/all_to_all | solution.py:502
  118.8 0.6 copy.14
  (31 shorter events, 0.1 us)
Async XLA Ops:
  0.6 13.6 %copy-start = (s32[8,2]{0,1:T(2,128)S(1)}, s32[8,2]{0,1:T(2,128)}, u32[]{:S(2)}) copy-start(s32[8,2]{0,1:T(2,128)} %param.16) | copy-start | bytes 196
  0.6 0.8 copy-start.4
  0.7 0.7 copy-start.7
  1.4 0.9 copy-start.2
  2.3 0.8 copy-start.5
  3.2 0.7 copy-start.8
  3.9 0.7 copy-start.9
  6.9 32.7 %copy-start.6 = (f32[32,512]{1,0:T(8,128)S(1)}, f32[32,512]{1,0:T(8,128)}, u32[]{:S(2)}) copy-start(f32[32,512]{1,0:T(8,128)} %refs_1_.1) | copy-start | bytes 196612
  6.9 16.5 %all-to-all-start = ((f32[16,24,128]{2,1,0:T(8,128)}), f32[16,24,128]{2,1,0:T(8,128)S(1)}, u32[]{:S(2)}, u32[]{:S(2)}) async-start(f32[16,24,128]{2,1,0:T(8,128)} %bitcast.4), calls=%async_computation | async-start | bytes 393216 | tf_op jit(solution)/shard_map/all_to_all | solution.py:451
  14.2 25.4 %copy-start.3 = (f32[2,32,512]{2,1,0:T(8,128)S(1)}, f32[2,32,512]{2,1,0:T(8,128)}, u32[]{:S(2)}) copy-start(f32[2,32,512]{2,1,0:T(8,128)} %refs_2_.1) | copy-start | bytes 393220
  23.4 16.2 %copy-start.1 = (f32[32,512]{1,0:T(8,128)S(1)}, f32[32,512]{1,0:T(8,128)}, u32[]{:S(2)}) copy-start(f32[32,512]{1,0:T(8,128)} %refs_8_.5) | copy-start | bytes 196612
  23.5 16.0 %collective-permute-start = (f32[144,128]{1,0:T(8,128)S(1)}, f32[144,128]{1,0:T(8,128)S(1)}, u32[]{:S(2)}, u32[]{:S(2)}) collective-permute-start(f32[144,128]{1,0:T(8,128)S(1)} %constant_dynamic-update-slice_fusion), channel_id=1, source_target_pairs={{8,16},{24,32},{40,48},{56,64},{72,80},{88,96},{104,112},{120,128}... | collective-permute-start | bytes 221192 | tf_op jit(solution)/shard_map/ppermute | solution.py:456
  54.9 7.4 %collective-permute-start.1 = (f32[80,128]{1,0:T(8,128)S(1)}, f32[80,128]{1,0:T(8,128)S(1)}, u32[]{:S(2)}, u32[]{:S(2)}) collective-permute-start(f32[80,128]{1,0:T(8,128)S(1)} %pad_maximum_fusion), channel_id=1, source_target_pairs={{8,16},{24,32},{40,48},{56,64},{72,80},{88,96},{104,112},{120,128}... | collective-permute-start | bytes 122888 | tf_op jit(solution)/shard_map/ppermute | solution.py:456
  76.5 7.4 %collective-permute-start.2 = (f32[80,128]{1,0:T(8,128)S(1)}, f32[80,128]{1,0:T(8,128)S(1)}, u32[]{:S(2)}, u32[]{:S(2)}) collective-permute-start(f32[80,128]{1,0:T(8,128)S(1)} %pad_maximum_fusion.1), channel_id=1, source_target_pairs={{8,16},{24,32},{40,48},{56,64},{72,80},{88,96},{104,112},{120,128}... | collective-permute-start | bytes 122888 | tf_op jit(solution)/shard_map/ppermute | solution.py:456
  98.2 7.4 %collective-permute-start.3 = (f32[80,128]{1,0:T(8,128)S(1)}, f32[80,128]{1,0:T(8,128)S(1)}, u32[]{:S(2)}, u32[]{:S(2)}) collective-permute-start(f32[80,128]{1,0:T(8,128)S(1)} %pad_maximum_fusion.2), channel_id=1, source_target_pairs={{8,16},{24,32},{40,48},{56,64},{72,80},{88,96},{104,112},{120,128}... | collective-permute-start | bytes 122888 | tf_op jit(solution)/shard_map/ppermute | solution.py:456

commit v2 on v1

--- a/solution.py
+++ b/solution.py
@@ -24,8 +24,9 @@
 FIELDS = 8
 BASINS = 8
 SLOT_ROWS = 3 * BASINS
-FIRST_ROWS = 24
-STEP_ROWS = 16
+BLOCK = 8
+EDGE = 16
+WHOLE = EDGE + FIELDS * BASINS
 INTERPRET = False
 
 
@@ -170,7 +171,7 @@
     return jnp.concatenate(found, axis=0)
 
 
-def put_edges(send_ref, across_ref, cells, even, mine, other, y, col_row, edge_row):
+def put_edges(send_ref, beside_ref, across_ref, cells, even, mine, y, col_row):
     lane_left = column_to_lane(cells[0][:, 0:1], 0)
     lane_right = column_to_lane(cells[0][:, COLS - 1 : COLS], 0)
     for k in (1, 2):
@@ -186,20 +187,21 @@
         for quad in range(QUADS):
             at = k * QUADS + quad
             lanes = slice(quad * LANES, (quad + 1) * LANES)
-            send_ref[other, y, edge_row + at : edge_row + at + 1, :] = inner[:, lanes]
+            beside_ref[at : at + 1, :] = inner[:, lanes]
             across_ref[at : at + 1, :] = outer[:, lanes]
 
 
-def get_edges(got_ref, over_ref, cells, scal, mine, other, y, col_row, edge_row, over_edge):
+def get_edges(got_ref, near_ref, over_ref, cells, scal, mine, y, col_row):
     even = scal[0] == 0
     is_first, is_last = scal[2] == 1, scal[3] == 1
     before = got_ref[mine, jnp.maximum(y - 1, 0), col_row : col_row + 1, :]
     after = got_ref[mine, jnp.minimum(y + 1, BASINS - 1), col_row : col_row + 1, :]
+    over_edge = BASINS * BLOCK
     top, low, left, right = [], [], [], []
     for k in range(3):
         inner = jnp.concatenate(
             [
-                got_ref[other, y, edge_row + k * QUADS + quad : edge_row + k * QUADS + quad + 1, :]
+                near_ref[k * QUADS + quad : k * QUADS + quad + 1, :]
                 for quad in range(QUADS)
             ],
             axis=1,
@@ -238,12 +240,24 @@
 
 
 def first_kernel(
-    scal, depth, discharge, cell_in, site_in, coeff_in, reach, send_ref, across_ref, cell_ref, site_ref, coeff_ref, slots_ref
+    scal,
+    depth,
+    discharge,
+    cell_in,
+    site_in,
+    coeff_in,
+    reach,
+    send_ref,
+    beside_ref,
+    across_ref,
+    cell_ref,
+    site_ref,
+    coeff_ref,
+    slots_ref,
 ):
     even = scal[0] == 0
     mine, other, y = scal[0], 1 - scal[0], scal[1]
     send_ref[...] = jnp.zeros_like(send_ref)
-    across_ref[...] = jnp.zeros_like(across_ref)
 
     def arranged(ref):
         low, own, high = ref[0:8], ref[8:16], ref[16:24]
@@ -259,19 +273,82 @@
     slots = depth_at_slots(depth, (), cell)
     slots_ref[...] = slots
     site_value = site.astype(jnp.float32)
-    level_rows = [own_row(reach[:, f * LANES : (f + 1) * LANES], y) for f in range(FIELDS)]
     for b in range(BASINS):
         for at, value in enumerate((slots, site_value, coeff)):
             send_ref[mine, b, at : at + 1, :] = value[b : b + 1]
             send_ref[other, b, at : at + 1, :] = value[8 + b : 9 + b]
             send_ref[mine, b, 3 + at : 4 + at, :] = value[16 + b : 17 + b]
+    for ref in (beside_ref, across_ref):
+        ref[0:EDGE] = jnp.zeros((EDGE, LANES), jnp.float32)
         for f in range(FIELDS):
-            send_ref[other, b, 15 + f : 16 + f, :] = level_rows[f]
+            ref[EDGE + 8 * f : EDGE + 8 * f + 8] = reach[:, f * LANES : (f + 1) * LANES]
     cells = [depth[...], discharge[0], discharge[1]]
-    put_edges(send_ref, across_ref, cells, even, mine, other, y, 6, 3)
-
-
-def step_kernel(first, last, *refs):
+    put_edges(send_ref, beside_ref, across_ref, cells, even, mine, y, 6)
+
+
+OVER = BASINS * BLOCK
+
+
+def gathered(got, over, scal, row, across_row):
+    mine, other = scal[0], 1 - scal[0]
+    return jnp.concatenate(
+        [got[mine, :, row, :], got[other, :, row, :], over[pl.ds(across_row, 8, stride=BLOCK), :]],
+        axis=0,
+    )
+
+
+def advance_levels(scal, current, outlets, own, site_owner, coeff_owner, segment_owner, slots_owner):
+    rates = coeff_owner * (segment_owner - slots_owner)
+    lateral = spread(rates, site_owner >> 7, site_owner & (LANES - 1), FIELDS)
+    return river_update(current, outlets, own, lateral)
+
+
+def advance_cells(scal, cells, got, near, over, rough, cell, coeff, segment, slots, col_row):
+    mine, y = scal[0], scal[1]
+    major, minor = cell_parts(cell)
+    rates = coeff * (segment - slots)
+    blocks = spread(rates, major, minor, QUADS * ROWS)
+    source = jnp.concatenate([blocks[q * ROWS : (q + 1) * ROWS] for q in range(QUADS)], axis=1)
+    top, low, left, right = get_edges(got, near, over, cells, scal, mine, y, col_row)
+    return flood_update(cells, top, low, left, right, rough, source)
+
+
+def levels_kernel(scal, levels, owner_levels, owner_site, owner_coeff, got, over, own, all_levels):
+    even = scal[0] == 0
+    outlets = jnp.where(even, over[pl.ds(2, 8, stride=BLOCK), :], got[1 - scal[0], :, 2, :])
+    new = advance_levels(
+        scal,
+        levels[...],
+        outlets,
+        own[...],
+        owner_site[...],
+        owner_coeff[...],
+        owner_levels[...],
+        gathered(got, over, scal, 0, 3),
+    )
+    for b in range(BASINS):
+        all_levels[b] = new
+
+
+def cells_kernel(scal, state, got, near, over, rough, cell_ref, coeff_ref, slots_ref, state_out):
+    new = advance_cells(
+        scal,
+        [state[0], state[1], state[2]],
+        got,
+        near,
+        over,
+        rough[...],
+        cell_ref[...],
+        coeff_ref[...],
+        gathered(got, over, scal, 1, 4),
+        slots_ref[...],
+        5,
+    )
+    for k in range(3):
+        state_out[k] = new[k]
+
+
+def step_kernel(first, *refs):
     refs = list(refs)
 
     def take(n):
@@ -281,47 +358,34 @@
 
     (scal,) = take(1)
     if first:
-        depth, discharge, reach = take(3)
+        depth, discharge, reach, site_ref = take(4)
     else:
         state, levels, owner_levels, owner_site, owner_coeff = take(5)
-    got, over, rough, own, cell_ref, coeff_ref, slots_ref = take(7)
+    got, near, over, rough, own, cell_ref, coeff_ref, slots_ref = take(8)
+    state_out, levels_out, owner_levels_out, slots_out, send_ref, beside_ref, across_ref = take(7)
     if first:
-        (site_ref,) = take(1)
-    (state_out,) = take(1)
-    if last:
-        (all_levels,) = take(1)
-    else:
-        levels_out, owner_levels_out, slots_out, send_ref, across_ref = take(5)
-        if first:
-            owner_site_out, owner_coeff_out = take(2)
+        owner_site_out, owner_coeff_out = take(2)
     even = scal[0] == 0
     mine, other, y = scal[0], 1 - scal[0], scal[1]
     cell = cell_ref[...]
 
-    def gathered(row, across_row):
-        return jnp.concatenate(
-            [got[mine, :, row, :], got[other, :, row, :], over[pl.ds(across_row, 8, stride=8), :]],
-            axis=0,
-        )
-
+    slots_owner = gathered(got, over, scal, 0, 3)
     if first:
         cells = [depth[...], discharge[0], discharge[1]]
         current = jnp.concatenate(
             [own_row(reach[:, f * LANES : (f + 1) * LANES], y) for f in range(FIELDS)], axis=0
         )
-        over_edge = 64
 
         def tile_rows(f, v):
             if v == 0:
                 return reach[:, f * LANES : (f + 1) * LANES]
             if v == 1:
-                return got[other, :, 15 + f, :]
-            return over[80 + 8 * f : 88 + 8 * f, :]
+                return near[EDGE + 8 * f : EDGE + 8 * f + 8, :]
+            return over[OVER + EDGE + 8 * f : OVER + EDGE + 8 * f + 8, :]
 
         segment = level_at_sites(tile_rows, site_ref[...])
-        site_owner = gathered(1, 4).astype(jnp.int32)
-        coeff_owner = gathered(2, 5)
-        slots_owner = gathered(0, 3)
+        site_owner = gathered(got, over, scal, 1, 4).astype(jnp.int32)
+        coeff_owner = gathered(got, over, scal, 2, 5)
         outlets = jnp.zeros((BASINS, LANES), jnp.float32)
         for f in range(FIELDS):
             source_rows = jnp.where(even, tile_rows(f, 2), tile_rows(f, 1))
@@ -331,44 +395,35 @@
         segment_owner = level_at_sites(
             lambda f, v: jnp.broadcast_to(current[f : f + 1], (8, LANES)), site_owner
         )
-        edge_rows = (6, 3)
+        owner_site_out[...] = site_owner
+        owner_coeff_out[...] = coeff_owner
     else:
         cells = [state[0], state[1], state[2]]
         current = levels[...]
-        over_edge = 64
-        segment = gathered(1, 4)
-        slots_owner = gathered(0, 3)
+        segment = gathered(got, over, scal, 1, 4)
         site_owner = owner_site[...]
         coeff_owner = owner_coeff[...]
         segment_owner = owner_levels[...]
-        outlets = jnp.where(even, over[pl.ds(2, 8, stride=8), :], got[other, :, 2, :])
-        edge_rows = (5, 3)
-
-    rates_owner = coeff_owner * (segment_owner - slots_owner)
-    lateral = spread(rates_owner, site_owner >> 7, site_owner & (LANES - 1), FIELDS)
-    levels_next = river_update(current, outlets, own[...], lateral)
-
-    major, minor = cell_parts(cell)
-    rates = coeff_ref[...] * (segment - slots_ref[...])
-    blocks = spread(rates, major, minor, QUADS * ROWS)
-    source = jnp.concatenate([blocks[q * ROWS : (q + 1) * ROWS] for q in range(QUADS)], axis=1)
-    top, low, left, right = get_edges(
-        got, over, cells, scal, mine, other, y, edge_rows[0], edge_rows[1], over_edge
-    )
-    new = flood_update(cells, top, low, left, right, rough[...], source)
+        outlets = jnp.where(even, over[pl.ds(2, 8, stride=BLOCK), :], got[other, :, 2, :])
+
+    levels_next = advance_levels(
+        scal, current, outlets, own[...], site_owner, coeff_owner, segment_owner, slots_owner
+    )
+    new = advance_cells(
+        scal,
+        cells,
+        got,
+        near,
+        over,
+        rough[...],
+        cell,
+        coeff_ref[...],
+        segment,
+        slots_ref[...],
+        6 if first else 5,
+    )
     for k in range(3):
         state_out[k] = new[k]
-
-    if last:
-        for b in range(BASINS):
-            all_levels[b] = levels_next
-        return
-
-    if first:
-        owner_site_out[...] = site_owner
-        owner_coeff_out[...] = coeff_owner
-    send_ref[...] = jnp.zeros_like(send_ref)
-    across_ref[...] = jnp.zeros_like(across_ref)
     levels_out[...] = levels_next
     owned = level_at_sites(
         lambda f, v: jnp.broadcast_to(levels_next[f : f + 1], (8, LANES)), site_owner
@@ -376,6 +431,9 @@
     owner_levels_out[...] = owned
     slots = depth_at_slots(state_out, (0,), cell)
     slots_out[...] = slots
+    send_ref[...] = jnp.zeros_like(send_ref)
+    beside_ref[...] = jnp.zeros_like(beside_ref)
+    across_ref[...] = jnp.zeros_like(across_ref)
     outlet_row = column_to_lane(levels_next[:, LANES - 1 : LANES], 0)
     for b in range(BASINS):
         for at, value in enumerate((slots, owned)):
@@ -384,10 +442,10 @@
             send_ref[mine, b, 3 + at : 4 + at, :] = value[16 + b : 17 + b]
         send_ref[mine, b, 2:3, :] = outlet_row
         send_ref[other, b, 2:3, :] = outlet_row
-    put_edges(send_ref, across_ref, new, even, mine, other, y, 5, 3)
-
-
-def call(kernel, outs, args):
+    put_edges(send_ref, beside_ref, across_ref, new, even, mine, y, 5)
+
+
+def call(kernel, outs, args, limit=16 << 20):
     specs = [pl.BlockSpec(memory_space=pltpu.SMEM)]
     specs += [pl.BlockSpec(memory_space=pltpu.VMEM) for _ in args[1:]]
     return pl.pallas_call(
@@ -395,7 +453,7 @@
         out_shape=outs,
         in_specs=specs,
         out_specs=[pl.BlockSpec(memory_space=pltpu.VMEM) for _ in outs],
-        compiler_params=None if INTERPRET else pltpu.CompilerParams(vmem_limit_bytes=16 << 20),
+        compiler_params=None if INTERPRET else pltpu.CompilerParams(vmem_limit_bytes=limit),
         interpret=INTERPRET,
     )(*args)
 
@@ -428,6 +486,7 @@
     pairs = [list(range(c * 2 * count_y, (c + 1) * 2 * count_y)) for c in range(count_x // 2)]
     border = [(i, i + 1) for i in range(1, count_x - 1, 2)]
     border = border + [(b, a) for a, b in border]
+    chip = [(i, i ^ 1) for i in range(count_x)]
     scal = jnp.stack(
         [core, gy, (gx == 0).astype(jnp.int32), (gx == count_x - 1).astype(jnp.int32)]
     ).astype(jnp.int32)
@@ -446,60 +505,60 @@
         axis=0,
     )
 
-    def exchange(send, across, extra):
-        rows = send.shape[2]
+    def exchange(send, beside, across):
         got = lax.all_to_all(
-            send.reshape(2 * BASINS, rows, LANES), ("gx", "gy"), 0, 0, axis_index_groups=pairs
-        )
-        part = lax.dynamic_slice(got, (core * BASINS, 0, 0), (BASINS, 8, LANES))
-        packed = jnp.concatenate([part.reshape(BASINS * 8, LANES), across] + extra, axis=0)
-        over = lax.ppermute(packed, "gx", border)
-        return got.reshape(2, BASINS, rows, LANES), over
-
-    send, across, cell, site, coeff, slots = call(
+            send.reshape(2 * BASINS, BLOCK, LANES), ("gx", "gy"), 0, 0, axis_index_groups=pairs
+        )
+        near = lax.ppermute(beside, "gx", chip)
+        got, near = lax.optimization_barrier((got, near))
+        part = lax.dynamic_slice(got, (core * BASINS, 0, 0), (BASINS, BLOCK, LANES))
+        over = lax.ppermute(
+            jnp.concatenate([part.reshape(BASINS * BLOCK, LANES), across], axis=0), "gx", border
+        )
+        return got.reshape(2, BASINS, BLOCK, LANES), near, over
+
+    table = (SLOT_ROWS, LANES)
+    block = f32(2, BASINS, BLOCK, LANES)
+    send, beside, across, cell, site, coeff, slots = call(
         first_kernel,
-        [
-            f32(2, BASINS, FIRST_ROWS, LANES),
-            f32(16, LANES),
-            i32(SLOT_ROWS, LANES),
-            i32(SLOT_ROWS, LANES),
-            f32(SLOT_ROWS, LANES),
-            f32(SLOT_ROWS, LANES),
-        ],
+        [block, f32(WHOLE, LANES), f32(WHOLE, LANES), i32(*table), i32(*table), f32(*table), f32(*table)],
         [scal, depth, discharge, bank_cell, bank_site, bank_coeff, reach_state],
-    )
-    fields_major = [reach_state[:, f * LANES : (f + 1) * LANES] for f in range(FIELDS)]
-    got, over = exchange(send, across, fields_major)
-    for step in range(STEPS):
-        first, last = step == 0, step == STEPS - 1
-        outs = [f32(3, ROWS, COLS)]
-        if last:
-            outs += [f32(BASINS, FIELDS, LANES)]
-        else:
-            outs += [
-                f32(FIELDS, LANES),
-                f32(SLOT_ROWS, LANES),
-                f32(SLOT_ROWS, LANES),
-                f32(2, BASINS, STEP_ROWS, LANES),
-                f32(16, LANES),
-            ]
+        limit=60 << 20,
+    )
+    got, near, over = exchange(send, beside, across)
+    for step in range(STEPS - 1):
+        first = step == 0
+        outs = [
+            f32(3, ROWS, COLS),
+            f32(FIELDS, LANES),
+            f32(*table),
+            f32(*table),
+            block,
+            f32(EDGE, LANES),
+            f32(EDGE, LANES),
+        ]
         if first:
-            outs += [i32(SLOT_ROWS, LANES), f32(SLOT_ROWS, LANES)]
-            args = [scal, depth, discharge, reach_state]
+            outs += [i32(*table), f32(*table)]
+            args = [scal, depth, discharge, reach_state, site]
         else:
             args = [scal, state, levels, owner_levels, owner_site, owner_coeff]
-        args += [got, over, roughness, own, cell, coeff, slots]
+        args += [got, near, over, roughness, own, cell, coeff, slots]
+        result = call(functools.partial(step_kernel, first), outs, args)
+        state, levels, owner_levels, slots, send, beside, across = result[:7]
         if first:
-            args += [site]
-        result = call(functools.partial(step_kernel, first, last), outs, args)
-        state = result[0]
-        if last:
-            break
-        levels, owner_levels, slots, send, across = result[1:6]
-        if first:
-            owner_site, owner_coeff = result[6:8]
-        got, over = exchange(send, across, [])
-    final = lax.all_to_all(result[1], "gy", 0, 0)
+            owner_site, owner_coeff = result[7:9]
+        got, near, over = exchange(send, beside, across)
+    copies = call(
+        levels_kernel,
+        [f32(BASINS, FIELDS, LANES)],
+        [scal, levels, owner_levels, owner_site, owner_coeff, got, over, own],
+    )[0]
+    final = lax.all_to_all(copies, "gy", 0, 0)
+    state = call(
+        cells_kernel,
+        [f32(3, ROWS, COLS)],
+        [scal, state, got, near, over, roughness, cell, coeff, slots],
+    )[0]
     return state, final.reshape(BASINS, FIELDS * LANES)
 
 

time: 120 us -> 116 us (0.967)
  blocking collectives: 46.8 us -> 0 us
  starting transfers between devices: 33.5 us -> 54.7 us
  waiting for transfers between devices: 20.2 us -> 41.3 us
  local copies, waits for them, and re-layouts: 5.46 us -> 1.66 us
  Pallas kernels: 12.4 us -> 16 us
    all_to_all x4 -> x0, blocking collectives: 46.8 us -> none  [the longest x3 35.8 us: exchange(): lax.all_to_all(send.reshape(2 * BASINS, rows, LANES), ('gx', 'gy'), 0, 0,...]
    all_to_all x1 -> x5, waiting for transfers between devices: 8.14 us -> 24.9 us  [the longest x4 19 us: exchange(): lax.all_to_all(send.reshape(2 * BASINS, BLOCK, LANES), ('gx', 'gy'), 0, 0...]
    all_to_all x1 -> x5, starting transfers between devices: 7.34 us -> 21.2 us  [the longest x4 17.9 us: exchange(): lax.all_to_all(send.reshape(2 * BASINS, BLOCK, LANES), ('gx', 'gy'), 0, 0...]
    ppermute x4 -> x8, starting transfers between devices: 26.1 us -> 33.5 us  [the longest x4 24.4 us: exchange(): lax.ppermute(jnp.concatenate([part.reshape(BASINS * BLOCK, LANES), across...]
    ppermute x4 -> x8, waiting for transfers between devices: 12.1 us -> 16.5 us  [the longest x4 14 us: exchange(): lax.ppermute(jnp.concatenate([part.reshape(BASINS * BLOCK, LANES), across...]
    unnamed x30 -> x23, local copies, waits for them, and re-layouts: 4.48 us -> 0.68 us
    pallas_call x5 -> x6, Pallas kernels: 12.4 us -> 16 us  [call(): pl.pallas_call(kernel, out_shape=outs, in_specs=specs, out_specs=[pl.Bloc...]
  transfers between devices with their start and end apart: 5 -> 13, of which waited for: 5 -> 12; matrix products, arithmetic and copies ran while one was open for 1% -> 1% of each run, Pallas kernels for 0% -> 2%
where the time goes in v2:
time: 116 us; the launch traced here: 115 us
  starting transfers between devices  54.7 us (47%)
  waiting for transfers between devices  41.3 us (36%)
  Pallas kernels  16 us (14%)
  local copies, waits for them, and re-layouts  1.66 us (1%)
    ppermute x4, starting transfers between devices, exchange(): lax.ppermute(jnp.concatenate([part.reshape(BASINS * BLOCK, LANES), across...  24.4 us
    all_to_all x4, waiting for transfers between devices, exchange(): lax.all_to_all(send.reshape(2 * BASINS, BLOCK, LANES), ('gx', 'gy'), 0, 0...  19 us
    all_to_all x4, starting transfers between devices, exchange(): lax.all_to_all(send.reshape(2 * BASINS, BLOCK, LANES), ('gx', 'gy'), 0, 0...  17.9 us
    pallas_call x6, Pallas kernels, call(): pl.pallas_call(kernel, out_shape=outs, in_specs=specs, out_specs=[pl.Bloc...  16 us
    ppermute x4, waiting for transfers between devices, exchange(): lax.ppermute(jnp.concatenate([part.reshape(BASINS * BLOCK, LANES), across...  14 us
    ppermute x4, starting transfers between devices, exchange(): near = lax.ppermute(beside, 'gx', chip)  9.01 us
    all_to_all x1, waiting for transfers between devices, per_device(): final = lax.all_to_all(copies, 'gy', 0, 0)  5.88 us
    all_to_all x1, starting transfers between devices, per_device(): final = lax.all_to_all(copies, 'gy', 0, 0)  3.34 us
  transfers between devices with their start and end apart: 13, of which 12 were waited for; matrix products, arithmetic and copies ran while one was open for 1% of the time, Pallas kernels for 2%

profile of v2, /device:TPU:6, one launch (start us, length us, event | category | flops | bytes accessed | tf_op | source)
XLA Modules:
  0.0 115.4 jit_solution(15869632938521097841)
XLA Ops:
  1.3 2.6 %shard_map.113 = (f32[2,8,8,128]{3,2,1,0:T(8,128)}, f32[80,128]{1,0:T(8,128)}, f32[80,128]{1,0:T(8,128)}, s32[24,128]{1,0:T(8,128)}, s32[24,128]{1,0:T(8,128)}, /*index=5*/f32[24,128]{1,0:T(8,128)}, f32[24,128]{1,0:T(8,128)}) custom-call(s32[4]{0:T(128)} %pad_add_fusion.scal.refs_0_, f32[32,512]{1,0:T(8,128)} %refs_1_.1, f32[2,32,512]{2,1,0:T(8,128)} %refs_2_.1, ...), custom_call_target="tpu_custom_call" | custom-call | tf_op jit(solution)/shard_map/pallas_call | solution.py:451
  4.0 7.3 %all-to-all-start = ((f32[16,8,128]{2,1,0:T(8,128)}), f32[16,8,128]{2,1,0:T(8,128)S(1)}, u32[]{:S(2)}, u32[]{:S(2)}) async-start(f32[16,8,128]{2,1,0:T(8,128)} %bitcast.34), calls=%async_computation | async-start | bytes 131072 | tf_op jit(solution)/shard_map/all_to_all | solution.py:509
  11.4 2.3 %collective-permute-start = (f32[80,128]{1,0:T(8,128)}, f32[80,128]{1,0:T(8,128)S(1)}, u32[]{:S(2)}, u32[]{:S(2)}) collective-permute-start(f32[80,128]{1,0:T(8,128)} %get-tuple-element.42), channel_id=1, source_target_pairs={{0,8},{8,0},{16,24},{24,16},{32,40},{40,32},{48,56},{56,48},{64,72... | collective-permute-start | bytes 122888 | tf_op jit(solution)/shard_map/ppermute | solution.py:512
  14.0 0.7 fusion.2
  14.8 4.6 %all-to-all-done = f32[16,8,128]{2,1,0:T(8,128)S(1)} async-done(((f32[16,8,128]{2,1,0:T(8,128)}), f32[16,8,128]{2,1,0:T(8,128)S(1)}, u32[]{:S(2)}, u32[]{:S(2)}) %all-to-all-start) | async-done | bytes 65568 | tf_op jit(solution)/shard_map/all_to_all | solution.py:509
  19.4 14.2 %collective-permute-start.1 = (f32[144,128]{1,0:T(8,128)S(1)}, f32[144,128]{1,0:T(8,128)S(1)}, u32[]{:S(2)}, u32[]{:S(2)}) collective-permute-start(f32[144,128]{1,0:T(8,128)S(1)} %pad_maximum_fusion), channel_id=1, source_target_pairs={{8,16},{24,32},{40,48},{56,64},{72,80},{88,96},{104,112},{120,128}... | collective-permute-start | bytes 221192 | tf_op jit(solution)/shard_map/ppermute | solution.py:515
  33.7 1.9 %collective-permute-done.1.refs_7_ = f32[144,128]{1,0:T(8,128)S(1)} collective-permute-done((f32[144,128]{1,0:T(8,128)S(1)}, f32[144,128]{1,0:T(8,128)S(1)}, u32[]{:S(2)}, u32[]{:S(2)}) %collective-permute-start.1) | collective-permute-done | bytes 73760 | tf_op jit(solution)/shard_map/ppermute | solution.py:515
  35.8 3.3 %shard_map.114 = (f32[3,32,512]{2,1,0:T(8,128)S(1)}, f32[8,128]{1,0:T(8,128)S(1)}, f32[24,128]{1,0:T(8,128)S(1)}, f32[24,128]{1,0:T(8,128)S(1)}, f32[2,8,8,128]{...) custom-call(s32[4]{0:T(128)S(1)} %copy-done.7, ...), custom_call_target="tpu_custom_call" | custom-call | tf_op jit(solution)/shard_map/pallas_call | solution.py:451
  39.1 3.5 %all-to-all-start.1 = ((f32[16,8,128]{2,1,0:T(8,128)}), f32[16,8,128]{2,1,0:T(8,128)S(1)}, u32[]{:S(2)}, u32[]{:S(2)}) async-start(f32[16,8,128]{2,1,0:T(8,128)} %bitcast.9), calls=%async_computation.1 | async-start | bytes 131072 | tf_op jit(solution)/shard_map/all_to_all | solution.py:509
  42.6 2.2 %collective-permute-start.2 = (f32[16,128]{1,0:T(8,128)S(1)}, f32[16,128]{1,0:T(8,128)S(1)}, u32[]{:S(2)}, u32[]{:S(2)}) collective-permute-start(f32[16,128]{1,0:T(8,128)S(1)} %get-tuple-element.55), channel_id=1, source_target_pairs={{0,8},{8,0},{16,24},{24,16},{32,40},{40,32},{48,56},{56,48},{64,72... | collective-permute-start | bytes 24584 | tf_op jit(solution)/shard_map/ppermute | solution.py:512
  44.8 0.8 collective-permute-done.2.refs_7_
  45.7 4.8 %all-to-all-done.1 = f32[16,8,128]{2,1,0:T(8,128)S(1)} async-done(((f32[16,8,128]{2,1,0:T(8,128)}), f32[16,8,128]{2,1,0:T(8,128)S(1)}, u32[]{:S(2)}, u32[]{:S(2)}) %all-to-all-start.1) | async-done | bytes 65568 | tf_op jit(solution)/shard_map/all_to_all | solution.py:509
  50.5 4.7 %collective-permute-start.3 = (f32[80,128]{1,0:T(8,128)S(1)}, f32[80,128]{1,0:T(8,128)S(1)}, u32[]{:S(2)}, u32[]{:S(2)}) collective-permute-start(f32[80,128]{1,0:T(8,128)S(1)} %pad_maximum_fusion.1), channel_id=1, source_target_pairs={{8,16},{24,32},{40,48},{56,64},{72,80},{88,96},{104,112},{120,128}... | collective-permute-start | bytes 122888 | tf_op jit(solution)/shard_map/ppermute | solution.py:515
  55.2 2.7 %collective-permute-done.3.refs_8_ = f32[80,128]{1,0:T(8,128)S(1)} collective-permute-done((f32[80,128]{1,0:T(8,128)S(1)}, f32[80,128]{1,0:T(8,128)S(1)}, u32[]{:S(2)}, u32[]{:S(2)}) %collective-permute-start.3) | collective-permute-done | bytes 40992 | tf_op jit(solution)/shard_map/ppermute | solution.py:515
  57.9 3.2 %shard_map.115 = (f32[3,32,512]{2,1,0:T(8,128)S(1)}, f32[8,128]{1,0:T(8,128)S(1)}, f32[24,128]{1,0:T(8,128)S(1)}, f32[24,128]{1,0:T(8,128)S(1)}, f32[2,8,8,128]{...) custom-call(s32[4]{0:T(128)S(1)} %copy-done.7, f32[3,32,512]{2,1,0:T(8,128)S(1)} %get-tuple-element.49.refs_1_, ...), custom_call_target="tpu_custom_call" | custom-call | tf_op jit(solution)/shard_map/pallas_call | solution.py:451
  61.1 3.5 %all-to-all-start.2 = ((f32[16,8,128]{2,1,0:T(8,128)}), f32[16,8,128]{2,1,0:T(8,128)S(1)}, u32[]{:S(2)}, u32[]{:S(2)}) async-start(f32[16,8,128]{2,1,0:T(8,128)} %bitcast.12), calls=%async_computation.2 | async-start | bytes 131072 | tf_op jit(solution)/shard_map/all_to_all | solution.py:509
  64.6 2.2 %collective-permute-start.4 = (f32[16,128]{1,0:T(8,128)S(1)}, f32[16,128]{1,0:T(8,128)S(1)}, u32[]{:S(2)}, u32[]{:S(2)}) collective-permute-start(f32[16,128]{1,0:T(8,128)S(1)} %get-tuple-element.64), channel_id=1, source_target_pairs={{0,8},{8,0},{16,24},{24,16},{32,40},{40,32},{48,56},{56,48},{64,72... | collective-permute-start | bytes 24584 | tf_op jit(solution)/shard_map/ppermute | solution.py:512
  66.9 0.8 collective-permute-done.4.refs_7_
  67.7 4.8 %all-to-all-done.2 = f32[16,8,128]{2,1,0:T(8,128)S(1)} async-done(((f32[16,8,128]{2,1,0:T(8,128)}), f32[16,8,128]{2,1,0:T(8,128)S(1)}, u32[]{:S(2)}, u32[]{:S(2)}) %all-to-all-start.2) | async-done | bytes 65568 | tf_op jit(solution)/shard_map/all_to_all | solution.py:509
  72.5 3.4 %collective-permute-start.5 = (f32[80,128]{1,0:T(8,128)S(1)}, f32[80,128]{1,0:T(8,128)S(1)}, u32[]{:S(2)}, u32[]{:S(2)}) collective-permute-start(f32[80,128]{1,0:T(8,128)S(1)} %pad_maximum_fusion.2), channel_id=1, source_target_pairs={{8,16},{24,32},{40,48},{56,64},{72,80},{88,96},{104,112},{120,128}... | collective-permute-start | bytes 122888 | tf_op jit(solution)/shard_map/ppermute | solution.py:515
  75.9 4.0 %collective-permute-done.5.refs_8_ = f32[80,128]{1,0:T(8,128)S(1)} collective-permute-done((f32[80,128]{1,0:T(8,128)S(1)}, f32[80,128]{1,0:T(8,128)S(1)}, u32[]{:S(2)}, u32[]{:S(2)}) %collective-permute-start.5) | collective-permute-done | bytes 40992 | tf_op jit(solution)/shard_map/ppermute | solution.py:515
  80.0 3.2 %shard_map.116 = (f32[3,32,512]{2,1,0:T(8,128)S(1)}, f32[8,128]{1,0:T(8,128)S(1)}, f32[24,128]{1,0:T(8,128)S(1)}, f32[24,128]{1,0:T(8,128)S(1)}, f32[2,8,8,128]{...) custom-call(s32[4]{0:T(128)S(1)} %copy-done.7, f32[3,32,512]{2,1,0:T(8,128)S(1)} %get-tuple-element.60.refs_1_, ...), custom_call_target="tpu_custom_call" | custom-call | tf_op jit(solution)/shard_map/pallas_call | solution.py:451
  83.2 3.5 %all-to-all-start.3 = ((f32[16,8,128]{2,1,0:T(8,128)}), f32[16,8,128]{2,1,0:T(8,128)S(1)}, u32[]{:S(2)}, u32[]{:S(2)}) async-start(f32[16,8,128]{2,1,0:T(8,128)} %bitcast.15), calls=%async_computation.3 | async-start | bytes 131072 | tf_op jit(solution)/shard_map/all_to_all | solution.py:509
  86.7 2.2 %collective-permute-start.6 = (f32[16,128]{1,0:T(8,128)S(1)}, f32[16,128]{1,0:T(8,128)S(1)}, u32[]{:S(2)}, u32[]{:S(2)}) collective-permute-start(f32[16,128]{1,0:T(8,128)S(1)} %get-tuple-element.71), channel_id=1, source_target_pairs={{0,8},{8,0},{16,24},{24,16},{32,40},{40,32},{48,56},{56,48},{64,72... | collective-permute-start | bytes 24584 | tf_op jit(solution)/shard_map/ppermute | solution.py:512
  88.9 0.8 collective-permute-done.6.near
  89.7 4.8 %all-to-all-done.3 = f32[16,8,128]{2,1,0:T(8,128)S(1)} async-done(((f32[16,8,128]{2,1,0:T(8,128)}), f32[16,8,128]{2,1,0:T(8,128)S(1)}, u32[]{:S(2)}, u32[]{:S(2)}) %all-to-all-start.3) | async-done | bytes 65568 | tf_op jit(solution)/shard_map/all_to_all | solution.py:509
  94.6 2.1 %collective-permute-start.7 = (f32[80,128]{1,0:T(8,128)S(1)}, f32[80,128]{1,0:T(8,128)S(1)}, u32[]{:S(2)}, u32[]{:S(2)}) collective-permute-start(f32[80,128]{1,0:T(8,128)S(1)} %pad_maximum_fusion.3), channel_id=1, source_target_pairs={{8,16},{24,32},{40,48},{56,64},{72,80},{88,96},{104,112},{120,128}... | collective-permute-start | bytes 122888 | tf_op jit(solution)/shard_map/ppermute | solution.py:515
  96.7 5.3 %collective-permute-done.7.over = f32[80,128]{1,0:T(8,128)S(1)} collective-permute-done((f32[80,128]{1,0:T(8,128)S(1)}, f32[80,128]{1,0:T(8,128)S(1)}, u32[]{:S(2)}, u32[]{:S(2)}) %collective-permute-start.7) | collective-permute-done | bytes 40992 | tf_op jit(solution)/shard_map/ppermute | solution.py:515
  102.0 1.5 %shard_map.118 = f32[8,8,128]{2,1,0:T(8,128)} custom-call(s32[4]{0:T(128)S(1)} %copy-done.7, f32[8,128]{1,0:T(8,128)S(1)} %get-tuple-element.76.levels, f32[24,128]{1,0:T(8,128)S(1)} %get-tuple-element.77.owner_levels, s32[24,128]{1,0:T(8,128)S(1)} %get-tuple-element.52.refs_4_.owner_site, f32[24,128]{1,0:T(8,128)S(1)} %get-tuple-element.53.refs_5_.owner_coeff, ...), custom_call_target="tpu_custom_call" | custom-call | tf_op jit(solution)/shard_map/pallas_call | solution.py:451
  103.5 3.3 %all-to-all-start.4 = ((f32[8,8,128]{2,1,0:T(8,128)}), f32[8,8,128]{2,1,0:T(8,128)S(1)}, u32[]{:S(2)}, u32[]{:S(2)}) async-start(f32[8,8,128]{2,1,0:T(8,128)} %shard_map.118), calls=%async_computation.4 | async-start | bytes 65536 | tf_op jit(solution)/shard_map/all_to_all | solution.py:556
  106.8 2.1 %shard_map.117 = f32[3,32,512]{2,1,0:T(8,128)} custom-call(s32[4]{0:T(128)S(1)} %copy-done.7, f32[3,32,512]{2,1,0:T(8,128)S(1)} %get-tuple-element.69.state, f32[2,8,8,128]{3,2,1,0:T(8,128)S(1)} %bitcast.29, f32[16,128]{1,0:T(8,128)S(1)} %collective-permute-done.6.near, f32[80,128]{1,0:T(8,128)S(1)} %collective-permute-done.7.over, f32[32,512]{1,0:T(8,128)S(1)} %copy-done.1, ...), custom_call_target="tpu_custom_call" | custom-call | tf_op jit(solution)/shard_map/pallas_call | solution.py:451
  108.9 5.9 %all-to-all-done.4 = f32[8,8,128]{2,1,0:T(8,128)S(1)} async-done(((f32[8,8,128]{2,1,0:T(8,128)}), f32[8,8,128]{2,1,0:T(8,128)S(1)}, u32[]{:S(2)}, u32[]{:S(2)}) %all-to-all-start.4) | async-done | bytes 32800 | tf_op jit(solution)/shard_map/all_to_all | solution.py:556
  (38 shorter events, 1.8 us)
Async XLA Ops:
  0.6 13.1 %copy-start = (s32[8,2]{0,1:T(2,128)S(1)}, s32[8,2]{0,1:T(2,128)}, u32[]{:S(2)}) copy-start(s32[8,2]{0,1:T(2,128)} %param.16) | copy-start | bytes 196
  4.0 15.4 %copy-start.10 = (f32[80,128]{1,0:T(8,128)S(1)}, f32[80,128]{1,0:T(8,128)}, u32[]{:S(2)}) copy-start(f32[80,128]{1,0:T(8,128)} %get-tuple-element.45) | copy-start | bytes 122884
  4.0 31.7 %copy-start.4 = (s32[24,128]{1,0:T(8,128)S(1)}, s32[24,128]{1,0:T(8,128)}, u32[]{:S(2)}) copy-start(s32[24,128]{1,0:T(8,128)} %get-tuple-element.46.refs_10_.refs_11_.cell_ref) | copy-start | bytes 36868
  4.0 31.7 %copy-start.5 = (f32[24,128]{1,0:T(8,128)S(1)}, f32[24,128]{1,0:T(8,128)}, u32[]{:S(2)}) copy-start(f32[24,128]{1,0:T(8,128)} %get-tuple-element.47.refs_11_.refs_12_.coeff_ref) | copy-start | bytes 36868
  4.0 31.7 %copy-start.6 = (f32[8,1024]{1,0:T(8,128)S(1)}, f32[8,1024]{1,0:T(8,128)}, u32[]{:S(2)}) copy-start(f32[8,1024]{1,0:T(8,128)} %refs_3_.1) | copy-start | bytes 98308
  4.0 31.7 %copy-start.8 = (s32[24,128]{1,0:T(8,128)S(1)}, s32[24,128]{1,0:T(8,128)}, u32[]{:S(2)}) copy-start(s32[24,128]{1,0:T(8,128)} %get-tuple-element.40.refs_4_) | copy-start | bytes 36868
  4.0 31.7 %copy-start.9 = (f32[24,128]{1,0:T(8,128)S(1)}, f32[24,128]{1,0:T(8,128)}, u32[]{:S(2)}) copy-start(f32[24,128]{1,0:T(8,128)} %get-tuple-element.48.refs_12_) | copy-start | bytes 36868
  4.0 15.3 %all-to-all-start = ((f32[16,8,128]{2,1,0:T(8,128)}), f32[16,8,128]{2,1,0:T(8,128)S(1)}, u32[]{:S(2)}, u32[]{:S(2)}) async-start(f32[16,8,128]{2,1,0:T(8,128)} %bitcast.34), calls=%async_computation | async-start | bytes 131072 | tf_op jit(solution)/shard_map/all_to_all | solution.py:509
  11.4 3.4 %collective-permute-start = (f32[80,128]{1,0:T(8,128)}, f32[80,128]{1,0:T(8,128)S(1)}, u32[]{:S(2)}, u32[]{:S(2)}) collective-permute-start(f32[80,128]{1,0:T(8,128)} %get-tuple-element.42), channel_id=1, source_target_pairs={{0,8},{8,0},{16,24},{24,16},{32,40},{40,32},{48,56},{56,48},{64,72... | collective-permute-start | bytes 122888 | tf_op jit(solution)/shard_map/ppermute | solution.py:512
  13.7 22.0 %copy-start.7 = (s32[4]{0:T(128)S(1)}, s32[4]{0:T(128)}, u32[]{:S(2)}) copy-start(s32[4]{0:T(128)} %pad_add_fusion.scal.refs_0_) | copy-start | bytes 52
  13.7 22.0 %copy-start.2 = (f32[2,32,512]{2,1,0:T(8,128)S(1)}, f32[2,32,512]{2,1,0:T(8,128)}, u32[]{:S(2)}) copy-start(f32[2,32,512]{2,1,0:T(8,128)} %refs_2_.1) | copy-start | bytes 393220
  19.4 16.4 %copy-start.1 = (f32[32,512]{1,0:T(8,128)S(1)}, f32[32,512]{1,0:T(8,128)}, u32[]{:S(2)}) copy-start(f32[32,512]{1,0:T(8,128)} %rough.1) | copy-start | bytes 196612
  19.4 16.4 %copy-start.3 = (f32[32,512]{1,0:T(8,128)S(1)}, f32[32,512]{1,0:T(8,128)}, u32[]{:S(2)}) copy-start(f32[32,512]{1,0:T(8,128)} %refs_1_.1) | copy-start | bytes 196612
  19.4 16.2 %collective-permute-start.1 = (f32[144,128]{1,0:T(8,128)S(1)}, f32[144,128]{1,0:T(8,128)S(1)}, u32[]{:S(2)}, u32[]{:S(2)}) collective-permute-start(f32[144,128]{1,0:T(8,128)S(1)} %pad_maximum_fusion), channel_id=1, source_target_pairs={{8,16},{24,32},{40,48},{56,64},{72,80},{88,96},{104,112},{120,128}... | collective-permute-start | bytes 221192 | tf_op jit(solution)/shard_map/ppermute | solution.py:515
  39.1 11.4 %all-to-all-start.1 = ((f32[16,8,128]{2,1,0:T(8,128)}), f32[16,8,128]{2,1,0:T(8,128)S(1)}, u32[]{:S(2)}, u32[]{:S(2)}) async-start(f32[16,8,128]{2,1,0:T(8,128)} %bitcast.9), calls=%async_computation.1 | async-start | bytes 131072 | tf_op jit(solution)/shard_map/all_to_all | solution.py:509
  42.6 3.1 %collective-permute-start.2 = (f32[16,128]{1,0:T(8,128)S(1)}, f32[16,128]{1,0:T(8,128)S(1)}, u32[]{:S(2)}, u32[]{:S(2)}) collective-permute-start(f32[16,128]{1,0:T(8,128)S(1)} %get-tuple-element.55), channel_id=1, source_target_pairs={{0,8},{8,0},{16,24},{24,16},{32,40},{40,32},{48,56},{56,48},{64,72... | collective-permute-start | bytes 24584 | tf_op jit(solution)/shard_map/ppermute | solution.py:512
  50.5 7.4 %collective-permute-start.3 = (f32[80,128]{1,0:T(8,128)S(1)}, f32[80,128]{1,0:T(8,128)S(1)}, u32[]{:S(2)}, u32[]{:S(2)}) collective-permute-start(f32[80,128]{1,0:T(8,128)S(1)} %pad_maximum_fusion.1), channel_id=1, source_target_pairs={{8,16},{24,32},{40,48},{56,64},{72,80},{88,96},{104,112},{120,128}... | collective-permute-start | bytes 122888 | tf_op jit(solution)/shard_map/ppermute | solution.py:515
  61.1 11.4 %all-to-all-start.2 = ((f32[16,8,128]{2,1,0:T(8,128)}), f32[16,8,128]{2,1,0:T(8,128)S(1)}, u32[]{:S(2)}, u32[]{:S(2)}) async-start(f32[16,8,128]{2,1,0:T(8,128)} %bitcast.12), calls=%async_computation.2 | async-start | bytes 131072 | tf_op jit(solution)/shard_map/all_to_all | solution.py:509
  64.6 3.1 %collective-permute-start.4 = (f32[16,128]{1,0:T(8,128)S(1)}, f32[16,128]{1,0:T(8,128)S(1)}, u32[]{:S(2)}, u32[]{:S(2)}) collective-permute-start(f32[16,128]{1,0:T(8,128)S(1)} %get-tuple-element.64), channel_id=1, source_target_pairs={{0,8},{8,0},{16,24},{24,16},{32,40},{40,32},{48,56},{56,48},{64,72... | collective-permute-start | bytes 24584 | tf_op jit(solution)/shard_map/ppermute | solution.py:512
  72.5 7.4 %collective-permute-start.5 = (f32[80,128]{1,0:T(8,128)S(1)}, f32[80,128]{1,0:T(8,128)S(1)}, u32[]{:S(2)}, u32[]{:S(2)}) collective-permute-start(f32[80,128]{1,0:T(8,128)S(1)} %pad_maximum_fusion.2), channel_id=1, source_target_pairs={{8,16},{24,32},{40,48},{56,64},{72,80},{88,96},{104,112},{120,128}... | collective-permute-start | bytes 122888 | tf_op jit(solution)/shard_map/ppermute | solution.py:515
  83.2 11.4 %all-to-all-start.3 = ((f32[16,8,128]{2,1,0:T(8,128)}), f32[16,8,128]{2,1,0:T(8,128)S(1)}, u32[]{:S(2)}, u32[]{:S(2)}) async-start(f32[16,8,128]{2,1,0:T(8,128)} %bitcast.15), calls=%async_computation.3 | async-start | bytes 131072 | tf_op jit(solution)/shard_map/all_to_all | solution.py:509
  86.7 3.1 %collective-permute-start.6 = (f32[16,128]{1,0:T(8,128)S(1)}, f32[16,128]{1,0:T(8,128)S(1)}, u32[]{:S(2)}, u32[]{:S(2)}) collective-permute-start(f32[16,128]{1,0:T(8,128)S(1)} %get-tuple-element.71), channel_id=1, source_target_pairs={{0,8},{8,0},{16,24},{24,16},{32,40},{40,32},{48,56},{56,48},{64,72... | collective-permute-start | bytes 24584 | tf_op jit(solution)/shard_map/ppermute | solution.py:512
  94.6 7.4 %collective-permute-start.7 = (f32[80,128]{1,0:T(8,128)S(1)}, f32[80,128]{1,0:T(8,128)S(1)}, u32[]{:S(2)}, u32[]{:S(2)}) collective-permute-start(f32[80,128]{1,0:T(8,128)S(1)} %pad_maximum_fusion.3), channel_id=1, source_target_pairs={{8,16},{24,32},{40,48},{56,64},{72,80},{88,96},{104,112},{120,128}... | collective-permute-start | bytes 122888 | tf_op jit(solution)/shard_map/ppermute | solution.py:515
  103.5 11.3 %all-to-all-start.4 = ((f32[8,8,128]{2,1,0:T(8,128)}), f32[8,8,128]{2,1,0:T(8,128)S(1)}, u32[]{:S(2)}, u32[]{:S(2)}) async-start(f32[8,8,128]{2,1,0:T(8,128)} %shard_map.118), calls=%async_computation.4 | async-start | bytes 65536 | tf_op jit(solution)/shard_map/all_to_all | solution.py:556

commit v3 on v2

--- a/solution.py
+++ b/solution.py
@@ -144,17 +144,17 @@
 
 def depth_at_slots(h_ref, index, cell):
     major, minor = cell_parts(cell)
-    index_rows = [minor[8 * v : 8 * v + 8] for v in range(3)]
-    key_rows = [major[8 * v : 8 * v + 8] for v in range(3)]
-    found = [jnp.zeros((8, LANES), jnp.float32) for _ in range(3)]
-    for quad in range(QUADS):
-        for row in range(ROWS):
-            values = h_ref[index + (slice(row, row + 1), slice(quad * LANES, (quad + 1) * LANES))]
-            values = jnp.broadcast_to(values, (8, LANES))
-            for v in range(3):
-                found[v] = jnp.where(
-                    key_rows[v] == quad * ROWS + row, lane_gather(values, index_rows[v]), found[v]
-                )
+    found = []
+    for v in range(3):
+        key = major[8 * v : 8 * v + 8]
+        lane = minor[8 * v : 8 * v + 8]
+        depth = jnp.zeros((8, LANES), jnp.float32)
+        for quad in range(QUADS):
+            for row in range(ROWS):
+                values = h_ref[index + (slice(row, row + 1), slice(quad * LANES, (quad + 1) * LANES))]
+                values = jnp.broadcast_to(values, (8, LANES))
+                depth = jnp.where(key == quad * ROWS + row, lane_gather(values, lane), depth)
+        found.append(depth)
     return jnp.concatenate(found, axis=0)
 
 
@@ -239,8 +239,24 @@
     return current - rate * (current - behind) + NU * mixing - (DT * RATIO) * lateral
 
 
+def owned_terms(celerity, base_inflow, upstream, y):
+    square = iota((FIELDS, FIELDS), 0) == iota((FIELDS, FIELDS), 1)
+
+    def by_field(ref):
+        row = jnp.broadcast_to(own_row(ref[...], y), (FIELDS, FIELDS))
+        return jnp.sum(jnp.where(square, row, 0.0), axis=1, keepdims=True)
+
+    feeders = own_row(upstream[...].astype(jnp.float32), y)
+    ids = ((lax.axis_index("gx") - 1) * BASINS + iota((BASINS, feeders.shape[1]), 0)).astype(jnp.float32)
+    hits = jnp.where(jnp.broadcast_to(feeders, ids.shape) == ids, 1.0, 0.0)
+    weight = jnp.sum(hits, axis=1, keepdims=True)
+    return jnp.concatenate(
+        [jnp.broadcast_to(column, (8, LANES)) for column in (by_field(celerity), by_field(base_inflow), weight)],
+        axis=0,
+    )
+
+
 def first_kernel(
-    scal,
     depth,
     discharge,
     cell_in,
@@ -255,6 +271,7 @@
     coeff_ref,
     slots_ref,
 ):
+    scal = place()
     even = scal[0] == 0
     mine, other, y = scal[0], 1 - scal[0], scal[1]
     send_ref[...] = jnp.zeros_like(send_ref)
@@ -289,6 +306,13 @@
 OVER = BASINS * BLOCK
 
 
+def place():
+    gx = lax.axis_index("gx")
+    y = lax.axis_index("gy")
+    last = lax.axis_size("gx") - 1
+    return gx & 1, y, (gx == 0).astype(jnp.int32), (gx == last).astype(jnp.int32)
+
+
 def gathered(got, over, scal, row, across_row):
     mine, other = scal[0], 1 - scal[0]
     return jnp.concatenate(
@@ -313,7 +337,8 @@
     return flood_update(cells, top, low, left, right, rough, source)
 
 
-def levels_kernel(scal, levels, owner_levels, owner_site, owner_coeff, got, over, own, all_levels):
+def levels_kernel(levels, owner_levels, owner_site, owner_coeff, got, over, own, all_levels):
+    scal = place()
     even = scal[0] == 0
     outlets = jnp.where(even, over[pl.ds(2, 8, stride=BLOCK), :], got[1 - scal[0], :, 2, :])
     new = advance_levels(
@@ -330,7 +355,8 @@
         all_levels[b] = new
 
 
-def cells_kernel(scal, state, got, near, over, rough, cell_ref, coeff_ref, slots_ref, state_out):
+def cells_kernel(state, got, near, over, rough, cell_ref, coeff_ref, slots_ref, state_out):
+    scal = place()
     new = advance_cells(
         scal,
         [state[0], state[1], state[2]],
@@ -356,15 +382,17 @@
         del refs[:n]
         return taken
 
-    (scal,) = take(1)
+    scal = place()
     if first:
-        depth, discharge, reach, site_ref = take(4)
+        depth, discharge, reach, site_ref, celerity, base_inflow, upstream = take(7)
     else:
         state, levels, owner_levels, owner_site, owner_coeff = take(5)
-    got, near, over, rough, own, cell_ref, coeff_ref, slots_ref = take(8)
+    if not first:
+        own = take(1)[0][...]
+    got, near, over, rough, cell_ref, coeff_ref, slots_ref = take(7)
     state_out, levels_out, owner_levels_out, slots_out, send_ref, beside_ref, across_ref = take(7)
     if first:
-        owner_site_out, owner_coeff_out = take(2)
+        owner_site_out, owner_coeff_out, own_out = take(3)
     even = scal[0] == 0
     mine, other, y = scal[0], 1 - scal[0], scal[1]
     cell = cell_ref[...]
@@ -397,6 +425,8 @@
         )
         owner_site_out[...] = site_owner
         owner_coeff_out[...] = coeff_owner
+        own = owned_terms(celerity, base_inflow, upstream, y)
+        own_out[...] = own
     else:
         cells = [state[0], state[1], state[2]]
         current = levels[...]
@@ -407,7 +437,7 @@
         outlets = jnp.where(even, over[pl.ds(2, 8, stride=BLOCK), :], got[other, :, 2, :])
 
     levels_next = advance_levels(
-        scal, current, outlets, own[...], site_owner, coeff_owner, segment_owner, slots_owner
+        scal, current, outlets, own, site_owner, coeff_owner, segment_owner, slots_owner
     )
     new = advance_cells(
         scal,
@@ -446,8 +476,7 @@
 
 
 def call(kernel, outs, args, limit=16 << 20):
-    specs = [pl.BlockSpec(memory_space=pltpu.SMEM)]
-    specs += [pl.BlockSpec(memory_space=pltpu.VMEM) for _ in args[1:]]
+    specs = [pl.BlockSpec(memory_space=pltpu.VMEM) for _ in args]
     return pl.pallas_call(
         kernel,
         out_shape=outs,
@@ -481,40 +510,21 @@
     count_x = lax.axis_size("gx")
     count_y = lax.axis_size("gy")
     gx = lax.axis_index("gx")
-    gy = lax.axis_index("gy")
-    core = gx % 2
+    core = gx & 1
     pairs = [list(range(c * 2 * count_y, (c + 1) * 2 * count_y)) for c in range(count_x // 2)]
     border = [(i, i + 1) for i in range(1, count_x - 1, 2)]
     border = border + [(b, a) for a, b in border]
     chip = [(i, i ^ 1) for i in range(count_x)]
-    scal = jnp.stack(
-        [core, gy, (gx == 0).astype(jnp.int32), (gx == count_x - 1).astype(jnp.int32)]
-    ).astype(jnp.int32)
-
-    def mine_of(array):
-        return lax.dynamic_slice_in_dim(array, gy, 1, axis=0)
-
-    ids = (gx - 1) * BASINS + jnp.arange(BASINS, dtype=jnp.int32)
-    weight = jnp.sum((mine_of(upstream) == ids[:, None]).astype(jnp.float32), axis=1, keepdims=True)
-    own = jnp.concatenate(
-        [
-            jnp.broadcast_to(mine_of(celerity).reshape(FIELDS, 1), (FIELDS, LANES)),
-            jnp.broadcast_to(mine_of(base_inflow).reshape(FIELDS, 1), (FIELDS, LANES)),
-            jnp.broadcast_to(weight, (BASINS, LANES)),
-        ],
-        axis=0,
-    )
-
     def exchange(send, beside, across):
         got = lax.all_to_all(
             send.reshape(2 * BASINS, BLOCK, LANES), ("gx", "gy"), 0, 0, axis_index_groups=pairs
         )
+        part = lax.dynamic_slice(got, (core * BASINS, 0, 0), (BASINS, BLOCK, LANES))
+        packed = jnp.concatenate([part.reshape(BASINS * BLOCK, LANES), across], axis=0)
+        packed, beside = lax.optimization_barrier((packed, beside))
+        over = lax.ppermute(packed, "gx", border)
         near = lax.ppermute(beside, "gx", chip)
-        got, near = lax.optimization_barrier((got, near))
-        part = lax.dynamic_slice(got, (core * BASINS, 0, 0), (BASINS, BLOCK, LANES))
-        over = lax.ppermute(
-            jnp.concatenate([part.reshape(BASINS * BLOCK, LANES), across], axis=0), "gx", border
-        )
+        near, over = lax.optimization_barrier((near, over))
         return got.reshape(2, BASINS, BLOCK, LANES), near, over
 
     table = (SLOT_ROWS, LANES)
@@ -522,7 +532,7 @@
     send, beside, across, cell, site, coeff, slots = call(
         first_kernel,
         [block, f32(WHOLE, LANES), f32(WHOLE, LANES), i32(*table), i32(*table), f32(*table), f32(*table)],
-        [scal, depth, discharge, bank_cell, bank_site, bank_coeff, reach_state],
+        [depth, discharge, bank_cell, bank_site, bank_coeff, reach_state],
         limit=60 << 20,
     )
     got, near, over = exchange(send, beside, across)
@@ -538,26 +548,26 @@
             f32(EDGE, LANES),
         ]
         if first:
-            outs += [i32(*table), f32(*table)]
-            args = [scal, depth, discharge, reach_state, site]
+            outs += [i32(*table), f32(*table), f32(*table)]
+            args = [depth, discharge, reach_state, site, celerity, base_inflow, upstream]
         else:
-            args = [scal, state, levels, owner_levels, owner_site, owner_coeff]
-        args += [got, near, over, roughness, own, cell, coeff, slots]
+            args = [state, levels, owner_levels, owner_site, owner_coeff, own]
+        args += [got, near, over, roughness, cell, coeff, slots]
         result = call(functools.partial(step_kernel, first), outs, args)
         state, levels, owner_levels, slots, send, beside, across = result[:7]
         if first:
-            owner_site, owner_coeff = result[7:9]
+            owner_site, owner_coeff, own = result[7:10]
         got, near, over = exchange(send, beside, across)
     copies = call(
         levels_kernel,
         [f32(BASINS, FIELDS, LANES)],
-        [scal, levels, owner_levels, owner_site, owner_coeff, got, over, own],
+        [levels, owner_levels, owner_site, owner_coeff, got, over, own],
     )[0]
     final = lax.all_to_all(copies, "gy", 0, 0)
     state = call(
         cells_kernel,
         [f32(3, ROWS, COLS)],
-        [scal, state, got, near, over, roughness, cell, coeff, slots],
+        [state, got, near, over, roughness, cell, coeff, slots],
     )[0]
     return state, final.reshape(BASINS, FIELDS * LANES)
 

time: 116 us -> 109 us (0.940)
  blocking collectives: 0 us -> 31.6 us
  waiting for transfers between devices: 41.3 us -> 22.8 us
  starting transfers between devices: 54.7 us -> 41.8 us
  Pallas kernels: 16 us -> 9.58 us
    all_to_all x0 -> x3, blocking collectives: none -> 31.6 us  [exchange(): lax.all_to_all(send.reshape(2 * BASINS, BLOCK, LANES), ('gx', 'gy'), 0, 0...]
    all_to_all x4 -> x1, waiting for transfers between devices: 19 us -> 7.94 us  [exchange(): lax.all_to_all(send.reshape(2 * BASINS, BLOCK, LANES), ('gx', 'gy'), 0, 0...]
    all_to_all x4 -> x1, starting transfers between devices: 17.9 us -> 7.35 us  [exchange(): lax.all_to_all(send.reshape(2 * BASINS, BLOCK, LANES), ('gx', 'gy'), 0, 0...]
    ppermute x4, waiting for transfers between devices: 14 us -> 3.83 us  [exchange(): over = lax.ppermute(packed, 'gx', border)]
    pallas_call x6, Pallas kernels: 16 us -> 9.58 us  [call(): pl.pallas_call(kernel, out_shape=outs, in_specs=specs, out_specs=[pl.Bloc...]
    ppermute x4, waiting for transfers between devices: 2.5 us -> 4.72 us  [exchange(): near = lax.ppermute(beside, 'gx', chip)]
    ppermute x4, starting transfers between devices: 9.01 us -> 7.68 us  [exchange(): near = lax.ppermute(beside, 'gx', chip)]
  transfers between devices with their start and end apart: 13 -> 10, of which waited for: 12 -> 9; matrix products, arithmetic and copies ran while one was open for 1% -> 0% of each run, Pallas kernels for 2% -> 2%
where the time goes in v3:
time: 109 us; the launch traced here: 108 us
  starting transfers between devices  41.8 us (38%)
  blocking collectives  31.6 us (29%)
  waiting for transfers between devices  22.8 us (21%)
  Pallas kernels  9.58 us (9%)
    all_to_all x3, blocking collectives, exchange(): lax.all_to_all(send.reshape(2 * BASINS, BLOCK, LANES), ('gx', 'gy'), 0, 0...  31.6 us
    ppermute x4, starting transfers between devices, exchange(): over = lax.ppermute(packed, 'gx', border)  23.4 us
    pallas_call x6, Pallas kernels, call(): pl.pallas_call(kernel, out_shape=outs, in_specs=specs, out_specs=[pl.Bloc...  9.58 us
    all_to_all x1, waiting for transfers between devices, exchange(): lax.all_to_all(send.reshape(2 * BASINS, BLOCK, LANES), ('gx', 'gy'), 0, 0...  7.94 us
    ppermute x4, starting transfers between devices, exchange(): near = lax.ppermute(beside, 'gx', chip)  7.68 us
    all_to_all x1, starting transfers between devices, exchange(): lax.all_to_all(send.reshape(2 * BASINS, BLOCK, LANES), ('gx', 'gy'), 0, 0...  7.35 us
    all_to_all x1, waiting for transfers between devices, per_device(): final = lax.all_to_all(copies, 'gy', 0, 0)  6.32 us
    ppermute x4, waiting for transfers between devices, exchange(): near = lax.ppermute(beside, 'gx', chip)  4.72 us
  transfers between devices with their start and end apart: 10, of which 9 were waited for; matrix products, arithmetic and copies ran while one was open for 0% of the time, Pallas kernels for 2%

profile of v3, /device:TPU:6, one launch (start us, length us, event | category | flops | bytes accessed | tf_op | source)
XLA Modules:
  0.0 108.3 jit_solution(12800746497140378391)
XLA Ops:
  0.6 2.1 %shard_map.113 = (f32[2,8,8,128]{3,2,1,0:T(8,128)}, f32[80,128]{1,0:T(8,128)}, f32[80,128]{1,0:T(8,128)}, s32[24,128]{1,0:T(8,128)}, s32[24,128]{1,0:T(8,128)}, /*index=5*/f32[24,128]{1,0:T(8,128)}, f32[24,128]{1,0:T(8,128)}) custom-call(f32[32,512]{1,0:T(8,128)} %refs_0_.1, f32[2,32,512]{2,1,0:T(8,128)} %refs_1_.1, s32[24,128]{1,0:T(8,128)} %cell_in.1, ...), custom_call_target="tpu_custom_call" | custom-call | tf_op jit(solution)/shard_map/pallas_call | solution.py:480
  2.7 0.0 copy-start.5
  2.8 7.3 %all-to-all-start = ((f32[16,8,128]{2,1,0:T(8,128)}), f32[16,8,128]{2,1,0:T(8,128)S(1)}, u32[]{:S(2)}, u32[]{:S(2)}) async-start(f32[16,8,128]{2,1,0:T(8,128)} %bitcast.29), calls=%async_computation | async-start | bytes 131072 | tf_op jit(solution)/shard_map/all_to_all | solution.py:519
  10.1 7.9 %all-to-all-done = f32[16,8,128]{2,1,0:T(8,128)S(1)} async-done(((f32[16,8,128]{2,1,0:T(8,128)}), f32[16,8,128]{2,1,0:T(8,128)S(1)}, u32[]{:S(2)}, u32[]{:S(2)}) %all-to-all-start) | async-done | bytes 65568 | tf_op jit(solution)/shard_map/all_to_all | solution.py:519
  18.1 0.8 pad_maximum_fusion
  19.0 14.2 %collective-permute-start.1 = (f32[144,128]{1,0:T(8,128)S(1)}, f32[144,128]{1,0:T(8,128)S(1)}, u32[]{:S(2)}, u32[]{:S(2)}) collective-permute-start(f32[144,128]{1,0:T(8,128)S(1)} %pad_maximum_fusion), channel_id=1, source_target_pairs={{8,16},{24,32},{40,48},{56,64},{72,80},{88,96},{104,112},{120,128}... | collective-permute-start | bytes 221192 | tf_op jit(solution)/shard_map/ppermute | solution.py:525
  33.2 1.9 %collective-permute-start = (f32[80,128]{1,0:T(8,128)}, f32[80,128]{1,0:T(8,128)S(1)}, u32[]{:S(2)}, u32[]{:S(2)}) collective-permute-start(f32[80,128]{1,0:T(8,128)} %get-tuple-element.53), channel_id=1, source_target_pairs={{0,8},{8,0},{16,24},{24,16},{32,40},{40,32},{48,56},{56,48},{64,72... | collective-permute-start | bytes 122888 | tf_op jit(solution)/shard_map/ppermute | solution.py:526
  35.1 0.1 copy.12.refs_6_
  35.2 1.3 %collective-permute-done.refs_8_ = f32[80,128]{1,0:T(8,128)S(1)} collective-permute-done((f32[80,128]{1,0:T(8,128)}, f32[80,128]{1,0:T(8,128)S(1)}, u32[]{:S(2)}, u32[]{:S(2)}) %collective-permute-start) | collective-permute-done | bytes 40992 | tf_op jit(solution)/shard_map/ppermute | solution.py:526
  36.6 1.7 %shard_map.114 = (f32[3,32,512]{2,1,0:T(8,128)S(1)}, f32[8,128]{1,0:T(8,128)S(1)}, f32[24,128]{1,0:T(8,128)S(1)}, f32[24,128]{1,0:T(8,128)S(1)}, f32[2,8,8,128]{...) custom-call(f32[32,512]{1,0:T(8,128)S(1)} %copy-done.2, ...), custom_call_target="tpu_custom_call" | custom-call | tf_op jit(solution)/shard_map/pallas_call | solution.py:480
  38.3 10.6 %all_to_all.25 = f32[16,8,128]{2,1,0:T(8,128)S(1)} all-to-all(f32[16,8,128]{2,1,0:T(8,128)S(1)} %bitcast.25), channel_id=1, replica_groups={{0,1,2,3,4,5,6,7,8,9,10,11,12,13,14,15},{16,17,18,19,20,21,22,23,24,25,..., dimensions={0} | all-to-all | bytes 131072 | tf_op jit(solution)/shard_map/all_to_all | solution.py:519
  48.9 3.7 %collective-permute-start.3 = (f32[80,128]{1,0:T(8,128)S(1)}, f32[80,128]{1,0:T(8,128)S(1)}, u32[]{:S(2)}, u32[]{:S(2)}) collective-permute-start(f32[80,128]{1,0:T(8,128)S(1)} %pad_maximum_fusion.1), channel_id=1, source_target_pairs={{8,16},{24,32},{40,48},{56,64},{72,80},{88,96},{104,112},{120,128}... | collective-permute-start | bytes 122888 | tf_op jit(solution)/shard_map/ppermute | solution.py:525
  52.5 1.9 %collective-permute-start.2 = (f32[16,128]{1,0:T(8,128)S(1)}, f32[16,128]{1,0:T(8,128)S(1)}, u32[]{:S(2)}, u32[]{:S(2)}) collective-permute-start(f32[16,128]{1,0:T(8,128)S(1)} %get-tuple-element.69), channel_id=1, source_target_pairs={{0,8},{8,0},{16,24},{24,16},{32,40},{40,32},{48,56},{56,48},{64,72... | collective-permute-start | bytes 24584 | tf_op jit(solution)/shard_map/ppermute | solution.py:526
  54.5 1.1 %collective-permute-done.2.refs_7_ = f32[16,128]{1,0:T(8,128)S(1)} collective-permute-done((f32[16,128]{1,0:T(8,128)S(1)}, f32[16,128]{1,0:T(8,128)S(1)}, u32[]{:S(2)}, u32[]{:S(2)}) %collective-permute-start.2) | collective-permute-done | bytes 8224 | tf_op jit(solution)/shard_map/ppermute | solution.py:526
  55.6 0.7 collective-permute-done.3.refs_8_
  56.3 1.6 %shard_map.115 = (f32[3,32,512]{2,1,0:T(8,128)S(1)}, f32[8,128]{1,0:T(8,128)S(1)}, f32[24,128]{1,0:T(8,128)S(1)}, f32[24,128]{1,0:T(8,128)S(1)}, f32[2,8,8,128]{...) custom-call(f32[3,32,512]{2,1,0:T(8,128)S(1)} %get-tuple-element.60.refs_0_, ...), custom_call_target="tpu_custom_call" | custom-call | tf_op jit(solution)/shard_map/pallas_call | solution.py:480
  57.9 10.5 %all_to_all.26 = f32[16,8,128]{2,1,0:T(8,128)S(1)} all-to-all(f32[16,8,128]{2,1,0:T(8,128)S(1)} %bitcast.26), channel_id=1, replica_groups={{0,1,2,3,4,5,6,7,8,9,10,11,12,13,14,15},{16,17,18,19,20,21,22,23,24,25,..., dimensions={0} | all-to-all | bytes 131072 | tf_op jit(solution)/shard_map/all_to_all | solution.py:519
  68.4 3.0 %collective-permute-start.5 = (f32[80,128]{1,0:T(8,128)S(1)}, f32[80,128]{1,0:T(8,128)S(1)}, u32[]{:S(2)}, u32[]{:S(2)}) collective-permute-start(f32[80,128]{1,0:T(8,128)S(1)} %pad_maximum_fusion.2), channel_id=1, source_target_pairs={{8,16},{24,32},{40,48},{56,64},{72,80},{88,96},{104,112},{120,128}... | collective-permute-start | bytes 122888 | tf_op jit(solution)/shard_map/ppermute | solution.py:525
  71.4 1.9 %collective-permute-start.4 = (f32[16,128]{1,0:T(8,128)S(1)}, f32[16,128]{1,0:T(8,128)S(1)}, u32[]{:S(2)}, u32[]{:S(2)}) collective-permute-start(f32[16,128]{1,0:T(8,128)S(1)} %get-tuple-element.80), channel_id=1, source_target_pairs={{0,8},{8,0},{16,24},{24,16},{32,40},{40,32},{48,56},{56,48},{64,72... | collective-permute-start | bytes 24584 | tf_op jit(solution)/shard_map/ppermute | solution.py:526
  73.3 1.1 %collective-permute-done.4.refs_7_ = f32[16,128]{1,0:T(8,128)S(1)} collective-permute-done((f32[16,128]{1,0:T(8,128)S(1)}, f32[16,128]{1,0:T(8,128)S(1)}, u32[]{:S(2)}, u32[]{:S(2)}) %collective-permute-start.4) | collective-permute-done | bytes 8224 | tf_op jit(solution)/shard_map/ppermute | solution.py:526
  74.5 1.4 %collective-permute-done.5.refs_8_ = f32[80,128]{1,0:T(8,128)S(1)} collective-permute-done((f32[80,128]{1,0:T(8,128)S(1)}, f32[80,128]{1,0:T(8,128)S(1)}, u32[]{:S(2)}, u32[]{:S(2)}) %collective-permute-start.5) | collective-permute-done | bytes 40992 | tf_op jit(solution)/shard_map/ppermute | solution.py:525
  75.9 1.6 %shard_map.116 = (f32[3,32,512]{2,1,0:T(8,128)S(1)}, f32[8,128]{1,0:T(8,128)S(1)}, f32[24,128]{1,0:T(8,128)S(1)}, f32[24,128]{1,0:T(8,128)S(1)}, f32[2,8,8,128]{...) custom-call(f32[3,32,512]{2,1,0:T(8,128)S(1)} %get-tuple-element.74.refs_0_, ...), custom_call_target="tpu_custom_call" | custom-call | tf_op jit(solution)/shard_map/pallas_call | solution.py:480
  77.5 10.5 %all_to_all.27 = f32[16,8,128]{2,1,0:T(8,128)S(1)} all-to-all(f32[16,8,128]{2,1,0:T(8,128)S(1)} %bitcast.27), channel_id=1, replica_groups={{0,1,2,3,4,5,6,7,8,9,10,11,12,13,14,15},{16,17,18,19,20,21,22,23,24,25,..., dimensions={0} | all-to-all | bytes 131072 | tf_op jit(solution)/shard_map/all_to_all | solution.py:519
  88.0 2.6 %collective-permute-start.7 = (f32[80,128]{1,0:T(8,128)S(1)}, f32[80,128]{1,0:T(8,128)S(1)}, u32[]{:S(2)}, u32[]{:S(2)}) collective-permute-start(f32[80,128]{1,0:T(8,128)S(1)} %pad_maximum_fusion.3), channel_id=1, source_target_pairs={{8,16},{24,32},{40,48},{56,64},{72,80},{88,96},{104,112},{120,128}... | collective-permute-start | bytes 122888 | tf_op jit(solution)/shard_map/ppermute | solution.py:525
  90.6 1.9 %collective-permute-start.6 = (f32[16,128]{1,0:T(8,128)S(1)}, f32[16,128]{1,0:T(8,128)S(1)}, u32[]{:S(2)}, u32[]{:S(2)}) collective-permute-start(f32[16,128]{1,0:T(8,128)S(1)} %get-tuple-element.89), channel_id=1, source_target_pairs={{0,8},{8,0},{16,24},{24,16},{32,40},{40,32},{48,56},{56,48},{64,72... | collective-permute-start | bytes 24584 | tf_op jit(solution)/shard_map/ppermute | solution.py:526
  92.5 1.1 %collective-permute-done.6.near = f32[16,128]{1,0:T(8,128)S(1)} collective-permute-done((f32[16,128]{1,0:T(8,128)S(1)}, f32[16,128]{1,0:T(8,128)S(1)}, u32[]{:S(2)}, u32[]{:S(2)}) %collective-permute-start.6) | collective-permute-done | bytes 8224 | tf_op jit(solution)/shard_map/ppermute | solution.py:526
  93.7 1.7 %collective-permute-done.7.over = f32[80,128]{1,0:T(8,128)S(1)} collective-permute-done((f32[80,128]{1,0:T(8,128)S(1)}, f32[80,128]{1,0:T(8,128)S(1)}, u32[]{:S(2)}, u32[]{:S(2)}) %collective-permute-start.7) | collective-permute-done | bytes 40992 | tf_op jit(solution)/shard_map/ppermute | solution.py:525
  95.4 0.9 shard_map.118
  96.4 3.3 %all-to-all-start.4 = ((f32[8,8,128]{2,1,0:T(8,128)}), f32[8,8,128]{2,1,0:T(8,128)S(1)}, u32[]{:S(2)}, u32[]{:S(2)}) async-start(f32[8,8,128]{2,1,0:T(8,128)} %shard_map.118), calls=%async_computation.4 | async-start | bytes 65536 | tf_op jit(solution)/shard_map/all_to_all | solution.py:566
  99.7 1.6 %shard_map.117 = f32[3,32,512]{2,1,0:T(8,128)} custom-call(f32[3,32,512]{2,1,0:T(8,128)S(1)} %get-tuple-element.85.state, f32[2,8,8,128]{3,2,1,0:T(8,128)S(1)} %bitcast.21, f32[16,128]{1,0:T(8,128)S(1)} %collective-permute-done.6.near, f32[80,128]{1,0:T(8,128)S(1)} %collective-permute-done.7.over, f32[32,512]{1,0:T(8,128)S(1)} %copy-done, ...), custom_call_target="tpu_custom_call" | custom-call | tf_op jit(solution)/shard_map/pallas_call | solution.py:480
  101.3 6.3 %all-to-all-done.4 = f32[8,8,128]{2,1,0:T(8,128)S(1)} async-done(((f32[8,8,128]{2,1,0:T(8,128)}), f32[8,8,128]{2,1,0:T(8,128)S(1)}, u32[]{:S(2)}, u32[]{:S(2)}) %all-to-all-start.4) | async-done | bytes 32800 | tf_op jit(solution)/shard_map/all_to_all | solution.py:566
  107.6 0.6 copy.15
  (29 shorter events, 0.1 us)
Async XLA Ops:
  2.7 33.8 %copy-start.2 = (f32[32,512]{1,0:T(8,128)S(1)}, f32[32,512]{1,0:T(8,128)}, u32[]{:S(2)}) copy-start(f32[32,512]{1,0:T(8,128)} %refs_0_.1) | copy-start | bytes 196612
  2.7 33.8 %copy-start.5 = (f32[8,1024]{1,0:T(8,128)S(1)}, f32[8,1024]{1,0:T(8,128)}, u32[]{:S(2)}) copy-start(f32[8,1024]{1,0:T(8,128)} %refs_2_.1) | copy-start | bytes 98308
  2.7 33.8 %copy-start.8 = (f32[8,8]{1,0:T(8,128)S(1)}, f32[8,8]{1,0:T(8,128)}, u32[]{:S(2)}) copy-start(f32[8,8]{1,0:T(8,128)} %refs_4_.1) | copy-start | bytes 772
  2.8 33.8 %copy-start.9 = (f32[8,8]{1,0:T(8,128)S(1)}, f32[8,8]{1,0:T(8,128)}, u32[]{:S(2)}) copy-start(f32[8,8]{1,0:T(8,128)} %refs_5_.1) | copy-start | bytes 772
  2.8 15.3 %all-to-all-start = ((f32[16,8,128]{2,1,0:T(8,128)}), f32[16,8,128]{2,1,0:T(8,128)S(1)}, u32[]{:S(2)}, u32[]{:S(2)}) async-start(f32[16,8,128]{2,1,0:T(8,128)} %bitcast.29), calls=%async_computation | async-start | bytes 131072 | tf_op jit(solution)/shard_map/all_to_all | solution.py:519
  10.1 26.4 %copy-start.1 = (f32[2,32,512]{2,1,0:T(8,128)S(1)}, f32[2,32,512]{2,1,0:T(8,128)}, u32[]{:S(2)}) copy-start(f32[2,32,512]{2,1,0:T(8,128)} %refs_1_.1) | copy-start | bytes 393220
  18.1 17.0 %copy-start.10 = (s32[8,2]{0,1:T(2,128)S(1)}, s32[8,2]{0,1:T(2,128)}, u32[]{:S(2)}) copy-start(s32[8,2]{0,1:T(2,128)} %param.16) | copy-start | bytes 196
  18.1 18.4 %copy-start = (f32[32,512]{1,0:T(8,128)S(1)}, f32[32,512]{1,0:T(8,128)}, u32[]{:S(2)}) copy-start(f32[32,512]{1,0:T(8,128)} %rough.1) | copy-start | bytes 196612
  18.1 18.4 %copy-start.4 = (f32[24,128]{1,0:T(8,128)S(1)}, f32[24,128]{1,0:T(8,128)}, u32[]{:S(2)}) copy-start(f32[24,128]{1,0:T(8,128)} %get-tuple-element.58.refs_12_.refs_11_.coeff_ref) | copy-start | bytes 36868
  18.1 18.4 %copy-start.6 = (s32[24,128]{1,0:T(8,128)S(1)}, s32[24,128]{1,0:T(8,128)}, u32[]{:S(2)}) copy-start(s32[24,128]{1,0:T(8,128)} %get-tuple-element.49.refs_3_) | copy-start | bytes 36868
  18.1 18.4 %copy-start.7 = (f32[24,128]{1,0:T(8,128)S(1)}, f32[24,128]{1,0:T(8,128)}, u32[]{:S(2)}) copy-start(f32[24,128]{1,0:T(8,128)} %get-tuple-element.59.refs_13_) | copy-start | bytes 36868
  19.0 17.6 %copy-start.3 = (s32[24,128]{1,0:T(8,128)S(1)}, s32[24,128]{1,0:T(8,128)}, u32[]{:S(2)}) copy-start(s32[24,128]{1,0:T(8,128)} %get-tuple-element.57.refs_11_.refs_10_.cell_ref) | copy-start | bytes 36868
  19.0 17.5 %collective-permute-start.1 = (f32[144,128]{1,0:T(8,128)S(1)}, f32[144,128]{1,0:T(8,128)S(1)}, u32[]{:S(2)}, u32[]{:S(2)}) collective-permute-start(f32[144,128]{1,0:T(8,128)S(1)} %pad_maximum_fusion), channel_id=1, source_target_pairs={{8,16},{24,32},{40,48},{56,64},{72,80},{88,96},{104,112},{120,128}... | collective-permute-start | bytes 221192 | tf_op jit(solution)/shard_map/ppermute | solution.py:525
  33.2 3.3 %collective-permute-start = (f32[80,128]{1,0:T(8,128)}, f32[80,128]{1,0:T(8,128)S(1)}, u32[]{:S(2)}, u32[]{:S(2)}) collective-permute-start(f32[80,128]{1,0:T(8,128)} %get-tuple-element.53), channel_id=1, source_target_pairs={{0,8},{8,0},{16,24},{24,16},{32,40},{40,32},{48,56},{56,48},{64,72... | collective-permute-start | bytes 122888 | tf_op jit(solution)/shard_map/ppermute | solution.py:526
  48.9 7.4 %collective-permute-start.3 = (f32[80,128]{1,0:T(8,128)S(1)}, f32[80,128]{1,0:T(8,128)S(1)}, u32[]{:S(2)}, u32[]{:S(2)}) collective-permute-start(f32[80,128]{1,0:T(8,128)S(1)} %pad_maximum_fusion.1), channel_id=1, source_target_pairs={{8,16},{24,32},{40,48},{56,64},{72,80},{88,96},{104,112},{120,128}... | collective-permute-start | bytes 122888 | tf_op jit(solution)/shard_map/ppermute | solution.py:525
  52.5 3.1 %collective-permute-start.2 = (f32[16,128]{1,0:T(8,128)S(1)}, f32[16,128]{1,0:T(8,128)S(1)}, u32[]{:S(2)}, u32[]{:S(2)}) collective-permute-start(f32[16,128]{1,0:T(8,128)S(1)} %get-tuple-element.69), channel_id=1, source_target_pairs={{0,8},{8,0},{16,24},{24,16},{32,40},{40,32},{48,56},{56,48},{64,72... | collective-permute-start | bytes 24584 | tf_op jit(solution)/shard_map/ppermute | solution.py:526
  68.4 7.4 %collective-permute-start.5 = (f32[80,128]{1,0:T(8,128)S(1)}, f32[80,128]{1,0:T(8,128)S(1)}, u32[]{:S(2)}, u32[]{:S(2)}) collective-permute-start(f32[80,128]{1,0:T(8,128)S(1)} %pad_maximum_fusion.2), channel_id=1, source_target_pairs={{8,16},{24,32},{40,48},{56,64},{72,80},{88,96},{104,112},{120,128}... | collective-permute-start | bytes 122888 | tf_op jit(solution)/shard_map/ppermute | solution.py:525
  71.4 3.1 %collective-permute-start.4 = (f32[16,128]{1,0:T(8,128)S(1)}, f32[16,128]{1,0:T(8,128)S(1)}, u32[]{:S(2)}, u32[]{:S(2)}) collective-permute-start(f32[16,128]{1,0:T(8,128)S(1)} %get-tuple-element.80), channel_id=1, source_target_pairs={{0,8},{8,0},{16,24},{24,16},{32,40},{40,32},{48,56},{56,48},{64,72... | collective-permute-start | bytes 24584 | tf_op jit(solution)/shard_map/ppermute | solution.py:526
  88.0 7.4 %collective-permute-start.7 = (f32[80,128]{1,0:T(8,128)S(1)}, f32[80,128]{1,0:T(8,128)S(1)}, u32[]{:S(2)}, u32[]{:S(2)}) collective-permute-start(f32[80,128]{1,0:T(8,128)S(1)} %pad_maximum_fusion.3), channel_id=1, source_target_pairs={{8,16},{24,32},{40,48},{56,64},{72,80},{88,96},{104,112},{120,128}... | collective-permute-start | bytes 122888 | tf_op jit(solution)/shard_map/ppermute | solution.py:525
  90.6 3.1 %collective-permute-start.6 = (f32[16,128]{1,0:T(8,128)S(1)}, f32[16,128]{1,0:T(8,128)S(1)}, u32[]{:S(2)}, u32[]{:S(2)}) collective-permute-start(f32[16,128]{1,0:T(8,128)S(1)} %get-tuple-element.89), channel_id=1, source_target_pairs={{0,8},{8,0},{16,24},{24,16},{32,40},{40,32},{48,56},{56,48},{64,72... | collective-permute-start | bytes 24584 | tf_op jit(solution)/shard_map/ppermute | solution.py:526
  96.4 11.3 %all-to-all-start.4 = ((f32[8,8,128]{2,1,0:T(8,128)}), f32[8,8,128]{2,1,0:T(8,128)S(1)}, u32[]{:S(2)}, u32[]{:S(2)}) async-start(f32[8,8,128]{2,1,0:T(8,128)} %shard_map.118), calls=%async_computation.4 | async-start | bytes 65536 | tf_op jit(solution)/shard_map/all_to_all | solution.py:566

commit v4 on v3

--- a/solution.py
+++ b/solution.py
@@ -25,6 +25,10 @@
 BASINS = 8
 SLOT_ROWS = 3 * BASINS
 BLOCK = 8
+FIRST_ROWS = 24
+STEP_ROWS = 16
+EDGE_ROW = 3
+LEVEL_ROW = 15
 EDGE = 16
 WHOLE = EDGE + FIELDS * BASINS
 INTERPRET = False
@@ -171,7 +175,7 @@
     return jnp.concatenate(found, axis=0)
 
 
-def put_edges(send_ref, beside_ref, across_ref, cells, even, mine, y, col_row):
+def put_edges(send_ref, across_ref, cells, even, mine, y, col_row):
     lane_left = column_to_lane(cells[0][:, 0:1], 0)
     lane_right = column_to_lane(cells[0][:, COLS - 1 : COLS], 0)
     for k in (1, 2):
@@ -187,11 +191,11 @@
         for quad in range(QUADS):
             at = k * QUADS + quad
             lanes = slice(quad * LANES, (quad + 1) * LANES)
-            beside_ref[at : at + 1, :] = inner[:, lanes]
+            send_ref[1 - mine, y, EDGE_ROW + at : EDGE_ROW + at + 1, :] = inner[:, lanes]
             across_ref[at : at + 1, :] = outer[:, lanes]
 
 
-def get_edges(got_ref, near_ref, over_ref, cells, scal, mine, y, col_row):
+def get_edges(got_ref, over_ref, cells, scal, mine, y, col_row):
     even = scal[0] == 0
     is_first, is_last = scal[2] == 1, scal[3] == 1
     before = got_ref[mine, jnp.maximum(y - 1, 0), col_row : col_row + 1, :]
@@ -201,7 +205,7 @@
     for k in range(3):
         inner = jnp.concatenate(
             [
-                near_ref[k * QUADS + quad : k * QUADS + quad + 1, :]
+                got_ref[1 - mine, y, EDGE_ROW + k * QUADS + quad : EDGE_ROW + k * QUADS + quad + 1, :]
                 for quad in range(QUADS)
             ],
             axis=1,
@@ -264,7 +268,6 @@
     coeff_in,
     reach,
     send_ref,
-    beside_ref,
     across_ref,
     cell_ref,
     site_ref,
@@ -295,12 +298,15 @@
             send_ref[mine, b, at : at + 1, :] = value[b : b + 1]
             send_ref[other, b, at : at + 1, :] = value[8 + b : 9 + b]
             send_ref[mine, b, 3 + at : 4 + at, :] = value[16 + b : 17 + b]
-    for ref in (beside_ref, across_ref):
-        ref[0:EDGE] = jnp.zeros((EDGE, LANES), jnp.float32)
-        for f in range(FIELDS):
-            ref[EDGE + 8 * f : EDGE + 8 * f + 8] = reach[:, f * LANES : (f + 1) * LANES]
+    across_ref[0:EDGE] = jnp.zeros((EDGE, LANES), jnp.float32)
+    for f in range(FIELDS):
+        rows = reach[:, f * LANES : (f + 1) * LANES]
+        across_ref[EDGE + 8 * f : EDGE + 8 * f + 8] = rows
+        row = own_row(rows, y)
+        for b in range(BASINS):
+            send_ref[other, b, LEVEL_ROW + f : LEVEL_ROW + f + 1, :] = row
     cells = [depth[...], discharge[0], discharge[1]]
-    put_edges(send_ref, beside_ref, across_ref, cells, even, mine, y, 6)
+    put_edges(send_ref, across_ref, cells, even, mine, y, 6)
 
 
 OVER = BASINS * BLOCK
@@ -327,13 +333,13 @@
     return river_update(current, outlets, own, lateral)
 
 
-def advance_cells(scal, cells, got, near, over, rough, cell, coeff, segment, slots, col_row):
+def advance_cells(scal, cells, got, over, rough, cell, coeff, segment, slots, col_row):
     mine, y = scal[0], scal[1]
     major, minor = cell_parts(cell)
     rates = coeff * (segment - slots)
     blocks = spread(rates, major, minor, QUADS * ROWS)
     source = jnp.concatenate([blocks[q * ROWS : (q + 1) * ROWS] for q in range(QUADS)], axis=1)
-    top, low, left, right = get_edges(got, near, over, cells, scal, mine, y, col_row)
+    top, low, left, right = get_edges(got, over, cells, scal, mine, y, col_row)
     return flood_update(cells, top, low, left, right, rough, source)
 
 
@@ -355,13 +361,12 @@
         all_levels[b] = new
 
 
-def cells_kernel(state, got, near, over, rough, cell_ref, coeff_ref, slots_ref, state_out):
+def cells_kernel(state, got, over, rough, cell_ref, coeff_ref, slots_ref, state_out):
     scal = place()
     new = advance_cells(
         scal,
         [state[0], state[1], state[2]],
         got,
-        near,
         over,
         rough[...],
         cell_ref[...],
@@ -389,8 +394,8 @@
         state, levels, owner_levels, owner_site, owner_coeff = take(5)
     if not first:
         own = take(1)[0][...]
-    got, near, over, rough, cell_ref, coeff_ref, slots_ref = take(7)
-    state_out, levels_out, owner_levels_out, slots_out, send_ref, beside_ref, across_ref = take(7)
+    got, over, rough, cell_ref, coeff_ref, slots_ref = take(6)
+    state_out, levels_out, owner_levels_out, slots_out, send_ref, across_ref = take(6)
     if first:
         owner_site_out, owner_coeff_out, own_out = take(3)
     even = scal[0] == 0
@@ -408,7 +413,7 @@
             if v == 0:
                 return reach[:, f * LANES : (f + 1) * LANES]
             if v == 1:
-                return near[EDGE + 8 * f : EDGE + 8 * f + 8, :]
+                return got[other, :, LEVEL_ROW + f, :]
             return over[OVER + EDGE + 8 * f : OVER + EDGE + 8 * f + 8, :]
 
         segment = level_at_sites(tile_rows, site_ref[...])
@@ -443,7 +448,6 @@
         scal,
         cells,
         got,
-        near,
         over,
         rough[...],
         cell,
@@ -462,7 +466,6 @@
     slots = depth_at_slots(state_out, (0,), cell)
     slots_out[...] = slots
     send_ref[...] = jnp.zeros_like(send_ref)
-    beside_ref[...] = jnp.zeros_like(beside_ref)
     across_ref[...] = jnp.zeros_like(across_ref)
     outlet_row = column_to_lane(levels_next[:, LANES - 1 : LANES], 0)
     for b in range(BASINS):
@@ -472,7 +475,7 @@
             send_ref[mine, b, 3 + at : 4 + at, :] = value[16 + b : 17 + b]
         send_ref[mine, b, 2:3, :] = outlet_row
         send_ref[other, b, 2:3, :] = outlet_row
-    put_edges(send_ref, beside_ref, across_ref, new, even, mine, y, 5)
+    put_edges(send_ref, across_ref, new, even, mine, y, 5)
 
 
 def call(kernel, outs, args, limit=16 << 20):
@@ -514,28 +517,31 @@
     pairs = [list(range(c * 2 * count_y, (c + 1) * 2 * count_y)) for c in range(count_x // 2)]
     border = [(i, i + 1) for i in range(1, count_x - 1, 2)]
     border = border + [(b, a) for a, b in border]
-    chip = [(i, i ^ 1) for i in range(count_x)]
-    def exchange(send, beside, across):
+    def exchange(send, across):
+        rows = send.shape[2]
         got = lax.all_to_all(
-            send.reshape(2 * BASINS, BLOCK, LANES), ("gx", "gy"), 0, 0, axis_index_groups=pairs
+            send.reshape(2 * BASINS, rows, LANES), ("gx", "gy"), 0, 0, axis_index_groups=pairs
         )
         part = lax.dynamic_slice(got, (core * BASINS, 0, 0), (BASINS, BLOCK, LANES))
         packed = jnp.concatenate([part.reshape(BASINS * BLOCK, LANES), across], axis=0)
-        packed, beside = lax.optimization_barrier((packed, beside))
         over = lax.ppermute(packed, "gx", border)
-        near = lax.ppermute(beside, "gx", chip)
-        near, over = lax.optimization_barrier((near, over))
-        return got.reshape(2, BASINS, BLOCK, LANES), near, over
+        return got.reshape(2, BASINS, rows, LANES), over
 
     table = (SLOT_ROWS, LANES)
-    block = f32(2, BASINS, BLOCK, LANES)
-    send, beside, across, cell, site, coeff, slots = call(
+    send, across, cell, site, coeff, slots = call(
         first_kernel,
-        [block, f32(WHOLE, LANES), f32(WHOLE, LANES), i32(*table), i32(*table), f32(*table), f32(*table)],
+        [
+            f32(2, BASINS, FIRST_ROWS, LANES),
+            f32(WHOLE, LANES),
+            i32(*table),
+            i32(*table),
+            f32(*table),
+            f32(*table),
+        ],
         [depth, discharge, bank_cell, bank_site, bank_coeff, reach_state],
         limit=60 << 20,
     )
-    got, near, over = exchange(send, beside, across)
+    got, over = exchange(send, across)
     for step in range(STEPS - 1):
         first = step == 0
         outs = [
@@ -543,8 +549,7 @@
             f32(FIELDS, LANES),
             f32(*table),
             f32(*table),
-            block,
-            f32(EDGE, LANES),
+            f32(2, BASINS, STEP_ROWS, LANES),
             f32(EDGE, LANES),
         ]
         if first:
@@ -552,12 +557,12 @@
             args = [depth, discharge, reach_state, site, celerity, base_inflow, upstream]
         else:
             args = [state, levels, owner_levels, owner_site, owner_coeff, own]
-        args += [got, near, over, roughness, cell, coeff, slots]
+        args += [got, over, roughness, cell, coeff, slots]
         result = call(functools.partial(step_kernel, first), outs, args)
-        state, levels, owner_levels, slots, send, beside, across = result[:7]
+        state, levels, owner_levels, slots, send, across = result[:6]
         if first:
-            owner_site, owner_coeff, own = result[7:10]
-        got, near, over = exchange(send, beside, across)
+            owner_site, owner_coeff, own = result[6:9]
+        got, over = exchange(send, across)
     copies = call(
         levels_kernel,
         [f32(BASINS, FIELDS, LANES)],
@@ -567,7 +572,7 @@
     state = call(
         cells_kernel,
         [f32(3, ROWS, COLS)],
-        [state, got, near, over, roughness, cell, coeff, slots],
+        [state, got, over, roughness, cell, coeff, slots],
     )[0]
     return state, final.reshape(BASINS, FIELDS * LANES)
 

time: 109 us -> 112 us (1.028)
  starting transfers between devices: 41.8 us -> 36.9 us
  waiting for transfers between devices: 22.8 us -> 27.5 us
  blocking collectives: 31.6 us -> 35.8 us
    ppermute x4, waiting for transfers between devices: 3.83 us -> 12.1 us  [exchange(): over = lax.ppermute(packed, 'gx', border)]
    ppermute x4 -> x0, starting transfers between devices: 7.68 us -> none  [exchange(): near = lax.ppermute(beside, 'gx', chip)]
    ppermute x4 -> x0, waiting for transfers between devices: 4.72 us -> none  [exchange(): near = lax.ppermute(beside, 'gx', chip)]
    all_to_all x3, blocking collectives: 31.6 us -> 35.8 us  [exchange(): lax.all_to_all(send.reshape(2 * BASINS, rows, LANES), ('gx', 'gy'), 0, 0,...]
    ppermute x4, starting transfers between devices: 23.4 us -> 26.2 us  [exchange(): over = lax.ppermute(packed, 'gx', border)]
    all_to_all x1, waiting for transfers between devices: 7.94 us -> 9.15 us  [exchange(): lax.all_to_all(send.reshape(2 * BASINS, rows, LANES), ('gx', 'gy'), 0, 0,...]
  transfers between devices with their start and end apart: 10 -> 6, of which waited for: 9 -> 6; matrix products, arithmetic and copies ran while one was open for 0% -> 0% of each run, Pallas kernels for 2% -> 1%
where the time goes in v4:
time: 112 us
  starting transfers between devices  36.9 us (33%)
  blocking collectives  35.8 us (32%)
  waiting for transfers between devices  27.5 us (25%)
  Pallas kernels  9.64 us (9%)
    all_to_all x3, blocking collectives, exchange(): lax.all_to_all(send.reshape(2 * BASINS, rows, LANES), ('gx', 'gy'), 0, 0,...  35.8 us
    ppermute x4, starting transfers between devices, exchange(): over = lax.ppermute(packed, 'gx', border)  26.2 us
    ppermute x4, waiting for transfers between devices, exchange(): over = lax.ppermute(packed, 'gx', border)  12.1 us
    pallas_call x6, Pallas kernels, call(): pl.pallas_call(kernel, out_shape=outs, in_specs=specs, out_specs=[pl.Bloc...  9.64 us
    all_to_all x1, waiting for transfers between devices, exchange(): lax.all_to_all(send.reshape(2 * BASINS, rows, LANES), ('gx', 'gy'), 0, 0,...  9.15 us
    all_to_all x1, starting transfers between devices, exchange(): lax.all_to_all(send.reshape(2 * BASINS, rows, LANES), ('gx', 'gy'), 0, 0,...  7.35 us
    all_to_all x1, waiting for transfers between devices, per_device(): final = lax.all_to_all(copies, 'gy', 0, 0)  6.33 us
    all_to_all x1, starting transfers between devices, per_device(): final = lax.all_to_all(copies, 'gy', 0, 0)  3.34 us
  transfers between devices with their start and end apart: 6, of which 6 were waited for; matrix products, arithmetic and copies ran while one was open for 0% of the time, Pallas kernels for 1%

profile of v4, /device:TPU:6, one launch (start us, length us, event | category | flops | bytes accessed | tf_op | source)
XLA Modules:
  0.0 111.6 jit_solution(13531104968671160072)
XLA Ops:
  0.6 2.1 %shard_map.113 = (f32[2,8,24,128]{3,2,1,0:T(8,128)}, f32[80,128]{1,0:T(8,128)}, s32[24,128]{1,0:T(8,128)}, s32[24,128]{1,0:T(8,128)}, f32[24,128]{1,0:T(8,128)}, /*index=5*/f32[24,128]{1,0:T(8,128)}) custom-call(f32[32,512]{1,0:T(8,128)} %refs_0_.1, f32[2,32,512]{2,1,0:T(8,128)} %refs_1_.1, s32[24,128]{1,0:T(8,128)} %cell_in.1, s32[24,128]{1,0:T(8,128)} %site_in.1, ...), custom_call_target="tpu_custom_call" | custom-call | tf_op jit(solution)/shard_map/pallas_call | solution.py:483
  2.8 0.0 copy-start.2
  2.8 0.0 copy-start.5
  2.8 0.0 copy-start.8
  2.8 0.0 copy-start.9
  2.8 7.3 %all-to-all-start = ((f32[16,24,128]{2,1,0:T(8,128)}), f32[16,24,128]{2,1,0:T(8,128)S(1)}, u32[]{:S(2)}, u32[]{:S(2)}) async-start(f32[16,24,128]{2,1,0:T(8,128)} %bitcast.28), calls=%async_computation | async-start | bytes 393216 | tf_op jit(solution)/shard_map/all_to_all | solution.py:522
  10.2 0.0 copy-start.1
  10.2 9.1 %all-to-all-done = f32[16,24,128]{2,1,0:T(8,128)S(1)} async-done(((f32[16,24,128]{2,1,0:T(8,128)}), f32[16,24,128]{2,1,0:T(8,128)S(1)}, u32[]{:S(2)}, u32[]{:S(2)}) %all-to-all-start) | async-done | bytes 196640 | tf_op jit(solution)/shard_map/all_to_all | solution.py:522
  19.4 0.0 copy-start
  19.4 0.0 copy-start.3
  19.4 14.1 %collective-permute-start = (f32[144,128]{1,0:T(8,128)S(1)}, f32[144,128]{1,0:T(8,128)S(1)}, u32[]{:S(2)}, u32[]{:S(2)}) collective-permute-start(f32[144,128]{1,0:T(8,128)S(1)} %pad_maximum_fusion), channel_id=1, source_target_pairs={{8,16},{24,32},{40,48},{56,64},{72,80},{88,96},{104,112},{120,128}... | collective-permute-start | bytes 221192 | tf_op jit(solution)/shard_map/ppermute | solution.py:527
  33.6 0.0 copy-done.11
  33.6 0.1 copy.12.refs_6_
  33.6 1.9 %collective-permute-done.refs_8_ = f32[144,128]{1,0:T(8,128)S(1)} collective-permute-done((f32[144,128]{1,0:T(8,128)S(1)}, f32[144,128]{1,0:T(8,128)S(1)}, u32[]{:S(2)}, u32[]{:S(2)}) %collective-permute-start) | collective-permute-done | bytes 73760 | tf_op jit(solution)/shard_map/ppermute | solution.py:527
  35.6 0.0 copy-done.9
  35.7 1.7 %shard_map.114 = (f32[3,32,512]{2,1,0:T(8,128)S(1)}, f32[8,128]{1,0:T(8,128)S(1)}, f32[24,128]{1,0:T(8,128)S(1)}, f32[24,128]{1,0:T(8,128)S(1)}, f32[2,8,16,128]...) custom-call(f32[32,512]{1,0:T(8,128)S(1)} %copy-done.2, ...), custom_call_target="tpu_custom_call" | custom-call | tf_op jit(solution)/shard_map/pallas_call | solution.py:483
  37.4 12.6 %all_to_all.25 = f32[16,16,128]{2,1,0:T(8,128)S(1)} all-to-all(f32[16,16,128]{2,1,0:T(8,128)S(1)} %bitcast.25), channel_id=1, replica_groups={{0,1,2,3,4,5,6,7,8,9,10,11,12,13,14,15},{16,17,18,19,20,21,22,23,24,25,..., dimensions={0} | all-to-all | bytes 262144 | tf_op jit(solution)/shard_map/all_to_all | solution.py:522
  50.0 4.6 %collective-permute-start.1 = (f32[80,128]{1,0:T(8,128)S(1)}, f32[80,128]{1,0:T(8,128)S(1)}, u32[]{:S(2)}, u32[]{:S(2)}) collective-permute-start(f32[80,128]{1,0:T(8,128)S(1)} %pad_maximum_fusion.1), channel_id=1, source_target_pairs={{8,16},{24,32},{40,48},{56,64},{72,80},{88,96},{104,112},{120,128}... | collective-permute-start | bytes 122888 | tf_op jit(solution)/shard_map/ppermute | solution.py:527
  54.6 2.8 %collective-permute-done.1.refs_7_ = f32[80,128]{1,0:T(8,128)S(1)} collective-permute-done((f32[80,128]{1,0:T(8,128)S(1)}, f32[80,128]{1,0:T(8,128)S(1)}, u32[]{:S(2)}, u32[]{:S(2)}) %collective-permute-start.1) | collective-permute-done | bytes 40992 | tf_op jit(solution)/shard_map/ppermute | solution.py:527
  57.4 1.6 %shard_map.115 = (f32[3,32,512]{2,1,0:T(8,128)S(1)}, f32[8,128]{1,0:T(8,128)S(1)}, f32[24,128]{1,0:T(8,128)S(1)}, f32[24,128]{1,0:T(8,128)S(1)}, f32[2,8,16,128]{3,2,1,0:T(8,128)S(1)}, /*index=5*/f32[16,128]{1,0:T(8,128)S(1)}) custom-call(f32[3,32,512]{2,1,0:T(8,128)S(1)} %get-tuple-element.35.refs_0_, f32[8,128]{1,0:T(8,128)S(1)} %get-tuple-element.36.refs_1_, ...), custom_call_target="tpu_custom_call" | custom-call | tf_op jit(solution)/shard_map/pallas_call | solution.py:483
  59.0 11.6 %all_to_all.26 = f32[16,16,128]{2,1,0:T(8,128)S(1)} all-to-all(f32[16,16,128]{2,1,0:T(8,128)S(1)} %bitcast.26), channel_id=1, replica_groups={{0,1,2,3,4,5,6,7,8,9,10,11,12,13,14,15},{16,17,18,19,20,21,22,23,24,25,..., dimensions={0} | all-to-all | bytes 262144 | tf_op jit(solution)/shard_map/all_to_all | solution.py:522
  70.6 4.0 %collective-permute-start.2 = (f32[80,128]{1,0:T(8,128)S(1)}, f32[80,128]{1,0:T(8,128)S(1)}, u32[]{:S(2)}, u32[]{:S(2)}) collective-permute-start(f32[80,128]{1,0:T(8,128)S(1)} %pad_maximum_fusion.2), channel_id=1, source_target_pairs={{8,16},{24,32},{40,48},{56,64},{72,80},{88,96},{104,112},{120,128}... | collective-permute-start | bytes 122888 | tf_op jit(solution)/shard_map/ppermute | solution.py:527
  74.7 3.4 %collective-permute-done.2.refs_7_ = f32[80,128]{1,0:T(8,128)S(1)} collective-permute-done((f32[80,128]{1,0:T(8,128)S(1)}, f32[80,128]{1,0:T(8,128)S(1)}, u32[]{:S(2)}, u32[]{:S(2)}) %collective-permute-start.2) | collective-permute-done | bytes 40992 | tf_op jit(solution)/shard_map/ppermute | solution.py:527
  78.1 1.6 %shard_map.116 = (f32[3,32,512]{2,1,0:T(8,128)S(1)}, f32[8,128]{1,0:T(8,128)S(1)}, f32[24,128]{1,0:T(8,128)S(1)}, f32[24,128]{1,0:T(8,128)S(1)}, f32[2,8,16,128]{3,2,1,0:T(8,128)S(1)}, /*index=5*/f32[16,128]{1,0:T(8,128)S(1)}) custom-call(f32[3,32,512]{2,1,0:T(8,128)S(1)} %get-tuple-element.44.refs_0_, f32[8,128]{1,0:T(8,128)S(1)} %get-tuple-element.45.refs_1_, ...), custom_call_target="tpu_custom_call" | custom-call | tf_op jit(solution)/shard_map/pallas_call | solution.py:483
  79.7 11.6 %all_to_all.27 = f32[16,16,128]{2,1,0:T(8,128)S(1)} all-to-all(f32[16,16,128]{2,1,0:T(8,128)S(1)} %bitcast.27), channel_id=1, replica_groups={{0,1,2,3,4,5,6,7,8,9,10,11,12,13,14,15},{16,17,18,19,20,21,22,23,24,25,..., dimensions={0} | all-to-all | bytes 262144 | tf_op jit(solution)/shard_map/all_to_all | solution.py:522
  91.3 3.5 %collective-permute-start.3 = (f32[80,128]{1,0:T(8,128)S(1)}, f32[80,128]{1,0:T(8,128)S(1)}, u32[]{:S(2)}, u32[]{:S(2)}) collective-permute-start(f32[80,128]{1,0:T(8,128)S(1)} %pad_maximum_fusion.3), channel_id=1, source_target_pairs={{8,16},{24,32},{40,48},{56,64},{72,80},{88,96},{104,112},{120,128}... | collective-permute-start | bytes 122888 | tf_op jit(solution)/shard_map/ppermute | solution.py:527
  94.8 3.9 %collective-permute-done.3.over = f32[80,128]{1,0:T(8,128)S(1)} collective-permute-done((f32[80,128]{1,0:T(8,128)S(1)}, f32[80,128]{1,0:T(8,128)S(1)}, u32[]{:S(2)}, u32[]{:S(2)}) %collective-permute-start.3) | collective-permute-done | bytes 40992 | tf_op jit(solution)/shard_map/ppermute | solution.py:527
  98.7 0.9 shard_map.118
  99.7 3.3 %all-to-all-start.4 = ((f32[8,8,128]{2,1,0:T(8,128)}), f32[8,8,128]{2,1,0:T(8,128)S(1)}, u32[]{:S(2)}, u32[]{:S(2)}) async-start(f32[8,8,128]{2,1,0:T(8,128)} %shard_map.118), calls=%async_computation.4 | async-start | bytes 65536 | tf_op jit(solution)/shard_map/all_to_all | solution.py:571
  103.0 1.6 %shard_map.117 = f32[3,32,512]{2,1,0:T(8,128)} custom-call(f32[3,32,512]{2,1,0:T(8,128)S(1)} %get-tuple-element.50.state, f32[2,8,16,128]{3,2,1,0:T(8,128)S(1)} %bitcast.21, f32[80,128]{1,0:T(8,128)S(1)} %collective-permute-done.3.over, f32[32,512]{1,0:T(8,128)S(1)} %copy-done, s32[24,128]{1,0:T(8,128)S(1)} %copy-done.3, f32[24,128]{1,0:T(8,128)S(1)} %copy-done.4, ...), custom_call_target="tpu_custom_call" | custom-call | tf_op jit(solution)/shard_map/pallas_call | solution.py:483
  104.6 6.3 %all-to-all-done.4 = f32[8,8,128]{2,1,0:T(8,128)S(1)} async-done(((f32[8,8,128]{2,1,0:T(8,128)}), f32[8,8,128]{2,1,0:T(8,128)S(1)}, u32[]{:S(2)}, u32[]{:S(2)}) %all-to-all-start.4) | async-done | bytes 32800 | tf_op jit(solution)/shard_map/all_to_all | solution.py:571
  111.0 0.6 copy.15
  (23 shorter events, 0.1 us)
Async XLA Ops:
  2.8 16.6 %copy-start.10 = (f32[80,128]{1,0:T(8,128)S(1)}, f32[80,128]{1,0:T(8,128)}, u32[]{:S(2)}) copy-start(f32[80,128]{1,0:T(8,128)} %get-tuple-element.31) | copy-start | bytes 122884
  2.8 32.8 %copy-start.2 = (f32[32,512]{1,0:T(8,128)S(1)}, f32[32,512]{1,0:T(8,128)}, u32[]{:S(2)}) copy-start(f32[32,512]{1,0:T(8,128)} %refs_0_.1) | copy-start | bytes 196612
  2.8 32.8 %copy-start.5 = (f32[8,1024]{1,0:T(8,128)S(1)}, f32[8,1024]{1,0:T(8,128)}, u32[]{:S(2)}) copy-start(f32[8,1024]{1,0:T(8,128)} %refs_2_.1) | copy-start | bytes 98308
  2.8 32.8 %copy-start.8 = (f32[8,8]{1,0:T(8,128)S(1)}, f32[8,8]{1,0:T(8,128)}, u32[]{:S(2)}) copy-start(f32[8,8]{1,0:T(8,128)} %refs_4_.1) | copy-start | bytes 772
  2.8 32.8 %copy-start.9 = (f32[8,8]{1,0:T(8,128)S(1)}, f32[8,8]{1,0:T(8,128)}, u32[]{:S(2)}) copy-start(f32[8,8]{1,0:T(8,128)} %refs_5_.1) | copy-start | bytes 772
  2.8 16.5 %all-to-all-start = ((f32[16,24,128]{2,1,0:T(8,128)}), f32[16,24,128]{2,1,0:T(8,128)S(1)}, u32[]{:S(2)}, u32[]{:S(2)}) async-start(f32[16,24,128]{2,1,0:T(8,128)} %bitcast.28), calls=%async_computation | async-start | bytes 393216 | tf_op jit(solution)/shard_map/all_to_all | solution.py:522
  10.2 25.4 %copy-start.1 = (f32[2,32,512]{2,1,0:T(8,128)S(1)}, f32[2,32,512]{2,1,0:T(8,128)}, u32[]{:S(2)}) copy-start(f32[2,32,512]{2,1,0:T(8,128)} %refs_1_.1) | copy-start | bytes 393220
  19.4 14.2 %copy-start.11 = (s32[8,2]{0,1:T(2,128)S(1)}, s32[8,2]{0,1:T(2,128)}, u32[]{:S(2)}) copy-start(s32[8,2]{0,1:T(2,128)} %param.16) | copy-start | bytes 196
  19.4 16.2 %copy-start = (f32[32,512]{1,0:T(8,128)S(1)}, f32[32,512]{1,0:T(8,128)}, u32[]{:S(2)}) copy-start(f32[32,512]{1,0:T(8,128)} %rough.1) | copy-start | bytes 196612
  19.4 16.2 %copy-start.4 = (f32[24,128]{1,0:T(8,128)S(1)}, f32[24,128]{1,0:T(8,128)}, u32[]{:S(2)}) copy-start(f32[24,128]{1,0:T(8,128)} %get-tuple-element.33.refs_11_.refs_10_.coeff_ref) | copy-start | bytes 36868
  19.4 16.2 %copy-start.6 = (s32[24,128]{1,0:T(8,128)S(1)}, s32[24,128]{1,0:T(8,128)}, u32[]{:S(2)}) copy-start(s32[24,128]{1,0:T(8,128)} %get-tuple-element.29.refs_3_) | copy-start | bytes 36868
  19.4 16.2 %copy-start.7 = (f32[24,128]{1,0:T(8,128)S(1)}, f32[24,128]{1,0:T(8,128)}, u32[]{:S(2)}) copy-start(f32[24,128]{1,0:T(8,128)} %get-tuple-element.34.refs_12_) | copy-start | bytes 36868
  19.4 16.2 %copy-start.3 = (s32[24,128]{1,0:T(8,128)S(1)}, s32[24,128]{1,0:T(8,128)}, u32[]{:S(2)}) copy-start(s32[24,128]{1,0:T(8,128)} %get-tuple-element.32.refs_10_.refs_9_.cell_ref) | copy-start | bytes 36868
  19.4 16.1 %collective-permute-start = (f32[144,128]{1,0:T(8,128)S(1)}, f32[144,128]{1,0:T(8,128)S(1)}, u32[]{:S(2)}, u32[]{:S(2)}) collective-permute-start(f32[144,128]{1,0:T(8,128)S(1)} %pad_maximum_fusion), channel_id=1, source_target_pairs={{8,16},{24,32},{40,48},{56,64},{72,80},{88,96},{104,112},{120,128}... | collective-permute-start | bytes 221192 | tf_op jit(solution)/shard_map/ppermute | solution.py:527
  50.0 7.4 %collective-permute-start.1 = (f32[80,128]{1,0:T(8,128)S(1)}, f32[80,128]{1,0:T(8,128)S(1)}, u32[]{:S(2)}, u32[]{:S(2)}) collective-permute-start(f32[80,128]{1,0:T(8,128)S(1)} %pad_maximum_fusion.1), channel_id=1, source_target_pairs={{8,16},{24,32},{40,48},{56,64},{72,80},{88,96},{104,112},{120,128}... | collective-permute-start | bytes 122888 | tf_op jit(solution)/shard_map/ppermute | solution.py:527
  70.6 7.4 %collective-permute-start.2 = (f32[80,128]{1,0:T(8,128)S(1)}, f32[80,128]{1,0:T(8,128)S(1)}, u32[]{:S(2)}, u32[]{:S(2)}) collective-permute-start(f32[80,128]{1,0:T(8,128)S(1)} %pad_maximum_fusion.2), channel_id=1, source_target_pairs={{8,16},{24,32},{40,48},{56,64},{72,80},{88,96},{104,112},{120,128}... | collective-permute-start | bytes 122888 | tf_op jit(solution)/shard_map/ppermute | solution.py:527
  91.3 7.4 %collective-permute-start.3 = (f32[80,128]{1,0:T(8,128)S(1)}, f32[80,128]{1,0:T(8,128)S(1)}, u32[]{:S(2)}, u32[]{:S(2)}) collective-permute-start(f32[80,128]{1,0:T(8,128)S(1)} %pad_maximum_fusion.3), channel_id=1, source_target_pairs={{8,16},{24,32},{40,48},{56,64},{72,80},{88,96},{104,112},{120,128}... | collective-permute-start | bytes 122888 | tf_op jit(solution)/shard_map/ppermute | solution.py:527
  99.7 11.3 %all-to-all-start.4 = ((f32[8,8,128]{2,1,0:T(8,128)}), f32[8,8,128]{2,1,0:T(8,128)S(1)}, u32[]{:S(2)}, u32[]{:S(2)}) async-start(f32[8,8,128]{2,1,0:T(8,128)} %shard_map.118), calls=%async_computation.4 | async-start | bytes 65536 | tf_op jit(solution)/shard_map/all_to_all | solution.py:571

commit v5 on v3

v5 whole, which is shorter than its diff:
```python
import functools

import jax
import jax.numpy as jnp
from jax import lax
from jax.experimental import pallas as pl
from jax.experimental.pallas import tpu as pltpu
from jax.sharding import PartitionSpec as P

STEPS = 4


GRAV = 9.81
DT = 0.5
DX = 10.0
NU = 0.1
RATIO = 0.25
FACTOR = DT / (2.0 * DX)

LANES = 128
ROWS = 32
QUADS = 4
COLS = QUADS * LANES
FIELDS = 8
BASINS = 8
SLOT_ROWS = 3 * BASINS
INTERPRET = False

FIRST_EDGE = 24
FIRST_LEVELS = 40
FIRST_SWAP = FIRST_LEVELS + FIELDS * BASINS
OUTLET = 16
EDGE = 24
SWAP = 40


def iota(shape, dim):
    return lax.broadcasted_iota(jnp.int32, shape, dim)


def lane_gather(rows, index):
    return jnp.take_along_axis(rows, index, axis=1, mode="promise_in_bounds")


def lane_to_column(row, count, offset):
    wide = jnp.broadcast_to(row, (count, LANES))
    hit = iota((count, LANES), 1) == iota((count, LANES), 0) + offset
    return jnp.sum(jnp.where(hit, wide, 0.0), axis=1, keepdims=True)


def column_to_lane(column, offset):
    count = column.shape[0]
    wide = jnp.broadcast_to(column, (count, LANES))
    hit = iota((count, LANES), 1) == iota((count, LANES), 0) + offset
    return jnp.sum(jnp.where(hit, wide, 0.0), axis=0, keepdims=True)


def own_row(block, y):
    return jnp.sum(jnp.where(iota(block.shape, 0) == y, block, 0.0), axis=0, keepdims=True)


def flux_terms(cells):
    h, p, q = cells
    inverse = 1.0 / h
    u = p * inverse
    v = q * inverse
    pressure = 0.5 * GRAV * h * h
    return (p, p * u + pressure, q * u), (q, p * v, q * v + pressure), u, v


def flood_update(cells, top, low, left, right, rough, source):
    flux_x, flux_y, u, v = flux_terms(cells)
    top_x = flux_terms(top)[0]
    low_x = flux_terms(low)[0]
    left_y = flux_terms(left)[1]
    right_y = flux_terms(right)[1]
    row = iota((ROWS, COLS), 0)
    col = iota((ROWS, COLS), 1)
    out = []
    for k in range(3):
        quarter = 0.25 * cells[k]
        from_top = jnp.where(
            row == 0, 0.25 * top[k] + FACTOR * top_x[k], pltpu.roll(quarter + FACTOR * flux_x[k], 1, 0)
        )
        from_low = jnp.where(
            row == ROWS - 1,
            0.25 * low[k] - FACTOR * low_x[k],
            pltpu.roll(quarter - FACTOR * flux_x[k], ROWS - 1, 0),
        )
        from_left = jnp.where(
            col == 0, 0.25 * left[k] + FACTOR * left_y[k], pltpu.roll(quarter + FACTOR * flux_y[k], 1, 1)
        )
        from_right = jnp.where(
            col == COLS - 1,
            0.25 * right[k] - FACTOR * right_y[k],
            pltpu.roll(quarter - FACTOR * flux_y[k], COLS - 1, 1),
        )
        out.append((from_top + from_low) + (from_left + from_right))
    h = cells[0]
    size = jnp.abs(h)
    root = jnp.exp(jnp.log(size) * (-1.0 / 3.0))
    root = root * (4.0 - size * (root * root * root)) * (1.0 / 3.0)
    root = jnp.where(h < 0.0, -root, root)
    drag = (GRAV * DT) * rough * rough * jnp.sqrt(u * u + v * v) * root
    return [out[0] + DT * source, out[1] - drag * u, out[2] - drag * v]


def halves(values):
    high = values.astype(jnp.bfloat16).astype(jnp.float32)
    return high, values - high


def spread(rates, major, minor, count):
    total = None
    rows = rates.shape[0]
    group = 4
    high, low = halves(rates)
    for start in range(0, rows, group):
        left, right = [], []
        for r in range(start, start + group):
            at = iota((count, LANES), 0) == major[r : r + 1]
            left.append(
                jnp.concatenate(
                    [
                        jnp.where(at, high[r : r + 1], 0.0),
                        jnp.where(at, low[r : r + 1], 0.0),
                    ],
                    axis=0,
                ).astype(jnp.bfloat16)
            )
            right.append(
                jnp.where(iota((LANES, LANES), 0) == minor[r : r + 1], 1.0, 0.0).astype(jnp.bfloat16)
            )
        part = lax.dot_general(
            jnp.concatenate(left, axis=1),
            jnp.concatenate(right, axis=1),
            (((1,), (1,)), ((), ())),
            preferred_element_type=jnp.float32,
        )
        total = part if total is None else total + part
    return total[:count] + total[count:]


def cell_parts(cell):
    col = cell & (COLS - 1)
    return (col >> 7) * ROWS + (cell >> 9), col & (LANES - 1)


def depth_at_slots(h_ref, index, cell):
    major, minor = cell_parts(cell)
    found = []
    for v in range(3):
        key = major[8 * v : 8 * v + 8]
        lane = minor[8 * v : 8 * v + 8]
        depth = jnp.zeros((8, LANES), jnp.float32)
        for quad in range(QUADS):
            for row in range(ROWS):
                values = h_ref[index + (slice(row, row + 1), slice(quad * LANES, (quad + 1) * LANES))]
                values = jnp.broadcast_to(values, (8, LANES))
                depth = jnp.where(key == quad * ROWS + row, lane_gather(values, lane), depth)
        found.append(depth)
    return jnp.concatenate(found, axis=0)


def level_at_sites(reach_rows, site):
    found = []
    for v in range(3):
        sites = site[8 * v : 8 * v + 8]
        field = sites >> 7
        station = sites & (LANES - 1)
        level = jnp.zeros((8, LANES), jnp.float32)
        for f in range(FIELDS):
            level = jnp.where(field == f, lane_gather(reach_rows(f, v), station), level)
        found.append(level)
    return jnp.concatenate(found, axis=0)


def edge_columns(cells):
    left = column_to_lane(cells[0][:, 0:1], 0)
    right = column_to_lane(cells[0][:, COLS - 1 : COLS], 0)
    for k in (1, 2):
        left = left + column_to_lane(cells[k][:, 0:1], k * ROWS)
        right = right + column_to_lane(cells[k][:, COLS - 1 : COLS], k * ROWS)
    return left, right


def put_edges(beside_ref, across_ref, cells, even, start):
    for k in range(3):
        first = cells[k][0:1]
        last = cells[k][ROWS - 1 : ROWS]
        inner = jnp.where(even, last, first)
        outer = jnp.where(even, first, last)
        for quad in range(QUADS):
            at = start + k * QUADS + quad
            lanes = slice(quad * LANES, (quad + 1) * LANES)
            beside_ref[at : at + 1, :] = inner[:, lanes]
            across_ref[at : at + 1, :] = outer[:, lanes]


def get_edges(got_ref, near_ref, over_ref, cells, spot, start, col_row):
    even, y, is_first, is_last = spot
    before = got_ref[jnp.maximum(y - 1, 0), col_row : col_row + 1, :]
    after = got_ref[jnp.minimum(y + 1, BASINS - 1), col_row : col_row + 1, :]

    def edge(ref, k):
        rows = [ref[start + k * QUADS + q : start + k * QUADS + q + 1, :] for q in range(QUADS)]
        return jnp.concatenate(rows, axis=1)

    top, low, left, right = [], [], [], []
    for k in range(3):
        inner = edge(near_ref, k)
        outer = edge(over_ref, k)
        top.append(jnp.where(is_first, cells[k][0:1], jnp.where(even, outer, inner)))
        low.append(jnp.where(is_last, cells[k][ROWS - 1 : ROWS], jnp.where(even, inner, outer)))
        left.append(jnp.where(y == 0, cells[k][:, 0:1], lane_to_column(before, ROWS, k * ROWS)))
        right.append(
            jnp.where(
                y == BASINS - 1, cells[k][:, COLS - 1 : COLS], lane_to_column(after, ROWS, k * ROWS)
            )
        )
    return top, low, left, right


def inflow_of(own, outlets):
    row = jnp.sum(own[16:24] * outlets, axis=0, keepdims=True)
    return own[8:16, 0:1] + lane_to_column(row, FIELDS, 0)


def river_update(current, inflow, rate, lateral):
    lane = iota((FIELDS, LANES), 1)
    sub = iota((FIELDS, LANES), 0)
    behind = jnp.where(lane == 0, inflow, pltpu.roll(current, 1, 1))
    above = jnp.where(sub == FIELDS - 1, current, pltpu.roll(current, FIELDS - 1, 0))
    below = jnp.where(sub == 0, current, pltpu.roll(current, 1, 0))
    mixing = above - 2.0 * current + below
    return current - rate * (current - behind) + NU * mixing - (DT * RATIO) * lateral


def owned_terms(celerity, base_inflow, upstream, y):
    square = iota((FIELDS, FIELDS), 0) == iota((FIELDS, FIELDS), 1)

    def by_field(ref):
        row = jnp.broadcast_to(own_row(ref[...], y), (FIELDS, FIELDS))
        return jnp.sum(jnp.where(square, row, 0.0), axis=1, keepdims=True)

    feeders = own_row(upstream[...].astype(jnp.float32), y)
    ids = ((lax.axis_index("gx") - 1) * BASINS + iota((BASINS, feeders.shape[1]), 0)).astype(jnp.float32)
    hits = jnp.where(jnp.broadcast_to(feeders, ids.shape) == ids, 1.0, 0.0)
    weight = jnp.sum(hits, axis=1, keepdims=True)
    return jnp.concatenate(
        [jnp.broadcast_to(column, (8, LANES)) for column in (by_field(celerity), by_field(base_inflow), weight)],
        axis=0,
    )


def place():
    gx = lax.axis_index("gx")
    return (gx & 1) == 0, lax.axis_index("gy"), gx == 0, gx == lax.axis_size("gx") - 1


def first_kernel(
    depth,
    discharge,
    cell_in,
    site_in,
    coeff_in,
    reach,
    beside_ref,
    across_ref,
    mine_ref,
    cell_ref,
    site_ref,
    coeff_ref,
    slots_ref,
):
    even = place()[0]

    def arranged(ref):
        low, own, high = ref[0:8], ref[8:16], ref[16:24]
        return jnp.concatenate([own, jnp.where(even, high, low), jnp.where(even, low, high)], axis=0)

    cell = arranged(cell_in)
    site = arranged(site_in)
    coeff = jnp.where(cell >= 0, arranged(coeff_in), 0.0)
    cell = jnp.maximum(cell, 0)
    cell_ref[...] = cell
    site_ref[...] = site
    coeff_ref[...] = coeff
    slots = depth_at_slots(depth, (), cell)
    slots_ref[...] = slots
    for at, value in enumerate((slots, site.astype(jnp.float32), coeff)):
        for v, ref in enumerate((mine_ref, beside_ref, across_ref)):
            ref[8 * at : 8 * at + 8] = value[8 * v : 8 * v + 8]
    cells = [depth[...], discharge[0], discharge[1]]
    mine_ref[24:32] = jnp.zeros((8, LANES), jnp.float32)
    left, right = edge_columns(cells)
    mine_ref[24:25] = left
    mine_ref[25:26] = right
    for ref in (beside_ref, across_ref):
        ref[FIRST_EDGE:FIRST_LEVELS] = jnp.zeros((FIRST_LEVELS - FIRST_EDGE, LANES), jnp.float32)
        for f in range(FIELDS):
            at = FIRST_LEVELS + 8 * f
            ref[at : at + 8] = reach[:, f * LANES : (f + 1) * LANES]
    put_edges(beside_ref, across_ref, cells, even, FIRST_EDGE)


def column_for(mine, b, start):
    y = lax.axis_index("gy")
    left = mine[start : start + 1]
    right = mine[start + 1 : start + 2]
    return jnp.where(b == y - 1, left, jnp.where(b == y + 1, right, 0.0))


def first_pack(mine, near, over, send):
    refs = (mine, near, over)
    for b in range(BASINS):
        for v, ref in enumerate(refs):
            send[b, v : v + 1] = ref[b : b + 1]
            send[b, 3 + v : 4 + v] = ref[16 + b : 17 + b]
            send[b, 8 + 8 * v : 16 + 8 * v] = ref[8:16]
        send[b, 6:7] = column_for(mine, b, 24)
        send[b, 7:8] = jnp.zeros((1, LANES), jnp.float32)


def pack(mine, near, over, send):
    even = place()[0]
    outlet = jnp.where(even, over[OUTLET : OUTLET + 1], near[OUTLET : OUTLET + 1])
    refs = (mine, near, over)
    for b in range(BASINS):
        for v, ref in enumerate(refs):
            send[b, v : v + 1] = ref[b : b + 1]
            send[b, 3 + v : 4 + v] = ref[8 + b : 9 + b]
        send[b, 6:7] = column_for(mine, b, 16)
        send[b, 7:8] = outlet


def last_pack(mine, near, over, send):
    even = place()[0]
    outlet = jnp.where(even, over[OUTLET : OUTLET + 1], near[OUTLET : OUTLET + 1])
    refs = (mine, near, over)
    for b in range(BASINS):
        for v, ref in enumerate(refs):
            send[b, 3 + v : 4 + v] = ref[8 + b : 9 + b]
            send[b, 8 + 8 * v : 16 + 8 * v] = ref[0:8]
            send[b, v : v + 1] = jnp.zeros((1, LANES), jnp.float32)
        send[b, 6:7] = column_for(mine, b, 16)
        send[b, 7:8] = outlet
        send[b, 32:40] = mine[24:32]


def gathered(got, row):
    return jnp.concatenate([got[:, row + v, :] for v in range(3)], axis=0)


def advance_levels(current, outlets, own, site_owner, coeff_owner, segment_owner, slots_owner):
    rates = coeff_owner * (segment_owner - slots_owner)
    lateral = spread(rates, site_owner >> 7, site_owner & (LANES - 1), FIELDS)
    return river_update(current, inflow_of(own, outlets), own[0:8], lateral)


def advance_cells(cells, edges, rough, cell, coeff, segment, slots):
    major, minor = cell_parts(cell)
    rates = coeff * (segment - slots)
    blocks = spread(rates, major, minor, QUADS * ROWS)
    source = jnp.concatenate([blocks[q * ROWS : (q + 1) * ROWS] for q in range(QUADS)], axis=1)
    return flood_update(cells, *edges, rough, source)


def last_kernel(
    state, got, near, over, rough, cell_ref, coeff_ref, slots_ref, got_first, celerity, base_inflow, upstream, state_out, reach_out
):
    cells = [state[0], state[1], state[2]]
    edges = get_edges(got, near, over, cells, place(), EDGE, 6)
    new = advance_cells(
        cells, edges, rough[...], cell_ref[...], coeff_ref[...], gathered(got, 3), slots_ref[...]
    )
    for k in range(3):
        state_out[k] = new[k]
    outlets = got[:, 7, :]
    lane = iota((FIELDS, LANES), 1)
    for b in range(BASINS):
        own = owned_terms(celerity, base_inflow, upstream, b)
        site = jnp.concatenate([got_first[:, 8 + 8 * v + b, :] for v in range(3)], axis=0)
        site = site.astype(jnp.int32)
        held = jnp.concatenate([got[:, 8 + 8 * v + b, :] for v in range(3)], axis=0)
        drawn = spread(held, site >> 7, site & (LANES - 1), FIELDS)
        entering = jnp.where(lane == 0, own[0:8] * inflow_of(own, outlets), 0.0)
        level = got[b, 32:40, :] + entering + (DT * RATIO) * drawn
        for f in range(FIELDS):
            reach_out[b : b + 1, f * LANES : (f + 1) * LANES] = level[f : f + 1]


def step_kernel(first, tail, *refs):
    refs = list(refs)

    def take(n):
        taken = refs[:n]
        del refs[:n]
        return taken

    if first:
        depth, discharge, reach, site_ref, celerity, base_inflow, upstream = take(7)
    else:
        state, levels, owner_levels, owner_site, owner_coeff, own_ref = take(6)
    got, near, over, rough, cell_ref, coeff_ref, slots_ref = take(7)
    state_out, levels_out, owner_levels_out, slots_out, beside_ref, across_ref, mine_ref = take(7)
    if first:
        owner_site_out, owner_coeff_out, own_out = take(3)
    spot = place()
    even, y = spot[0], spot[1]
    cell = cell_ref[...]

    slots_owner = gathered(got, 0)
    if first:
        cells = [depth[...], discharge[0], discharge[1]]
        current = jnp.concatenate(
            [own_row(reach[:, f * LANES : (f + 1) * LANES], y) for f in range(FIELDS)], axis=0
        )

        def tile_rows(f, v):
            if v == 0:
                return reach[:, f * LANES : (f + 1) * LANES]
            return (near if v == 1 else over)[FIRST_LEVELS + 8 * f : FIRST_LEVELS + 8 * f + 8, :]

        segment = level_at_sites(tile_rows, site_ref[...])
        site_owner = jnp.concatenate([got[:, 8 + 8 * v + y, :] for v in range(3)], axis=0)
        site_owner = site_owner.astype(jnp.int32)
        coeff_owner = gathered(got, 3)
        outlets = jnp.zeros((BASINS, LANES), jnp.float32)
        for f in range(FIELDS):
            source_rows = jnp.where(even, tile_rows(f, 2), tile_rows(f, 1))
            outlets = jnp.where(
                iota((BASINS, LANES), 1) == f, source_rows[:, LANES - 1 : LANES], outlets
            )
        segment_owner = level_at_sites(
            lambda f, v: jnp.broadcast_to(current[f : f + 1], (8, LANES)), site_owner
        )
        own = owned_terms(celerity, base_inflow, upstream, y)
        owner_site_out[...] = site_owner
        owner_coeff_out[...] = coeff_owner
        own_out[...] = own
    else:
        cells = [state[0], state[1], state[2]]
        current = levels[...]
        segment = gathered(got, 3)
        site_owner = owner_site[...]
        coeff_owner = owner_coeff[...]
        segment_owner = owner_levels[...]
        outlets = got[:, 7, :]
        own = own_ref[...]

    levels_next = advance_levels(
        current, outlets, own, site_owner, coeff_owner, segment_owner, slots_owner
    )
    edges = get_edges(got, near, over, cells, spot, FIRST_EDGE if first else EDGE, 6)
    new = advance_cells(cells, edges, rough[...], cell, coeff_ref[...], segment, slots_ref[...])
    for k in range(3):
        state_out[k] = new[k]
    levels_out[...] = levels_next
    owned = level_at_sites(
        lambda f, v: jnp.broadcast_to(levels_next[f : f + 1], (8, LANES)), site_owner
    )
    owner_levels_out[...] = owned
    slots = depth_at_slots(state_out, (0,), cell)
    slots_out[...] = slots
    if tail:
        slots = slots * coeff_ref[...]
    blank = jnp.zeros((8, LANES), jnp.float32)
    outlet_row = column_to_lane(levels_next[:, LANES - 1 : LANES], 0)
    for v, ref in enumerate((mine_ref, beside_ref, across_ref)):
        ref[0:8] = slots[8 * v : 8 * v + 8]
        ref[8:16] = owned[8 * v : 8 * v + 8]
        ref[16:24] = blank
        if v > 0:
            ref[OUTLET : OUTLET + 1] = outlet_row
            ref[EDGE : EDGE + 8] = blank
            ref[EDGE + 8 : EDGE + 16] = blank
    left, right = edge_columns(new)
    mine_ref[16:17] = left
    mine_ref[17:18] = right
    put_edges(beside_ref, across_ref, new, even, EDGE)
    if tail:
        total = spread(coeff_owner, site_owner >> 7, site_owner & (LANES - 1), FIELDS)
        none = jnp.zeros((FIELDS, 1), jnp.float32)
        mine_ref[24:32] = river_update(levels_next, none, own[0:8], total * levels_next)
    else:
        mine_ref[24:32] = blank


def call(kernel, outs, args, limit=16 << 20):
    return pl.pallas_call(
        kernel,
        out_shape=outs,
        in_specs=[pl.BlockSpec(memory_space=pltpu.VMEM) for _ in args],
        out_specs=[pl.BlockSpec(memory_space=pltpu.VMEM) for _ in outs],
        compiler_params=None if INTERPRET else pltpu.CompilerParams(vmem_limit_bytes=limit),
        interpret=INTERPRET,
    )(*args)


def f32(*shape):
    return jax.ShapeDtypeStruct(shape, jnp.float32)


def i32(*shape):
    return jax.ShapeDtypeStruct(shape, jnp.int32)


def per_device(
    depth,
    discharge,
    roughness,
    reach_state,
    celerity,
    base_inflow,
    upstream,
    bank_cell,
    bank_site,
    bank_coeff,
):
    count_x = lax.axis_size("gx")
    chip = [(i, i ^ 1) for i in range(count_x)]
    border = [(i, i + 1) for i in range(1, count_x - 1, 2)]
    border = border + [(b, a) for a, b in border]

    def exchange(kernel, rows, beside, across, mine):
        across, beside = lax.optimization_barrier((across, beside))
        near = lax.ppermute(beside, "gx", chip)
        over = lax.ppermute(across, "gx", border)
        over, near = lax.optimization_barrier((over, near))
        send = call(kernel, [f32(BASINS, rows, LANES)], [mine, near, over])[0]
        return lax.all_to_all(send, "gy", 0, 0), near, over

    table = (SLOT_ROWS, LANES)
    beside, across, mine, cell, site, coeff, slots = call(
        first_kernel,
        [
            f32(FIRST_SWAP, LANES),
            f32(FIRST_SWAP, LANES),
            f32(32, LANES),
            i32(*table),
            i32(*table),
            f32(*table),
            f32(*table),
        ],
        [depth, discharge, bank_cell, bank_site, bank_coeff, reach_state],
        limit=60 << 20,
    )
    got, near, over = exchange(first_pack, 32, beside, across, mine)
    got_first = got
    for step in range(STEPS - 1):
        first, tail = step == 0, step == STEPS - 2
        outs = [
            f32(3, ROWS, COLS),
            f32(FIELDS, LANES),
            f32(*table),
            f32(*table),
            f32(SWAP, LANES),
            f32(SWAP, LANES),
            f32(32, LANES),
        ]
        if first:
            outs += [i32(*table), f32(*table), f32(*table)]
            args = [depth, discharge, reach_state, site, celerity, base_inflow, upstream]
        else:
            args = [state, levels, owner_levels, owner_site, owner_coeff, own]
        args += [got, near, over, roughness, cell, coeff, slots]
        result = call(functools.partial(step_kernel, first, tail), outs, args)
        state, levels, owner_levels, slots, beside, across, mine = result[:7]
        if first:
            owner_site, owner_coeff, own = result[7:10]
        got, near, over = exchange(last_pack if tail else pack, 40 if tail else 8, beside, across, mine)
    state, reach = call(
        last_kernel,
        [f32(3, ROWS, COLS), f32(BASINS, FIELDS * LANES)],
        [state, got, near, over, roughness, cell, coeff, slots, got_first, celerity, base_inflow, upstream],
    )
    return state, reach


def solution(mesh):
    return jax.shard_map(
        per_device,
        mesh=mesh,
        in_specs=(
            P("gx", "gy"),
            P(None, "gx", "gy"),
            P("gx", "gy"),
            P("gx", None),
            P("gx", None),
            P("gx", None),
            P("gx", None),
            P("gx", "gy"),
            P("gx", "gy"),
            P("gx", "gy"),
        ),
        out_specs=(P(None, "gx", "gy"), P("gx", None)),
        check_vma=False,
    )
```

time: 109 us -> 102 us (0.936)
  waiting for transfers between devices: 22.8 us -> 18.3 us
  starting transfers between devices: 41.8 us -> 37.4 us
  Pallas kernels: 9.58 us -> 11.6 us
    all_to_all x2 -> x1, waiting for transfers between devices: 14.3 us -> 9.29 us  [exchange(): return (lax.all_to_all(send, 'gy', 0, 0), near, over)]
    ppermute x4, waiting for transfers between devices: 3.83 us -> 7.78 us  [exchange(): over = lax.ppermute(across, 'gx', border)]
    all_to_all x2 -> x1, starting transfers between devices: 10.7 us -> 7.23 us  [exchange(): return (lax.all_to_all(send, 'gy', 0, 0), near, over)]
    ppermute x4, waiting for transfers between devices: 4.72 us -> 1.26 us  [exchange(): near = lax.ppermute(beside, 'gx', chip)]
    pallas_call x6 -> x9, Pallas kernels: 9.58 us -> 11.6 us  [call(): pl.pallas_call(kernel, out_shape=outs, in_specs=[pl.BlockSpec(memory_spac...]
  transfers between devices with their start and end apart: 10 -> 9, of which waited for: 9 -> 6; matrix products, arithmetic and copies ran while one was open for 0% -> 0% of each run, Pallas kernels for 2% -> 0%
where the time goes in v5:
time: 102 us
  starting transfers between devices  37.4 us (37%)
  blocking collectives  32.6 us (32%)
  waiting for transfers between devices  18.3 us (18%)
  Pallas kernels  11.6 us (11%)
    all_to_all x3, blocking collectives, exchange(): return (lax.all_to_all(send, 'gy', 0, 0), near, over)  32.6 us
    ppermute x4, starting transfers between devices, exchange(): over = lax.ppermute(across, 'gx', border)  22.5 us
    pallas_call x9, Pallas kernels, call(): pl.pallas_call(kernel, out_shape=outs, in_specs=[pl.BlockSpec(memory_spac...  11.6 us
    all_to_all x1, waiting for transfers between devices, exchange(): return (lax.all_to_all(send, 'gy', 0, 0), near, over)  9.29 us
    ppermute x4, waiting for transfers between devices, exchange(): over = lax.ppermute(across, 'gx', border)  7.78 us
    ppermute x4, starting transfers between devices, exchange(): near = lax.ppermute(beside, 'gx', chip)  7.68 us
    all_to_all x1, starting transfers between devices, exchange(): return (lax.all_to_all(send, 'gy', 0, 0), near, over)  7.23 us
  transfers between devices with their start and end apart: 9, of which 6 were waited for; matrix products, arithmetic and copies ran while one was open for 0% of the time, Pallas kernels for 0%

profile of v5, /device:TPU:6, one launch (start us, length us, event | category | flops | bytes accessed | tf_op | source)
XLA Modules:
  0.0 101.6 jit_solution(13869123831211227640)
XLA Ops:
  0.6 2.1 %shard_map.113 = (f32[104,128]{1,0:T(8,128)}, f32[104,128]{1,0:T(8,128)}, f32[32,128]{1,0:T(8,128)}, s32[24,128]{1,0:T(8,128)}, s32[24,128]{1,0:T(8,128)}, /*index=5*/f32[24,128]{1,0:T(8,128)}, f32[24,128]{1,0:T(8,128)}) custom-call(f32[32,512]{1,0:T(8,128)} %refs_0_.1, f32[2,32,512]{2,1,0:T(8,128)} %refs_1_.1, s32[24,128]{1,0:T(8,128)} %cell_in.1, ...), custom_call_target="tpu_custom_call" | custom-call | tf_op jit(solution)/shard_map/pallas_call | solution.py:491
  2.7 14.3 %collective-permute-start = (f32[104,128]{1,0:T(8,128)}, f32[104,128]{1,0:T(8,128)S(1)}, u32[]{:S(2)}, u32[]{:S(2)}) collective-permute-start(f32[104,128]{1,0:T(8,128)} %get-tuple-element.51), channel_id=1, source_target_pairs={{8,16},{24,32},{40,48},{56,64},{72,80},{88,96},{104,112},{120,128}... | collective-permute-start | bytes 159752 | tf_op jit(solution)/shard_map/ppermute | solution.py:529
  17.0 1.9 %collective-permute-start.1 = (f32[104,128]{1,0:T(8,128)}, f32[104,128]{1,0:T(8,128)S(1)}, u32[]{:S(2)}, u32[]{:S(2)}) collective-permute-start(f32[104,128]{1,0:T(8,128)} %get-tuple-element.52), channel_id=1, source_target_pairs={{0,8},{8,0},{16,24},{24,16},{32,40},{40,32},{48,56},{56,48},{64,72... | collective-permute-start | bytes 159752 | tf_op jit(solution)/shard_map/ppermute | solution.py:528
  18.9 0.2 collective-permute-done.over.refs_9_
  19.1 1.3 %collective-permute-done.1.near.refs_8_ = f32[104,128]{1,0:T(8,128)S(1)} collective-permute-done((f32[104,128]{1,0:T(8,128)}, f32[104,128]{1,0:T(8,128)S(1)}, u32[]{:S(2)}, u32[]{:S(2)}) %collective-permute-start.1) | collective-permute-done | bytes 53280 | tf_op jit(solution)/shard_map/ppermute | solution.py:528
  20.3 0.7 copy-done.8
  21.1 0.0 copy-start.7
  21.1 0.7 shard_map.114
  21.8 7.2 %all-to-all-start = ((f32[8,32,128]{2,1,0:T(8,128)}), f32[8,32,128]{2,1,0:T(8,128)S(1)}, u32[]{:S(2)}, u32[]{:S(2)}) async-start(f32[8,32,128]{2,1,0:T(8,128)} %shard_map.114), calls=%async_computation | async-start | bytes 262144 | tf_op jit(solution)/shard_map/all_to_all | solution.py:532
  29.0 0.0 copy-done.11
  29.0 0.1 copy.12.refs_6_.upstream
  29.1 9.3 %all-to-all-done.refs_7_.got_first = f32[8,32,128]{2,1,0:T(8,128)S(1)} async-done(((f32[8,32,128]{2,1,0:T(8,128)}), f32[8,32,128]{2,1,0:T(8,128)S(1)}, u32[]{:S(2)}, u32[]{:S(2)}) %all-to-all-start) | async-done | bytes 131104 | tf_op jit(solution)/shard_map/all_to_all | solution.py:532
  38.4 0.0 copy-done.7
  38.5 1.7 %shard_map.115 = (f32[3,32,512]{2,1,0:T(8,128)S(1)}, f32[8,128]{1,0:T(8,128)S(1)}, f32[24,128]{1,0:T(8,128)S(1)}, f32[24,128]{1,0:T(8,128)S(1)}, f32[40,128]{1,0...) custom-call(f32[32,512]{1,0:T(8,128)S(1)} %copy-done.2, ...), custom_call_target="tpu_custom_call" | custom-call | tf_op jit(solution)/shard_map/pallas_call | solution.py:491
  40.2 3.4 %collective-permute-start.2 = (f32[40,128]{1,0:T(8,128)S(1)}, f32[40,128]{1,0:T(8,128)S(1)}, u32[]{:S(2)}, u32[]{:S(2)}) collective-permute-start(f32[40,128]{1,0:T(8,128)S(1)} %get-tuple-element.67), channel_id=1, source_target_pairs={{8,16},{24,32},{40,48},{56,64},{72,80},{88,96},{104,112},{120,128}... | collective-permute-start | bytes 61448 | tf_op jit(solution)/shard_map/ppermute | solution.py:529
  43.6 1.9 %collective-permute-start.3 = (f32[40,128]{1,0:T(8,128)S(1)}, f32[40,128]{1,0:T(8,128)S(1)}, u32[]{:S(2)}, u32[]{:S(2)}) collective-permute-start(f32[40,128]{1,0:T(8,128)S(1)} %get-tuple-element.68), channel_id=1, source_target_pairs={{0,8},{8,0},{16,24},{24,16},{32,40},{40,32},{48,56},{56,48},{64,72... | collective-permute-start | bytes 61448 | tf_op jit(solution)/shard_map/ppermute | solution.py:528
  45.5 1.9 %collective-permute-done.2.over.refs_8_ = f32[40,128]{1,0:T(8,128)S(1)} collective-permute-done((f32[40,128]{1,0:T(8,128)S(1)}, f32[40,128]{1,0:T(8,128)S(1)}, u32[]{:S(2)}, u32[]{:S(2)}) %collective-permute-start.2) | collective-permute-done | bytes 20512 | tf_op jit(solution)/shard_map/ppermute | solution.py:529
  47.4 0.0 collective-permute-done.3.near.refs_7_
  47.4 10.4 %all_to_all.20.refs_6_ = f32[8,8,128]{2,1,0:T(8,128)S(1)} all-to-all(f32[8,8,128]{2,1,0:T(8,128)S(1)} %shard_map.116), channel_id=1, replica_groups=mesh['gx'=96,'gy'=8] {'gy'}, dimensions={0} | all-to-all | bytes 65536 | tf_op jit(solution)/shard_map/all_to_all | solution.py:532
  57.8 1.6 %shard_map.117 = (f32[3,32,512]{2,1,0:T(8,128)S(1)}, f32[8,128]{1,0:T(8,128)S(1)}, f32[24,128]{1,0:T(8,128)S(1)}, f32[24,128]{1,0:T(8,128)S(1)}, f32[40,128]{1,0...) custom-call(f32[3,32,512]{2,1,0:T(8,128)S(1)} %get-tuple-element.58.refs_0_, ...), custom_call_target="tpu_custom_call" | custom-call | tf_op jit(solution)/shard_map/pallas_call | solution.py:491
  59.5 2.4 %collective-permute-start.4 = (f32[40,128]{1,0:T(8,128)S(1)}, f32[40,128]{1,0:T(8,128)S(1)}, u32[]{:S(2)}, u32[]{:S(2)}) collective-permute-start(f32[40,128]{1,0:T(8,128)S(1)} %get-tuple-element.78), channel_id=1, source_target_pairs={{8,16},{24,32},{40,48},{56,64},{72,80},{88,96},{104,112},{120,128}... | collective-permute-start | bytes 61448 | tf_op jit(solution)/shard_map/ppermute | solution.py:529
  61.9 1.9 %collective-permute-start.5 = (f32[40,128]{1,0:T(8,128)S(1)}, f32[40,128]{1,0:T(8,128)S(1)}, u32[]{:S(2)}, u32[]{:S(2)}) collective-permute-start(f32[40,128]{1,0:T(8,128)S(1)} %get-tuple-element.79), channel_id=1, source_target_pairs={{0,8},{8,0},{16,24},{24,16},{32,40},{40,32},{48,56},{56,48},{64,72... | collective-permute-start | bytes 61448 | tf_op jit(solution)/shard_map/ppermute | solution.py:528
  63.8 2.9 %collective-permute-done.4.over.refs_8_ = f32[40,128]{1,0:T(8,128)S(1)} collective-permute-done((f32[40,128]{1,0:T(8,128)S(1)}, f32[40,128]{1,0:T(8,128)S(1)}, u32[]{:S(2)}, u32[]{:S(2)}) %collective-permute-start.4) | collective-permute-done | bytes 20512 | tf_op jit(solution)/shard_map/ppermute | solution.py:529
  66.7 0.0 collective-permute-done.5.near.refs_7_
  66.7 10.4 %all_to_all.21.refs_6_ = f32[8,8,128]{2,1,0:T(8,128)S(1)} all-to-all(f32[8,8,128]{2,1,0:T(8,128)S(1)} %shard_map.118), channel_id=1, replica_groups=mesh['gx'=96,'gy'=8] {'gy'}, dimensions={0} | all-to-all | bytes 65536 | tf_op jit(solution)/shard_map/all_to_all | solution.py:532
  77.1 2.3 %shard_map.119 = (f32[3,32,512]{2,1,0:T(8,128)S(1)}, f32[8,128]{1,0:T(8,128)}, f32[24,128]{1,0:T(8,128)}, f32[24,128]{1,0:T(8,128)S(1)}, f32[40,128]{1,0:T(8,128...) custom-call(f32[3,32,512]{2,1,0:T(8,128)S(1)} %get-tuple-element.72.refs_0_, ...), custom_call_target="tpu_custom_call" | custom-call | tf_op jit(solution)/shard_map/pallas_call | solution.py:491
  79.4 2.4 %collective-permute-start.6 = (f32[40,128]{1,0:T(8,128)S(1)}, f32[40,128]{1,0:T(8,128)S(1)}, u32[]{:S(2)}, u32[]{:S(2)}) collective-permute-start(f32[40,128]{1,0:T(8,128)S(1)} %get-tuple-element.87), channel_id=1, source_target_pairs={{8,16},{24,32},{40,48},{56,64},{72,80},{88,96},{104,112},{120,128}... | collective-permute-start | bytes 61448 | tf_op jit(solution)/shard_map/ppermute | solution.py:529
  81.8 1.9 %collective-permute-start.7 = (f32[40,128]{1,0:T(8,128)S(1)}, f32[40,128]{1,0:T(8,128)S(1)}, u32[]{:S(2)}, u32[]{:S(2)}) collective-permute-start(f32[40,128]{1,0:T(8,128)S(1)} %get-tuple-element.88), channel_id=1, source_target_pairs={{0,8},{8,0},{16,24},{24,16},{32,40},{40,32},{48,56},{56,48},{64,72... | collective-permute-start | bytes 61448 | tf_op jit(solution)/shard_map/ppermute | solution.py:528
  83.8 2.9 %collective-permute-done.6.over = f32[40,128]{1,0:T(8,128)S(1)} collective-permute-done((f32[40,128]{1,0:T(8,128)S(1)}, f32[40,128]{1,0:T(8,128)S(1)}, u32[]{:S(2)}, u32[]{:S(2)}) %collective-permute-start.6) | collective-permute-done | bytes 20512 | tf_op jit(solution)/shard_map/ppermute | solution.py:529
  86.6 0.0 collective-permute-done.7.near
  86.7 11.8 %all_to_all.22.got = f32[8,40,128]{2,1,0:T(8,128)S(1)} all-to-all(f32[8,40,128]{2,1,0:T(8,128)S(1)} %shard_map.120), channel_id=1, replica_groups=mesh['gx'=96,'gy'=8] {'gy'}, dimensions={0} | all-to-all | bytes 327680 | tf_op jit(solution)/shard_map/all_to_all | solution.py:532
  98.5 3.1 %shard_map.121 = (f32[3,32,512]{2,1,0:T(8,128)}, f32[8,1024]{1,0:T(8,128)}) custom-call(f32[3,32,512]{2,1,0:T(8,128)S(1)} %get-tuple-element.83.state, f32[8,40,128]{2,1,0:T(8,128)S(1)} %all_to_all.22.got, f32[40,128]{1,0:T(8,128)S(1)} %collective-permute-done.7.near, f32[40,128]{1,0:T(8,128)S(1)} %collective-permute-done.6.over, f32[32,512]{1,0:T(8,128)S(1)} %copy-done, ...), custom_call_target="tpu_custom_call" | custom-call | tf_op jit(solution)/shard_map/pallas_call | solution.py:491
  (23 shorter events, 0.1 us)
Async XLA Ops:
  2.7 16.4 %collective-permute-start = (f32[104,128]{1,0:T(8,128)}, f32[104,128]{1,0:T(8,128)S(1)}, u32[]{:S(2)}, u32[]{:S(2)}) collective-permute-start(f32[104,128]{1,0:T(8,128)} %get-tuple-element.51), channel_id=1, source_target_pairs={{8,16},{24,32},{40,48},{56,64},{72,80},{88,96},{104,112},{120,128}... | collective-permute-start | bytes 159752 | tf_op jit(solution)/shard_map/ppermute | solution.py:529
  17.0 3.3 %collective-permute-start.1 = (f32[104,128]{1,0:T(8,128)}, f32[104,128]{1,0:T(8,128)S(1)}, u32[]{:S(2)}, u32[]{:S(2)}) collective-permute-start(f32[104,128]{1,0:T(8,128)} %get-tuple-element.52), channel_id=1, source_target_pairs={{0,8},{8,0},{16,24},{24,16},{32,40},{40,32},{48,56},{56,48},{64,72... | collective-permute-start | bytes 159752 | tf_op jit(solution)/shard_map/ppermute | solution.py:528
  20.3 0.7 copy-start.8
  21.0 8.0 %copy-start.11 = (s32[8,2]{0,1:T(2,128)S(1)}, s32[8,2]{0,1:T(2,128)}, u32[]{:S(2)}) copy-start(s32[8,2]{0,1:T(2,128)} %param.16) | copy-start | bytes 196
  21.0 17.4 %copy-start.4 = (f32[24,128]{1,0:T(8,128)S(1)}, f32[24,128]{1,0:T(8,128)}, u32[]{:S(2)}) copy-start(f32[24,128]{1,0:T(8,128)} %get-tuple-element.56.refs_12_.refs_11_.coeff_ref) | copy-start | bytes 36868
  21.0 17.4 %copy-start.5 = (f32[8,1024]{1,0:T(8,128)S(1)}, f32[8,1024]{1,0:T(8,128)}, u32[]{:S(2)}) copy-start(f32[8,1024]{1,0:T(8,128)} %refs_2_.1) | copy-start | bytes 98308
  21.1 17.4 %copy-start.6 = (f32[8,8]{1,0:T(8,128)S(1)}, f32[8,8]{1,0:T(8,128)}, u32[]{:S(2)}) copy-start(f32[8,8]{1,0:T(8,128)} %celerity.1) | copy-start | bytes 772
  21.1 17.4 %copy-start.7 = (f32[8,8]{1,0:T(8,128)S(1)}, f32[8,8]{1,0:T(8,128)}, u32[]{:S(2)}) copy-start(f32[8,8]{1,0:T(8,128)} %base_inflow.1) | copy-start | bytes 772
  21.1 17.4 %copy-start.9 = (s32[24,128]{1,0:T(8,128)S(1)}, s32[24,128]{1,0:T(8,128)}, u32[]{:S(2)}) copy-start(s32[24,128]{1,0:T(8,128)} %get-tuple-element.47.refs_3_) | copy-start | bytes 36868
  21.1 17.4 %copy-start.10 = (f32[24,128]{1,0:T(8,128)S(1)}, f32[24,128]{1,0:T(8,128)}, u32[]{:S(2)}) copy-start(f32[24,128]{1,0:T(8,128)} %get-tuple-element.57.refs_13_) | copy-start | bytes 36868
  21.8 16.7 %copy-start = (f32[32,512]{1,0:T(8,128)S(1)}, f32[32,512]{1,0:T(8,128)}, u32[]{:S(2)}) copy-start(f32[32,512]{1,0:T(8,128)} %rough.1) | copy-start | bytes 196612
  21.8 16.7 %copy-start.1 = (f32[2,32,512]{2,1,0:T(8,128)S(1)}, f32[2,32,512]{2,1,0:T(8,128)}, u32[]{:S(2)}) copy-start(f32[2,32,512]{2,1,0:T(8,128)} %refs_1_.1) | copy-start | bytes 393220
  21.8 16.7 %copy-start.2 = (f32[32,512]{1,0:T(8,128)S(1)}, f32[32,512]{1,0:T(8,128)}, u32[]{:S(2)}) copy-start(f32[32,512]{1,0:T(8,128)} %refs_0_.1) | copy-start | bytes 196612
  21.8 16.6 %all-to-all-start = ((f32[8,32,128]{2,1,0:T(8,128)}), f32[8,32,128]{2,1,0:T(8,128)S(1)}, u32[]{:S(2)}, u32[]{:S(2)}) async-start(f32[8,32,128]{2,1,0:T(8,128)} %shard_map.114), calls=%async_computation | async-start | bytes 262144 | tf_op jit(solution)/shard_map/all_to_all | solution.py:532
  29.0 9.5 %copy-start.3 = (s32[24,128]{1,0:T(8,128)S(1)}, s32[24,128]{1,0:T(8,128)}, u32[]{:S(2)}) copy-start(s32[24,128]{1,0:T(8,128)} %get-tuple-element.55.refs_11_.refs_10_.cell_ref) | copy-start | bytes 36868
  40.2 7.2 %collective-permute-start.2 = (f32[40,128]{1,0:T(8,128)S(1)}, f32[40,128]{1,0:T(8,128)S(1)}, u32[]{:S(2)}, u32[]{:S(2)}) collective-permute-start(f32[40,128]{1,0:T(8,128)S(1)} %get-tuple-element.67), channel_id=1, source_target_pairs={{8,16},{24,32},{40,48},{56,64},{72,80},{88,96},{104,112},{120,128}... | collective-permute-start | bytes 61448 | tf_op jit(solution)/shard_map/ppermute | solution.py:529
  43.6 3.8 %collective-permute-start.3 = (f32[40,128]{1,0:T(8,128)S(1)}, f32[40,128]{1,0:T(8,128)S(1)}, u32[]{:S(2)}, u32[]{:S(2)}) collective-permute-start(f32[40,128]{1,0:T(8,128)S(1)} %get-tuple-element.68), channel_id=1, source_target_pairs={{0,8},{8,0},{16,24},{24,16},{32,40},{40,32},{48,56},{56,48},{64,72... | collective-permute-start | bytes 61448 | tf_op jit(solution)/shard_map/ppermute | solution.py:528
  59.5 7.2 %collective-permute-start.4 = (f32[40,128]{1,0:T(8,128)S(1)}, f32[40,128]{1,0:T(8,128)S(1)}, u32[]{:S(2)}, u32[]{:S(2)}) collective-permute-start(f32[40,128]{1,0:T(8,128)S(1)} %get-tuple-element.78), channel_id=1, source_target_pairs={{8,16},{24,32},{40,48},{56,64},{72,80},{88,96},{104,112},{120,128}... | collective-permute-start | bytes 61448 | tf_op jit(solution)/shard_map/ppermute | solution.py:529
  61.9 4.8 %collective-permute-start.5 = (f32[40,128]{1,0:T(8,128)S(1)}, f32[40,128]{1,0:T(8,128)S(1)}, u32[]{:S(2)}, u32[]{:S(2)}) collective-permute-start(f32[40,128]{1,0:T(8,128)S(1)} %get-tuple-element.79), channel_id=1, source_target_pairs={{0,8},{8,0},{16,24},{24,16},{32,40},{40,32},{48,56},{56,48},{64,72... | collective-permute-start | bytes 61448 | tf_op jit(solution)/shard_map/ppermute | solution.py:528
  79.4 7.2 %collective-permute-start.6 = (f32[40,128]{1,0:T(8,128)S(1)}, f32[40,128]{1,0:T(8,128)S(1)}, u32[]{:S(2)}, u32[]{:S(2)}) collective-permute-start(f32[40,128]{1,0:T(8,128)S(1)} %get-tuple-element.87), channel_id=1, source_target_pairs={{8,16},{24,32},{40,48},{56,64},{72,80},{88,96},{104,112},{120,128}... | collective-permute-start | bytes 61448 | tf_op jit(solution)/shard_map/ppermute | solution.py:529
  81.8 4.8 %collective-permute-start.7 = (f32[40,128]{1,0:T(8,128)S(1)}, f32[40,128]{1,0:T(8,128)S(1)}, u32[]{:S(2)}, u32[]{:S(2)}) collective-permute-start(f32[40,128]{1,0:T(8,128)S(1)} %get-tuple-element.88), channel_id=1, source_target_pairs={{0,8},{8,0},{16,24},{24,16},{32,40},{40,32},{48,56},{56,48},{64,72... | collective-permute-start | bytes 61448 | tf_op jit(solution)/shard_map/ppermute | solution.py:528

commit v6 on v5

--- a/solution.py
+++ b/solution.py
@@ -68,33 +68,17 @@
     return (p, p * u + pressure, q * u), (q, p * v, q * v + pressure), u, v
 
 
-def flood_update(cells, top, low, left, right, rough, source):
+def flood_base(cells, rough):
     flux_x, flux_y, u, v = flux_terms(cells)
-    top_x = flux_terms(top)[0]
-    low_x = flux_terms(low)[0]
-    left_y = flux_terms(left)[1]
-    right_y = flux_terms(right)[1]
     row = iota((ROWS, COLS), 0)
     col = iota((ROWS, COLS), 1)
     out = []
     for k in range(3):
         quarter = 0.25 * cells[k]
-        from_top = jnp.where(
-            row == 0, 0.25 * top[k] + FACTOR * top_x[k], pltpu.roll(quarter + FACTOR * flux_x[k], 1, 0)
-        )
-        from_low = jnp.where(
-            row == ROWS - 1,
-            0.25 * low[k] - FACTOR * low_x[k],
-            pltpu.roll(quarter - FACTOR * flux_x[k], ROWS - 1, 0),
-        )
-        from_left = jnp.where(
-            col == 0, 0.25 * left[k] + FACTOR * left_y[k], pltpu.roll(quarter + FACTOR * flux_y[k], 1, 1)
-        )
-        from_right = jnp.where(
-            col == COLS - 1,
-            0.25 * right[k] - FACTOR * right_y[k],
-            pltpu.roll(quarter - FACTOR * flux_y[k], COLS - 1, 1),
-        )
+        from_top = jnp.where(row == 0, 0.0, pltpu.roll(quarter + FACTOR * flux_x[k], 1, 0))
+        from_low = jnp.where(row == ROWS - 1, 0.0, pltpu.roll(quarter - FACTOR * flux_x[k], ROWS - 1, 0))
+        from_left = jnp.where(col == 0, 0.0, pltpu.roll(quarter + FACTOR * flux_y[k], 1, 1))
+        from_right = jnp.where(col == COLS - 1, 0.0, pltpu.roll(quarter - FACTOR * flux_y[k], COLS - 1, 1))
         out.append((from_top + from_low) + (from_left + from_right))
     h = cells[0]
     size = jnp.abs(h)
@@ -102,7 +86,30 @@
     root = root * (4.0 - size * (root * root * root)) * (1.0 / 3.0)
     root = jnp.where(h < 0.0, -root, root)
     drag = (GRAV * DT) * rough * rough * jnp.sqrt(u * u + v * v) * root
-    return [out[0] + DT * source, out[1] - drag * u, out[2] - drag * v]
+    return [out[0], out[1] - drag * u, out[2] - drag * v]
+
+
+def flood_finish(base, edges, source):
+    top, low, left, right = edges
+    top_x = flux_terms(top)[0]
+    low_x = flux_terms(low)[0]
+    left_y = flux_terms(left)[1]
+    right_y = flux_terms(right)[1]
+    first_row = iota((8, COLS), 0) == 0
+    last_row = iota((8, COLS), 0) == 7
+    first_col = iota((ROWS, LANES), 1) == 0
+    last_col = iota((ROWS, LANES), 1) == LANES - 1
+    out = []
+    for k in range(3):
+        cells = base[k]
+        upper = cells[0:8] + jnp.where(first_row, 0.25 * top[k] + FACTOR * top_x[k], 0.0)
+        lower = cells[ROWS - 8 : ROWS] + jnp.where(last_row, 0.25 * low[k] - FACTOR * low_x[k], 0.0)
+        cells = jnp.concatenate([upper, cells[8 : ROWS - 8], lower], axis=0)
+        west = cells[:, :LANES] + jnp.where(first_col, 0.25 * left[k] + FACTOR * left_y[k], 0.0)
+        east = cells[:, COLS - LANES :] + jnp.where(last_col, 0.25 * right[k] - FACTOR * right_y[k], 0.0)
+        out.append(jnp.concatenate([west, cells[:, LANES : COLS - LANES], east], axis=1))
+    out[0] = out[0] + DT * source
+    return out
 
 
 def halves(values):
@@ -258,7 +265,21 @@
     return (gx & 1) == 0, lax.axis_index("gy"), gx == 0, gx == lax.axis_size("gx") - 1
 
 
-def first_kernel(
+def first_kernel(*refs):
+    count = len(refs) - 1
+    sources, held, arrived = refs[:6], refs[count - 6 : count], refs[count]
+    copies = [
+        pltpu.make_async_copy(source, target, arrived.at[i])
+        for i, (source, target) in enumerate(zip(sources, held))
+    ]
+    for copy in copies:
+        copy.start()
+    for copy in copies:
+        copy.wait()
+    first_body(*held, *refs[6 : count - 6])
+
+
+def first_body(
     depth,
     discharge,
     cell_in,
@@ -358,21 +379,39 @@
     return river_update(current, inflow_of(own, outlets), own[0:8], lateral)
 
 
-def advance_cells(cells, edges, rough, cell, coeff, segment, slots):
+def advance_cells(base, edges, cell, coeff, segment, slots):
     major, minor = cell_parts(cell)
     rates = coeff * (segment - slots)
     blocks = spread(rates, major, minor, QUADS * ROWS)
     source = jnp.concatenate([blocks[q * ROWS : (q + 1) * ROWS] for q in range(QUADS)], axis=1)
-    return flood_update(cells, *edges, rough, source)
+    return flood_finish([base[0], base[1], base[2]], edges, source)
+
+
+def first_flow(depth, discharge, rough, base):
+    new = flood_base([depth[...], discharge[0], discharge[1]], rough[...])
+    for k in range(3):
+        base[k] = new[k]
+
+
+def flow(state, rough, base):
+    new = flood_base([state[0], state[1], state[2]], rough[...])
+    for k in range(3):
+        base[k] = new[k]
+
+
+def flow_and_total(state, rough, owner_coeff, owner_site, base, total):
+    flow(state, rough, base)
+    site = owner_site[...]
+    total[...] = spread(owner_coeff[...], site >> 7, site & (LANES - 1), FIELDS)
 
 
 def last_kernel(
-    state, got, near, over, rough, cell_ref, coeff_ref, slots_ref, got_first, celerity, base_inflow, upstream, state_out, reach_out
+    state, got, near, over, base, cell_ref, coeff_ref, slots_ref, got_first, celerity, base_inflow, upstream, state_out, reach_out
 ):
     cells = [state[0], state[1], state[2]]
     edges = get_edges(got, near, over, cells, place(), EDGE, 6)
     new = advance_cells(
-        cells, edges, rough[...], cell_ref[...], coeff_ref[...], gathered(got, 3), slots_ref[...]
+        base, edges, cell_ref[...], coeff_ref[...], gathered(got, 3), slots_ref[...]
     )
     for k in range(3):
         state_out[k] = new[k]
@@ -402,7 +441,9 @@
         depth, discharge, reach, site_ref, celerity, base_inflow, upstream = take(7)
     else:
         state, levels, owner_levels, owner_site, owner_coeff, own_ref = take(6)
-    got, near, over, rough, cell_ref, coeff_ref, slots_ref = take(7)
+    got, near, over, base, cell_ref, coeff_ref, slots_ref = take(7)
+    if tail:
+        (total,) = take(1)
     state_out, levels_out, owner_levels_out, slots_out, beside_ref, across_ref, mine_ref = take(7)
     if first:
         owner_site_out, owner_coeff_out, own_out = take(3)
@@ -453,7 +494,7 @@
         current, outlets, own, site_owner, coeff_owner, segment_owner, slots_owner
     )
     edges = get_edges(got, near, over, cells, spot, FIRST_EDGE if first else EDGE, 6)
-    new = advance_cells(cells, edges, rough[...], cell, coeff_ref[...], segment, slots_ref[...])
+    new = advance_cells(base, edges, cell, coeff_ref[...], segment, slots_ref[...])
     for k in range(3):
         state_out[k] = new[k]
     levels_out[...] = levels_next
@@ -480,9 +521,8 @@
     mine_ref[17:18] = right
     put_edges(beside_ref, across_ref, new, even, EDGE)
     if tail:
-        total = spread(coeff_owner, site_owner >> 7, site_owner & (LANES - 1), FIELDS)
         none = jnp.zeros((FIELDS, 1), jnp.float32)
-        mine_ref[24:32] = river_update(levels_next, none, own[0:8], total * levels_next)
+        mine_ref[24:32] = river_update(levels_next, none, own[0:8], total[...] * levels_next)
     else:
         mine_ref[24:32] = blank
 
@@ -523,31 +563,41 @@
     border = [(i, i + 1) for i in range(1, count_x - 1, 2)]
     border = border + [(b, a) for a, b in border]
 
-    def exchange(kernel, rows, beside, across, mine):
+    def exchange(kernel, rows, beside, across, mine, base=None):
         across, beside = lax.optimization_barrier((across, beside))
         near = lax.ppermute(beside, "gx", chip)
         over = lax.ppermute(across, "gx", border)
         over, near = lax.optimization_barrier((over, near))
         send = call(kernel, [f32(BASINS, rows, LANES)], [mine, near, over])[0]
-        return lax.all_to_all(send, "gy", 0, 0), near, over
+        if base is not None:
+            send, base = lax.optimization_barrier((send, base))
+        return lax.all_to_all(send, "gy", 0, 0), near, over, base
 
     table = (SLOT_ROWS, LANES)
-    beside, across, mine, cell, site, coeff, slots = call(
+    outs = [
+        f32(FIRST_SWAP, LANES),
+        f32(FIRST_SWAP, LANES),
+        f32(32, LANES),
+        i32(*table),
+        i32(*table),
+        f32(*table),
+        f32(*table),
+    ]
+    inputs = [depth, discharge, bank_cell, bank_site, bank_coeff, reach_state]
+    inputs = [pltpu.with_memory_space_constraint(x, pltpu.HBM) for x in inputs]
+    beside, across, mine, cell, site, coeff, slots = pl.pallas_call(
         first_kernel,
-        [
-            f32(FIRST_SWAP, LANES),
-            f32(FIRST_SWAP, LANES),
-            f32(32, LANES),
-            i32(*table),
-            i32(*table),
-            f32(*table),
-            f32(*table),
-        ],
-        [depth, discharge, bank_cell, bank_site, bank_coeff, reach_state],
-        limit=60 << 20,
-    )
-    got, near, over = exchange(first_pack, 32, beside, across, mine)
+        out_shape=outs,
+        in_specs=[pl.BlockSpec(memory_space=pltpu.HBM) for _ in inputs],
+        out_specs=[pl.BlockSpec(memory_space=pltpu.VMEM) for _ in outs],
+        scratch_shapes=[pltpu.VMEM(x.shape, x.dtype) for x in inputs]
+        + [pltpu.SemaphoreType.DMA((len(inputs),))],
+        compiler_params=None if INTERPRET else pltpu.CompilerParams(vmem_limit_bytes=16 << 20),
+        interpret=pltpu.InterpretParams() if INTERPRET else False,
+    )(*inputs)
+    got, near, over, _ = exchange(first_pack, 32, beside, across, mine)
     got_first = got
+    base = call(first_flow, [f32(3, ROWS, COLS)], [depth, discharge, roughness])[0]
     for step in range(STEPS - 1):
         first, tail = step == 0, step == STEPS - 2
         outs = [
@@ -564,16 +614,28 @@
             args = [depth, discharge, reach_state, site, celerity, base_inflow, upstream]
         else:
             args = [state, levels, owner_levels, owner_site, owner_coeff, own]
-        args += [got, near, over, roughness, cell, coeff, slots]
+        args += [got, near, over, base, cell, coeff, slots]
+        if tail:
+            args += [total]
         result = call(functools.partial(step_kernel, first, tail), outs, args)
         state, levels, owner_levels, slots, beside, across, mine = result[:7]
         if first:
             owner_site, owner_coeff, own = result[7:10]
-        got, near, over = exchange(last_pack if tail else pack, 40 if tail else 8, beside, across, mine)
+        if first:
+            base, total = call(
+                flow_and_total,
+                [f32(3, ROWS, COLS), f32(FIELDS, LANES)],
+                [state, roughness, owner_coeff, owner_site],
+            )
+        else:
+            base = call(flow, [f32(3, ROWS, COLS)], [state, roughness])[0]
+        got, near, over, base = exchange(
+            last_pack if tail else pack, 40 if tail else BASINS, beside, across, mine, base
+        )
     state, reach = call(
         last_kernel,
         [f32(3, ROWS, COLS), f32(BASINS, FIELDS * LANES)],
-        [state, got, near, over, roughness, cell, coeff, slots, got_first, celerity, base_inflow, upstream],
+        [state, got, near, over, base, cell, coeff, slots, got_first, celerity, base_inflow, upstream],
     )
     return state, reach
 

time: 102 us -> 99.6 us (0.976)
  waiting for transfers between devices: 18.3 us -> 16.9 us
    pallas_call x9 -> x12, Pallas kernels: 11.6 us -> 9.66 us  [call(): pl.pallas_call(kernel, out_shape=outs, in_specs=[pl.BlockSpec(memory_spac...]
    pallas_call x0 -> x1, Pallas kernels: none -> 1.54 us  [per_device(): pl.pallas_call(first_kernel, out_shape=outs, in_specs=[pl.BlockSpec(memor...]
    ppermute x4, waiting for transfers between devices: 7.78 us -> 6.72 us  [exchange(): over = lax.ppermute(across, 'gx', border)]
  transfers between devices with their start and end apart: 9 -> 9, of which waited for: 6 -> 5; matrix products, arithmetic and copies ran while one was open for 0% -> 0% of each run, Pallas kernels for 0% -> 1%
where the time goes in v6:
time: 99.6 us; the launch traced here: 99 us
  starting transfers between devices  37.4 us (38%)
  blocking collectives  32.6 us (33%)
  waiting for transfers between devices  16.9 us (17%)
  Pallas kernels  11.2 us (11%)
    all_to_all x3, blocking collectives, exchange(): return (lax.all_to_all(send, 'gy', 0, 0), near, over, base)  32.6 us
    ppermute x4, starting transfers between devices, exchange(): over = lax.ppermute(across, 'gx', border)  22.5 us
    pallas_call x12, Pallas kernels, call(): pl.pallas_call(kernel, out_shape=outs, in_specs=[pl.BlockSpec(memory_spac...  9.66 us
    all_to_all x1, waiting for transfers between devices, exchange(): return (lax.all_to_all(send, 'gy', 0, 0), near, over, base)  9.02 us
    ppermute x4, starting transfers between devices, exchange(): near = lax.ppermute(beside, 'gx', chip)  7.68 us
    all_to_all x1, starting transfers between devices, exchange(): return (lax.all_to_all(send, 'gy', 0, 0), near, over, base)  7.23 us
    ppermute x4, waiting for transfers between devices, exchange(): over = lax.ppermute(across, 'gx', border)  6.72 us
  transfers between devices with their start and end apart: 9, of which 5 were waited for; matrix products, arithmetic and copies ran while one was open for 0% of the time, Pallas kernels for 1%

profile of v6, /device:TPU:6, one launch (start us, length us, event | category | flops | bytes accessed | tf_op | source)
XLA Modules:
  0.0 99.0 jit_solution(2695943078919972490)
XLA Ops:
  0.6 1.5 %shard_map.113 = (f32[104,128]{1,0:T(8,128)S(1)}, f32[104,128]{1,0:T(8,128)S(1)}, f32[32,128]{1,0:T(8,128)S(1)}, s32[24,128]{1,0:T(8,128)S(1)}, s32[24,128]{1,0:...) custom-call(f32[32,512]{1,0:T(8,128)} %refs_0_.3, f32[2,32,512]{2,1,0:T(8,128)} %refs_1_.3, ...), custom_call_target="tpu_custom_call" | custom-call | tf_op jit(solution)/shard_map/pallas_call | solution.py:588
  2.2 14.3 %collective-permute-start = (f32[104,128]{1,0:T(8,128)S(1)}, f32[104,128]{1,0:T(8,128)S(1)}, u32[]{:S(2)}, u32[]{:S(2)}) collective-permute-start(f32[104,128]{1,0:T(8,128)S(1)} %get-tuple-element.59), channel_id=1, source_target_pairs={{8,16},{24,32},{40,48},{56,64},{72,80},{88,96},{104,112},{120,128}... | collective-permute-start | bytes 159752 | tf_op jit(solution)/shard_map/ppermute | solution.py:569
  16.5 1.9 %collective-permute-start.1 = (f32[104,128]{1,0:T(8,128)S(1)}, f32[104,128]{1,0:T(8,128)S(1)}, u32[]{:S(2)}, u32[]{:S(2)}) collective-permute-start(f32[104,128]{1,0:T(8,128)S(1)} %get-tuple-element.60), channel_id=1, source_target_pairs={{0,8},{8,0},{16,24},{24,16},{32,40},{40,32},{48,56},{56,48},{64,72... | collective-permute-start | bytes 159752 | tf_op jit(solution)/shard_map/ppermute | solution.py:568
  18.4 0.0 collective-permute-done.over.refs_9_
  18.4 1.2 %collective-permute-done.1.near.refs_8_ = f32[104,128]{1,0:T(8,128)S(1)} collective-permute-done((f32[104,128]{1,0:T(8,128)S(1)}, f32[104,128]{1,0:T(8,128)S(1)}, u32[]{:S(2)}, u32[]{:S(2)}) %collective-permute-start.1) | collective-permute-done | bytes 53280 | tf_op jit(solution)/shard_map/ppermute | solution.py:568
  19.6 0.7 shard_map.114
  20.3 7.2 %all-to-all-start = ((f32[8,32,128]{2,1,0:T(8,128)}), f32[8,32,128]{2,1,0:T(8,128)S(1)}, u32[]{:S(2)}, u32[]{:S(2)}) async-start(f32[8,32,128]{2,1,0:T(8,128)} %shard_map.114), calls=%async_computation | async-start | bytes 262144 | tf_op jit(solution)/shard_map/all_to_all | solution.py:574
  27.5 0.1 copy.12.refs_6_.upstream
  27.6 0.0 copy-start.5
  27.7 0.2 shard_map.115.refs_10_
  27.9 0.0 copy-start.4
  27.9 9.0 %all-to-all-done.refs_7_.got_first = f32[8,32,128]{2,1,0:T(8,128)S(1)} async-done(((f32[8,32,128]{2,1,0:T(8,128)}), f32[8,32,128]{2,1,0:T(8,128)S(1)}, u32[]{:S(2)}, u32[]{:S(2)}) %all-to-all-start) | async-done | bytes 131104 | tf_op jit(solution)/shard_map/all_to_all | solution.py:574
  36.9 1.5 %shard_map.116 = (f32[3,32,512]{2,1,0:T(8,128)S(1)}, f32[8,128]{1,0:T(8,128)S(1)}, f32[24,128]{1,0:T(8,128)S(1)}, f32[24,128]{1,0:T(8,128)S(1)}, f32[40,128]{1,0...) custom-call(f32[32,512]{1,0:T(8,128)S(1)} %copy-done.2, ...), custom_call_target="tpu_custom_call" | custom-call | tf_op jit(solution)/shard_map/pallas_call | solution.py:531
  38.4 3.4 %collective-permute-start.2 = (f32[40,128]{1,0:T(8,128)S(1)}, f32[40,128]{1,0:T(8,128)S(1)}, u32[]{:S(2)}, u32[]{:S(2)}) collective-permute-start(f32[40,128]{1,0:T(8,128)S(1)} %get-tuple-element.75), channel_id=1, source_target_pairs={{8,16},{24,32},{40,48},{56,64},{72,80},{88,96},{104,112},{120,128}... | collective-permute-start | bytes 61448 | tf_op jit(solution)/shard_map/ppermute | solution.py:569
  41.8 1.9 %collective-permute-start.3 = (f32[40,128]{1,0:T(8,128)S(1)}, f32[40,128]{1,0:T(8,128)S(1)}, u32[]{:S(2)}, u32[]{:S(2)}) collective-permute-start(f32[40,128]{1,0:T(8,128)S(1)} %get-tuple-element.76), channel_id=1, source_target_pairs={{0,8},{8,0},{16,24},{24,16},{32,40},{40,32},{48,56},{56,48},{64,72... | collective-permute-start | bytes 61448 | tf_op jit(solution)/shard_map/ppermute | solution.py:568
  43.8 0.4 shard_map.118
  44.2 1.5 %collective-permute-done.2.over.refs_8_ = f32[40,128]{1,0:T(8,128)S(1)} collective-permute-done((f32[40,128]{1,0:T(8,128)S(1)}, f32[40,128]{1,0:T(8,128)S(1)}, u32[]{:S(2)}, u32[]{:S(2)}) %collective-permute-start.2) | collective-permute-done | bytes 20512 | tf_op jit(solution)/shard_map/ppermute | solution.py:569
  45.7 0.0 collective-permute-done.3.near.refs_7_
  45.7 10.4 %all_to_all.20.refs_6_ = f32[8,8,128]{2,1,0:T(8,128)S(1)} all-to-all(f32[8,8,128]{2,1,0:T(8,128)S(1)} %shard_map.117), channel_id=1, replica_groups=mesh['gx'=96,'gy'=8] {'gy'}, dimensions={0} | all-to-all | bytes 65536 | tf_op jit(solution)/shard_map/all_to_all | solution.py:574
  56.1 1.4 %shard_map.119 = (f32[3,32,512]{2,1,0:T(8,128)S(1)}, f32[8,128]{1,0:T(8,128)S(1)}, f32[24,128]{1,0:T(8,128)S(1)}, f32[24,128]{1,0:T(8,128)S(1)}, f32[40,128]{1,0...) custom-call(f32[3,32,512]{2,1,0:T(8,128)S(1)} %get-tuple-element.66.state.refs_0_, ...), custom_call_target="tpu_custom_call" | custom-call | tf_op jit(solution)/shard_map/pallas_call | solution.py:531
  57.5 2.4 %collective-permute-start.4 = (f32[40,128]{1,0:T(8,128)S(1)}, f32[40,128]{1,0:T(8,128)S(1)}, u32[]{:S(2)}, u32[]{:S(2)}) collective-permute-start(f32[40,128]{1,0:T(8,128)S(1)} %get-tuple-element.89), channel_id=1, source_target_pairs={{8,16},{24,32},{40,48},{56,64},{72,80},{88,96},{104,112},{120,128}... | collective-permute-start | bytes 61448 | tf_op jit(solution)/shard_map/ppermute | solution.py:569
  59.9 1.9 %collective-permute-start.5 = (f32[40,128]{1,0:T(8,128)S(1)}, f32[40,128]{1,0:T(8,128)S(1)}, u32[]{:S(2)}, u32[]{:S(2)}) collective-permute-start(f32[40,128]{1,0:T(8,128)S(1)} %get-tuple-element.90), channel_id=1, source_target_pairs={{0,8},{8,0},{16,24},{24,16},{32,40},{40,32},{48,56},{56,48},{64,72... | collective-permute-start | bytes 61448 | tf_op jit(solution)/shard_map/ppermute | solution.py:568
  61.9 0.2 shard_map.121.refs_9_
  62.1 2.6 %collective-permute-done.4.over.refs_8_ = f32[40,128]{1,0:T(8,128)S(1)} collective-permute-done((f32[40,128]{1,0:T(8,128)S(1)}, f32[40,128]{1,0:T(8,128)S(1)}, u32[]{:S(2)}, u32[]{:S(2)}) %collective-permute-start.4) | collective-permute-done | bytes 20512 | tf_op jit(solution)/shard_map/ppermute | solution.py:569
  64.8 10.4 %all_to_all.21.refs_6_ = f32[8,8,128]{2,1,0:T(8,128)S(1)} all-to-all(f32[8,8,128]{2,1,0:T(8,128)S(1)} %shard_map.120), channel_id=1, replica_groups=mesh['gx'=96,'gy'=8] {'gy'}, dimensions={0} | all-to-all | bytes 65536 | tf_op jit(solution)/shard_map/all_to_all | solution.py:574
  75.2 1.9 %shard_map.122 = (f32[3,32,512]{2,1,0:T(8,128)S(1)}, f32[8,128]{1,0:T(8,128)}, f32[24,128]{1,0:T(8,128)}, f32[24,128]{1,0:T(8,128)S(1)}, f32[40,128]{1,0:T(8,128...) custom-call(f32[3,32,512]{2,1,0:T(8,128)S(1)} %get-tuple-element.83.state.refs_0_, ...), custom_call_target="tpu_custom_call" | custom-call | tf_op jit(solution)/shard_map/pallas_call | solution.py:531
  77.1 2.4 %collective-permute-start.6 = (f32[40,128]{1,0:T(8,128)S(1)}, f32[40,128]{1,0:T(8,128)S(1)}, u32[]{:S(2)}, u32[]{:S(2)}) collective-permute-start(f32[40,128]{1,0:T(8,128)S(1)} %get-tuple-element.101), channel_id=1, source_target_pairs={{8,16},{24,32},{40,48},{56,64},{72,80},{88,96},{104,112},{120,128}... | collective-permute-start | bytes 61448 | tf_op jit(solution)/shard_map/ppermute | solution.py:569
  79.5 1.9 %collective-permute-start.7 = (f32[40,128]{1,0:T(8,128)S(1)}, f32[40,128]{1,0:T(8,128)S(1)}, u32[]{:S(2)}, u32[]{:S(2)}) collective-permute-start(f32[40,128]{1,0:T(8,128)S(1)} %get-tuple-element.102), channel_id=1, source_target_pairs={{0,8},{8,0},{16,24},{24,16},{32,40},{40,32},{48,56},{56,48},{64,72... | collective-permute-start | bytes 61448 | tf_op jit(solution)/shard_map/ppermute | solution.py:568
  81.4 0.2 shard_map.124.base
  81.7 2.6 %collective-permute-done.6.over = f32[40,128]{1,0:T(8,128)S(1)} collective-permute-done((f32[40,128]{1,0:T(8,128)S(1)}, f32[40,128]{1,0:T(8,128)S(1)}, u32[]{:S(2)}, u32[]{:S(2)}) %collective-permute-start.6) | collective-permute-done | bytes 20512 | tf_op jit(solution)/shard_map/ppermute | solution.py:569
  84.3 11.8 %all_to_all.22.got = f32[8,40,128]{2,1,0:T(8,128)S(1)} all-to-all(f32[8,40,128]{2,1,0:T(8,128)S(1)} %shard_map.123), channel_id=1, replica_groups=mesh['gx'=96,'gy'=8] {'gy'}, dimensions={0} | all-to-all | bytes 327680 | tf_op jit(solution)/shard_map/all_to_all | solution.py:574
  96.2 2.9 %shard_map.125 = (f32[3,32,512]{2,1,0:T(8,128)}, f32[8,1024]{1,0:T(8,128)}) custom-call(f32[3,32,512]{2,1,0:T(8,128)S(1)} %get-tuple-element.97.state, f32[8,40,128]{2,1,0:T(8,128)S(1)} %all_to_all.22.got, f32[40,128]{1,0:T(8,128)S(1)} %collective-permute-done.7.near, f32[40,128]{1,0:T(8,128)S(1)} %collective-permute-done.6.over, ...), custom_call_target="tpu_custom_call" | custom-call | tf_op jit(solution)/shard_map/pallas_call | solution.py:531
  (17 shorter events, 0.1 us)
Async XLA Ops:
  2.2 16.2 %collective-permute-start = (f32[104,128]{1,0:T(8,128)S(1)}, f32[104,128]{1,0:T(8,128)S(1)}, u32[]{:S(2)}, u32[]{:S(2)}) collective-permute-start(f32[104,128]{1,0:T(8,128)S(1)} %get-tuple-element.59), channel_id=1, source_target_pairs={{8,16},{24,32},{40,48},{56,64},{72,80},{88,96},{104,112},{120,128}... | collective-permute-start | bytes 159752 | tf_op jit(solution)/shard_map/ppermute | solution.py:569
  16.5 3.1 %collective-permute-start.1 = (f32[104,128]{1,0:T(8,128)S(1)}, f32[104,128]{1,0:T(8,128)S(1)}, u32[]{:S(2)}, u32[]{:S(2)}) collective-permute-start(f32[104,128]{1,0:T(8,128)S(1)} %get-tuple-element.60), channel_id=1, source_target_pairs={{0,8},{8,0},{16,24},{24,16},{32,40},{40,32},{48,56},{56,48},{64,72... | collective-permute-start | bytes 159752 | tf_op jit(solution)/shard_map/ppermute | solution.py:568
  19.6 7.9 %copy-start.6 = (s32[8,2]{0,1:T(2,128)S(1)}, s32[8,2]{0,1:T(2,128)}, u32[]{:S(2)}) copy-start(s32[8,2]{0,1:T(2,128)} %param.16) | copy-start | bytes 196
  20.3 7.3 %copy-start = (f32[2,32,512]{2,1,0:T(8,128)S(1)}, f32[2,32,512]{2,1,0:T(8,128)}, u32[]{:S(2)}) copy-start(f32[2,32,512]{2,1,0:T(8,128)} %refs_1_.3) | copy-start | bytes 393220
  20.3 7.3 %copy-start.1 = (f32[32,512]{1,0:T(8,128)S(1)}, f32[32,512]{1,0:T(8,128)}, u32[]{:S(2)}) copy-start(f32[32,512]{1,0:T(8,128)} %rough.7) | copy-start | bytes 196612
  20.3 7.3 %copy-start.2 = (f32[32,512]{1,0:T(8,128)S(1)}, f32[32,512]{1,0:T(8,128)}, u32[]{:S(2)}) copy-start(f32[32,512]{1,0:T(8,128)} %refs_0_.3) | copy-start | bytes 196612
  20.3 16.6 %all-to-all-start = ((f32[8,32,128]{2,1,0:T(8,128)}), f32[8,32,128]{2,1,0:T(8,128)S(1)}, u32[]{:S(2)}, u32[]{:S(2)}) async-start(f32[8,32,128]{2,1,0:T(8,128)} %shard_map.114), calls=%async_computation | async-start | bytes 262144 | tf_op jit(solution)/shard_map/all_to_all | solution.py:574
  27.6 9.3 %copy-start.3 = (f32[8,1024]{1,0:T(8,128)S(1)}, f32[8,1024]{1,0:T(8,128)}, u32[]{:S(2)}) copy-start(f32[8,1024]{1,0:T(8,128)} %refs_2_.3) | copy-start | bytes 98308
  27.6 9.3 %copy-start.5 = (f32[8,8]{1,0:T(8,128)S(1)}, f32[8,8]{1,0:T(8,128)}, u32[]{:S(2)}) copy-start(f32[8,8]{1,0:T(8,128)} %base_inflow.1) | copy-start | bytes 772
  27.9 9.0 %copy-start.4 = (f32[8,8]{1,0:T(8,128)S(1)}, f32[8,8]{1,0:T(8,128)}, u32[]{:S(2)}) copy-start(f32[8,8]{1,0:T(8,128)} %celerity.1) | copy-start | bytes 772
  38.4 7.2 %collective-permute-start.2 = (f32[40,128]{1,0:T(8,128)S(1)}, f32[40,128]{1,0:T(8,128)S(1)}, u32[]{:S(2)}, u32[]{:S(2)}) collective-permute-start(f32[40,128]{1,0:T(8,128)S(1)} %get-tuple-element.75), channel_id=1, source_target_pairs={{8,16},{24,32},{40,48},{56,64},{72,80},{88,96},{104,112},{120,128}... | collective-permute-start | bytes 61448 | tf_op jit(solution)/shard_map/ppermute | solution.py:569
  41.8 3.8 %collective-permute-start.3 = (f32[40,128]{1,0:T(8,128)S(1)}, f32[40,128]{1,0:T(8,128)S(1)}, u32[]{:S(2)}, u32[]{:S(2)}) collective-permute-start(f32[40,128]{1,0:T(8,128)S(1)} %get-tuple-element.76), channel_id=1, source_target_pairs={{0,8},{8,0},{16,24},{24,16},{32,40},{40,32},{48,56},{56,48},{64,72... | collective-permute-start | bytes 61448 | tf_op jit(solution)/shard_map/ppermute | solution.py:568
  57.5 7.2 %collective-permute-start.4 = (f32[40,128]{1,0:T(8,128)S(1)}, f32[40,128]{1,0:T(8,128)S(1)}, u32[]{:S(2)}, u32[]{:S(2)}) collective-permute-start(f32[40,128]{1,0:T(8,128)S(1)} %get-tuple-element.89), channel_id=1, source_target_pairs={{8,16},{24,32},{40,48},{56,64},{72,80},{88,96},{104,112},{120,128}... | collective-permute-start | bytes 61448 | tf_op jit(solution)/shard_map/ppermute | solution.py:569
  59.9 4.8 %collective-permute-start.5 = (f32[40,128]{1,0:T(8,128)S(1)}, f32[40,128]{1,0:T(8,128)S(1)}, u32[]{:S(2)}, u32[]{:S(2)}) collective-permute-start(f32[40,128]{1,0:T(8,128)S(1)} %get-tuple-element.90), channel_id=1, source_target_pairs={{0,8},{8,0},{16,24},{24,16},{32,40},{40,32},{48,56},{56,48},{64,72... | collective-permute-start | bytes 61448 | tf_op jit(solution)/shard_map/ppermute | solution.py:568
  77.1 7.2 %collective-permute-start.6 = (f32[40,128]{1,0:T(8,128)S(1)}, f32[40,128]{1,0:T(8,128)S(1)}, u32[]{:S(2)}, u32[]{:S(2)}) collective-permute-start(f32[40,128]{1,0:T(8,128)S(1)} %get-tuple-element.101), channel_id=1, source_target_pairs={{8,16},{24,32},{40,48},{56,64},{72,80},{88,96},{104,112},{120,128}... | collective-permute-start | bytes 61448 | tf_op jit(solution)/shard_map/ppermute | solution.py:569
  79.5 4.8 %collective-permute-start.7 = (f32[40,128]{1,0:T(8,128)S(1)}, f32[40,128]{1,0:T(8,128)S(1)}, u32[]{:S(2)}, u32[]{:S(2)}) collective-permute-start(f32[40,128]{1,0:T(8,128)S(1)} %get-tuple-element.102), channel_id=1, source_target_pairs={{0,8},{8,0},{16,24},{24,16},{32,40},{40,32},{48,56},{56,48},{64,72... | collective-permute-start | bytes 61448 | tf_op jit(solution)/shard_map/ppermute | solution.py:568

commit v7 on v6

--- a/solution.py
+++ b/solution.py
@@ -387,10 +387,12 @@
     return flood_finish([base[0], base[1], base[2]], edges, source)
 
 
-def first_flow(depth, discharge, rough, base):
+def first_flow(depth, discharge, rough, celerity, base_inflow, upstream, base, terms):
     new = flood_base([depth[...], discharge[0], discharge[1]], rough[...])
     for k in range(3):
         base[k] = new[k]
+    for b in range(BASINS):
+        terms[b] = owned_terms(celerity, base_inflow, upstream, b)
 
 
 def flow(state, rough, base):
@@ -406,7 +408,7 @@
 
 
 def last_kernel(
-    state, got, near, over, base, cell_ref, coeff_ref, slots_ref, got_first, celerity, base_inflow, upstream, state_out, reach_out
+    state, got, near, over, base, cell_ref, coeff_ref, slots_ref, got_first, terms, state_out, reach_out, held_state, sent
 ):
     cells = [state[0], state[1], state[2]]
     edges = get_edges(got, near, over, cells, place(), EDGE, 6)
@@ -414,11 +416,13 @@
         base, edges, cell_ref[...], coeff_ref[...], gathered(got, 3), slots_ref[...]
     )
     for k in range(3):
-        state_out[k] = new[k]
+        held_state[k] = new[k]
+    copy = pltpu.make_async_copy(held_state, state_out, sent)
+    copy.start()
     outlets = got[:, 7, :]
     lane = iota((FIELDS, LANES), 1)
     for b in range(BASINS):
-        own = owned_terms(celerity, base_inflow, upstream, b)
+        own = terms[b]
         site = jnp.concatenate([got_first[:, 8 + 8 * v + b, :] for v in range(3)], axis=0)
         site = site.astype(jnp.int32)
         held = jnp.concatenate([got[:, 8 + 8 * v + b, :] for v in range(3)], axis=0)
@@ -427,6 +431,7 @@
         level = got[b, 32:40, :] + entering + (DT * RATIO) * drawn
         for f in range(FIELDS):
             reach_out[b : b + 1, f * LANES : (f + 1) * LANES] = level[f : f + 1]
+    copy.wait()
 
 
 def step_kernel(first, tail, *refs):
@@ -438,13 +443,15 @@
         return taken
 
     if first:
-        depth, discharge, reach, site_ref, celerity, base_inflow, upstream = take(7)
+        depth, discharge, reach, site_ref, terms = take(5)
     else:
         state, levels, owner_levels, owner_site, owner_coeff, own_ref = take(6)
     got, near, over, base, cell_ref, coeff_ref, slots_ref = take(7)
     if tail:
         (total,) = take(1)
-    state_out, levels_out, owner_levels_out, slots_out, beside_ref, across_ref, mine_ref = take(7)
+    state_out, slots_out, beside_ref, across_ref, mine_ref = take(5)
+    if not tail:
+        levels_out, owner_levels_out = take(2)
     if first:
         owner_site_out, owner_coeff_out, own_out = take(3)
     spot = place()
@@ -476,7 +483,7 @@
         segment_owner = level_at_sites(
             lambda f, v: jnp.broadcast_to(current[f : f + 1], (8, LANES)), site_owner
         )
-        own = owned_terms(celerity, base_inflow, upstream, y)
+        own = terms[y]
         owner_site_out[...] = site_owner
         owner_coeff_out[...] = coeff_owner
         own_out[...] = own
@@ -497,11 +504,12 @@
     new = advance_cells(base, edges, cell, coeff_ref[...], segment, slots_ref[...])
     for k in range(3):
         state_out[k] = new[k]
-    levels_out[...] = levels_next
     owned = level_at_sites(
         lambda f, v: jnp.broadcast_to(levels_next[f : f + 1], (8, LANES)), site_owner
     )
-    owner_levels_out[...] = owned
+    if not tail:
+        levels_out[...] = levels_next
+        owner_levels_out[...] = owned
     slots = depth_at_slots(state_out, (0,), cell)
     slots_out[...] = slots
     if tail:
@@ -563,15 +571,14 @@
     border = [(i, i + 1) for i in range(1, count_x - 1, 2)]
     border = border + [(b, a) for a, b in border]
 
-    def exchange(kernel, rows, beside, across, mine, base=None):
+    def exchange(kernel, rows, beside, across, mine, ready):
         across, beside = lax.optimization_barrier((across, beside))
         near = lax.ppermute(beside, "gx", chip)
         over = lax.ppermute(across, "gx", border)
         over, near = lax.optimization_barrier((over, near))
         send = call(kernel, [f32(BASINS, rows, LANES)], [mine, near, over])[0]
-        if base is not None:
-            send, base = lax.optimization_barrier((send, base))
-        return lax.all_to_all(send, "gy", 0, 0), near, over, base
+        send, ready = lax.optimization_barrier((send, ready))
+        return lax.all_to_all(send, "gy", 0, 0), near, over, ready
 
     table = (SLOT_ROWS, LANES)
     outs = [
@@ -595,30 +602,36 @@
         compiler_params=None if INTERPRET else pltpu.CompilerParams(vmem_limit_bytes=16 << 20),
         interpret=pltpu.InterpretParams() if INTERPRET else False,
     )(*inputs)
-    got, near, over, _ = exchange(first_pack, 32, beside, across, mine)
+    base, terms = call(
+        first_flow,
+        [f32(3, ROWS, COLS), f32(BASINS, 24, LANES)],
+        [depth, discharge, roughness, celerity, base_inflow, upstream],
+    )
+    got, near, over, (base, terms) = exchange(first_pack, 32, beside, across, mine, (base, terms))
     got_first = got
-    base = call(first_flow, [f32(3, ROWS, COLS)], [depth, discharge, roughness])[0]
     for step in range(STEPS - 1):
         first, tail = step == 0, step == STEPS - 2
         outs = [
             f32(3, ROWS, COLS),
-            f32(FIELDS, LANES),
-            f32(*table),
             f32(*table),
             f32(SWAP, LANES),
             f32(SWAP, LANES),
             f32(32, LANES),
         ]
+        if not tail:
+            outs += [f32(FIELDS, LANES), f32(*table)]
         if first:
             outs += [i32(*table), f32(*table), f32(*table)]
-            args = [depth, discharge, reach_state, site, celerity, base_inflow, upstream]
+            args = [depth, discharge, reach_state, site, terms]
         else:
             args = [state, levels, owner_levels, owner_site, owner_coeff, own]
         args += [got, near, over, base, cell, coeff, slots]
         if tail:
             args += [total]
         result = call(functools.partial(step_kernel, first, tail), outs, args)
-        state, levels, owner_levels, slots, beside, across, mine = result[:7]
+        state, slots, beside, across, mine = result[:5]
+        if not tail:
+            levels, owner_levels = result[5:7]
         if first:
             owner_site, owner_coeff, own = result[7:10]
         if first:
@@ -632,11 +645,16 @@
         got, near, over, base = exchange(
             last_pack if tail else pack, 40 if tail else BASINS, beside, across, mine, base
         )
-    state, reach = call(
+    inputs = [state, got, near, over, base, cell, coeff, slots, got_first, terms]
+    state, reach = pl.pallas_call(
         last_kernel,
-        [f32(3, ROWS, COLS), f32(BASINS, FIELDS * LANES)],
-        [state, got, near, over, base, cell, coeff, slots, got_first, celerity, base_inflow, upstream],
-    )
+        out_shape=[f32(3, ROWS, COLS), f32(BASINS, FIELDS * LANES)],
+        in_specs=[pl.BlockSpec(memory_space=pltpu.VMEM) for _ in inputs],
+        out_specs=[pl.BlockSpec(memory_space=pl.ANY), pl.BlockSpec(memory_space=pltpu.VMEM)],
+        scratch_shapes=[pltpu.VMEM((3, ROWS, COLS), jnp.float32), pltpu.SemaphoreType.DMA],
+        compiler_params=None if INTERPRET else pltpu.CompilerParams(vmem_limit_bytes=16 << 20),
+        interpret=pltpu.InterpretParams() if INTERPRET else False,
+    )(*inputs)
     return state, reach
 
 

time: 99.6 us -> 98.7 us (level)
  blocking collectives: 32.6 us -> 48.9 us
  waiting for transfers between devices: 16.9 us -> 7.5 us
  starting transfers between devices: 37.4 us -> 30.2 us
    all_to_all x3 -> x4, blocking collectives: 32.6 us -> 48.9 us  [exchange(): return (lax.all_to_all(send, 'gy', 0, 0), near, over, ready)]
    all_to_all x1 -> x0, waiting for transfers between devices: 9.02 us -> none  [exchange(): return (lax.all_to_all(send, 'gy', 0, 0), near, over, base)]
    all_to_all x1 -> x0, starting transfers between devices: 7.23 us -> none  [exchange(): return (lax.all_to_all(send, 'gy', 0, 0), near, over, base)]
    pallas_call x12 -> x11, Pallas kernels: 9.66 us -> 5.69 us  [call(): pl.pallas_call(kernel, out_shape=outs, in_specs=[pl.BlockSpec(memory_spac...]
    pallas_call x0 -> x1, Pallas kernels: none -> 3.42 us  [per_device(): pl.pallas_call(last_kernel, out_shape=[f32(3, ROWS, COLS), f32(BASINS, FI...]
  transfers between devices with their start and end apart: 9 -> 8, of which waited for: 5 -> 4; matrix products, arithmetic and copies ran while one was open for 0% -> 0% of each run, Pallas kernels for 1% -> 1%
where the time goes in v7:
time: 98.7 us; the launch traced here: 98.2 us
  blocking collectives  48.9 us (50%)
  starting transfers between devices  30.2 us (31%)
  Pallas kernels  10.7 us (11%)
  waiting for transfers between devices  7.5 us (8%)
    all_to_all x4, blocking collectives, exchange(): return (lax.all_to_all(send, 'gy', 0, 0), near, over, ready)  48.9 us
    ppermute x4, starting transfers between devices, exchange(): over = lax.ppermute(across, 'gx', border)  22.5 us
    ppermute x4, starting transfers between devices, exchange(): near = lax.ppermute(beside, 'gx', chip)  7.68 us
    ppermute x4, waiting for transfers between devices, exchange(): over = lax.ppermute(across, 'gx', border)  6.72 us
    pallas_call x11, Pallas kernels, call(): pl.pallas_call(kernel, out_shape=outs, in_specs=[pl.BlockSpec(memory_spac...  5.69 us
    pallas_call x1, Pallas kernels, per_device(): pl.pallas_call(last_kernel, out_shape=[f32(3, ROWS, COLS), f32(BASINS, FI...  3.42 us
  transfers between devices with their start and end apart: 8, of which 4 were waited for; matrix products, arithmetic and copies ran while one was open for 0% of the time, Pallas kernels for 1%

profile of v7, /device:TPU:6, one launch (start us, length us, event | category | flops | bytes accessed | tf_op | source)
XLA Modules:
  0.0 98.2 jit_solution(14086444778864057430)
XLA Ops:
  0.7 1.6 %shard_map.113 = (f32[104,128]{1,0:T(8,128)S(1)}, f32[104,128]{1,0:T(8,128)S(1)}, f32[32,128]{1,0:T(8,128)S(1)}, s32[24,128]{1,0:T(8,128)S(1)}, s32[24,128]{1,0:...) custom-call(f32[32,512]{1,0:T(8,128)} %refs_0_.3, f32[2,32,512]{2,1,0:T(8,128)} %refs_1_.3, ...), custom_call_target="tpu_custom_call" | custom-call | tf_op jit(solution)/shard_map/pallas_call | solution.py:595
  2.3 0.0 copy-start.4
  2.3 0.0 copy-start.5
  2.3 14.3 %collective-permute-start = (f32[104,128]{1,0:T(8,128)S(1)}, f32[104,128]{1,0:T(8,128)S(1)}, u32[]{:S(2)}, u32[]{:S(2)}) collective-permute-start(f32[104,128]{1,0:T(8,128)S(1)} %get-tuple-element.64), channel_id=1, source_target_pairs={{8,16},{24,32},{40,48},{56,64},{72,80},{88,96},{104,112},{120,128}... | collective-permute-start | bytes 159752 | tf_op jit(solution)/shard_map/ppermute | solution.py:577
  16.6 1.9 %collective-permute-start.1 = (f32[104,128]{1,0:T(8,128)S(1)}, f32[104,128]{1,0:T(8,128)S(1)}, u32[]{:S(2)}, u32[]{:S(2)}) collective-permute-start(f32[104,128]{1,0:T(8,128)S(1)} %get-tuple-element.65), channel_id=1, source_target_pairs={{0,8},{8,0},{16,24},{24,16},{32,40},{40,32},{48,56},{56,48},{64,72... | collective-permute-start | bytes 159752 | tf_op jit(solution)/shard_map/ppermute | solution.py:576
  18.5 0.1 copy.12.upstream
  18.6 0.3 shard_map.115
  19.0 0.0 collective-permute-done.over.refs_7_
  19.0 0.8 collective-permute-done.1.near.refs_6_
  19.8 0.0 copy-start.3
  19.8 16.3 %all_to_all.20.refs_5_.got_first = f32[8,32,128]{2,1,0:T(8,128)S(1)} all-to-all(f32[8,32,128]{2,1,0:T(8,128)S(1)} %shard_map.114), channel_id=1, replica_groups=mesh['gx'=96,'gy'=8] {'gy'}, dimensions={0} | all-to-all | bytes 262144 | tf_op jit(solution)/shard_map/all_to_all | solution.py:581
  36.1 1.5 %shard_map.116 = (f32[3,32,512]{2,1,0:T(8,128)S(1)}, f32[24,128]{1,0:T(8,128)S(1)}, f32[40,128]{1,0:T(8,128)S(1)}, f32[40,128]{1,0:T(8,128)S(1)}, f32[32,128]{1,...) custom-call(f32[32,512]{1,0:T(8,128)S(1)} %copy-done.2, ...), custom_call_target="tpu_custom_call" | custom-call | tf_op jit(solution)/shard_map/pallas_call | solution.py:539
  37.6 3.4 %collective-permute-start.2 = (f32[40,128]{1,0:T(8,128)S(1)}, f32[40,128]{1,0:T(8,128)S(1)}, u32[]{:S(2)}, u32[]{:S(2)}) collective-permute-start(f32[40,128]{1,0:T(8,128)S(1)} %get-tuple-element.85), channel_id=1, source_target_pairs={{8,16},{24,32},{40,48},{56,64},{72,80},{88,96},{104,112},{120,128}... | collective-permute-start | bytes 61448 | tf_op jit(solution)/shard_map/ppermute | solution.py:577
  41.0 1.9 %collective-permute-start.3 = (f32[40,128]{1,0:T(8,128)S(1)}, f32[40,128]{1,0:T(8,128)S(1)}, u32[]{:S(2)}, u32[]{:S(2)}) collective-permute-start(f32[40,128]{1,0:T(8,128)S(1)} %get-tuple-element.86), channel_id=1, source_target_pairs={{0,8},{8,0},{16,24},{24,16},{32,40},{40,32},{48,56},{56,48},{64,72... | collective-permute-start | bytes 61448 | tf_op jit(solution)/shard_map/ppermute | solution.py:576
  42.9 0.4 shard_map.118
  43.3 1.5 %collective-permute-done.2.over.refs_8_ = f32[40,128]{1,0:T(8,128)S(1)} collective-permute-done((f32[40,128]{1,0:T(8,128)S(1)}, f32[40,128]{1,0:T(8,128)S(1)}, u32[]{:S(2)}, u32[]{:S(2)}) %collective-permute-start.2) | collective-permute-done | bytes 20512 | tf_op jit(solution)/shard_map/ppermute | solution.py:577
  44.8 10.4 %all_to_all.21.refs_6_ = f32[8,8,128]{2,1,0:T(8,128)S(1)} all-to-all(f32[8,8,128]{2,1,0:T(8,128)S(1)} %shard_map.117), channel_id=1, replica_groups=mesh['gx'=96,'gy'=8] {'gy'}, dimensions={0} | all-to-all | bytes 65536 | tf_op jit(solution)/shard_map/all_to_all | solution.py:581
  55.2 1.4 %shard_map.119 = (f32[3,32,512]{2,1,0:T(8,128)S(1)}, f32[24,128]{1,0:T(8,128)S(1)}, f32[40,128]{1,0:T(8,128)S(1)}, f32[40,128]{1,0:T(8,128)S(1)}, f32[32,128]{1,...) custom-call(f32[3,32,512]{2,1,0:T(8,128)S(1)} %get-tuple-element.76.state.refs_0_, ...), custom_call_target="tpu_custom_call" | custom-call | tf_op jit(solution)/shard_map/pallas_call | solution.py:539
  56.6 2.4 %collective-permute-start.4 = (f32[40,128]{1,0:T(8,128)S(1)}, f32[40,128]{1,0:T(8,128)S(1)}, u32[]{:S(2)}, u32[]{:S(2)}) collective-permute-start(f32[40,128]{1,0:T(8,128)S(1)} %get-tuple-element.99), channel_id=1, source_target_pairs={{8,16},{24,32},{40,48},{56,64},{72,80},{88,96},{104,112},{120,128}... | collective-permute-start | bytes 61448 | tf_op jit(solution)/shard_map/ppermute | solution.py:577
  59.1 1.9 %collective-permute-start.5 = (f32[40,128]{1,0:T(8,128)S(1)}, f32[40,128]{1,0:T(8,128)S(1)}, u32[]{:S(2)}, u32[]{:S(2)}) collective-permute-start(f32[40,128]{1,0:T(8,128)S(1)} %get-tuple-element.100), channel_id=1, source_target_pairs={{0,8},{8,0},{16,24},{24,16},{32,40},{40,32},{48,56},{56,48},{64,72... | collective-permute-start | bytes 61448 | tf_op jit(solution)/shard_map/ppermute | solution.py:576
  61.0 0.2 shard_map.121.refs_9_
  61.2 2.6 %collective-permute-done.4.over.refs_8_ = f32[40,128]{1,0:T(8,128)S(1)} collective-permute-done((f32[40,128]{1,0:T(8,128)S(1)}, f32[40,128]{1,0:T(8,128)S(1)}, u32[]{:S(2)}, u32[]{:S(2)}) %collective-permute-start.4) | collective-permute-done | bytes 20512 | tf_op jit(solution)/shard_map/ppermute | solution.py:577
  63.9 0.0 collective-permute-done.5.near.refs_7_
  63.9 10.4 %all_to_all.22.refs_6_ = f32[8,8,128]{2,1,0:T(8,128)S(1)} all-to-all(f32[8,8,128]{2,1,0:T(8,128)S(1)} %shard_map.120), channel_id=1, replica_groups=mesh['gx'=96,'gy'=8] {'gy'}, dimensions={0} | all-to-all | bytes 65536 | tf_op jit(solution)/shard_map/all_to_all | solution.py:581
  74.3 1.4 %shard_map.122 = (f32[3,32,512]{2,1,0:T(8,128)S(1)}, f32[24,128]{1,0:T(8,128)S(1)}, f32[40,128]{1,0:T(8,128)S(1)}, f32[40,128]{1,0:T(8,128)S(1)}, f32[32,128]{1,0:T(8,128)S(1)}) custom-call(f32[3,32,512]{2,1,0:T(8,128)S(1)} %get-tuple-element.93.state.refs_0_, f32[8,128]{1,0:T(8,128)S(1)} %get-tuple-element.94.refs_1_, ...), custom_call_target="tpu_custom_call" | custom-call | tf_op jit(solution)/shard_map/pallas_call | solution.py:539
  75.7 2.4 %collective-permute-start.6 = (f32[40,128]{1,0:T(8,128)S(1)}, f32[40,128]{1,0:T(8,128)S(1)}, u32[]{:S(2)}, u32[]{:S(2)}) collective-permute-start(f32[40,128]{1,0:T(8,128)S(1)} %get-tuple-element.111), channel_id=1, source_target_pairs={{8,16},{24,32},{40,48},{56,64},{72,80},{88,96},{104,112},{120,128}... | collective-permute-start | bytes 61448 | tf_op jit(solution)/shard_map/ppermute | solution.py:577
  78.1 1.9 %collective-permute-start.7 = (f32[40,128]{1,0:T(8,128)S(1)}, f32[40,128]{1,0:T(8,128)S(1)}, u32[]{:S(2)}, u32[]{:S(2)}) collective-permute-start(f32[40,128]{1,0:T(8,128)S(1)} %get-tuple-element.112), channel_id=1, source_target_pairs={{0,8},{8,0},{16,24},{24,16},{32,40},{40,32},{48,56},{56,48},{64,72... | collective-permute-start | bytes 61448 | tf_op jit(solution)/shard_map/ppermute | solution.py:576
  80.1 0.2 shard_map.124.base
  80.3 2.6 %collective-permute-done.6.over = f32[40,128]{1,0:T(8,128)S(1)} collective-permute-done((f32[40,128]{1,0:T(8,128)S(1)}, f32[40,128]{1,0:T(8,128)S(1)}, u32[]{:S(2)}, u32[]{:S(2)}) %collective-permute-start.6) | collective-permute-done | bytes 20512 | tf_op jit(solution)/shard_map/ppermute | solution.py:577
  82.9 0.0 collective-permute-done.7.near
  83.0 11.8 %all_to_all.23.got = f32[8,40,128]{2,1,0:T(8,128)S(1)} all-to-all(f32[8,40,128]{2,1,0:T(8,128)S(1)} %shard_map.123), channel_id=1, replica_groups=mesh['gx'=96,'gy'=8] {'gy'}, dimensions={0} | all-to-all | bytes 327680 | tf_op jit(solution)/shard_map/all_to_all | solution.py:581
  94.8 3.4 %shard_map.125 = (f32[3,32,512]{2,1,0:T(8,128)}, f32[8,1024]{1,0:T(8,128)}) custom-call(f32[3,32,512]{2,1,0:T(8,128)S(1)} %get-tuple-element.107.state, f32[8,40,128]{2,1,0:T(8,128)S(1)} %all_to_all.23.got, f32[40,128]{1,0:T(8,128)S(1)} %collective-permute-done.7.near, f32[40,128]{1,0:T(8,128)S(1)} %collective-permute-done.6.over, ...), custom_call_target="tpu_custom_call" | custom-call | tf_op jit(solution)/shard_map/pallas_call | solution.py:649
  (16 shorter events, 0.2 us)
Async XLA Ops:
  0.6 18.0 %copy-start = (f32[2,32,512]{2,1,0:T(8,128)S(1)}, f32[2,32,512]{2,1,0:T(8,128)}, u32[]{:S(2)}) copy-start(f32[2,32,512]{2,1,0:T(8,128)} %refs_1_.3) | copy-start | bytes 393220
  0.6 18.0 %copy-start.2 = (f32[32,512]{1,0:T(8,128)S(1)}, f32[32,512]{1,0:T(8,128)}, u32[]{:S(2)}) copy-start(f32[32,512]{1,0:T(8,128)} %refs_0_.3) | copy-start | bytes 196612
  0.7 18.0 %copy-start.1 = (f32[32,512]{1,0:T(8,128)S(1)}, f32[32,512]{1,0:T(8,128)}, u32[]{:S(2)}) copy-start(f32[32,512]{1,0:T(8,128)} %rough.7) | copy-start | bytes 196612
  0.7 17.9 %copy-start.6 = (s32[8,2]{0,1:T(2,128)S(1)}, s32[8,2]{0,1:T(2,128)}, u32[]{:S(2)}) copy-start(s32[8,2]{0,1:T(2,128)} %param.16) | copy-start | bytes 196
  2.3 16.4 %copy-start.4 = (f32[8,8]{1,0:T(8,128)S(1)}, f32[8,8]{1,0:T(8,128)}, u32[]{:S(2)}) copy-start(f32[8,8]{1,0:T(8,128)} %celerity.1) | copy-start | bytes 772
  2.3 16.3 %copy-start.5 = (f32[8,8]{1,0:T(8,128)S(1)}, f32[8,8]{1,0:T(8,128)}, u32[]{:S(2)}) copy-start(f32[8,8]{1,0:T(8,128)} %base_inflow.1) | copy-start | bytes 772
  2.3 16.7 %collective-permute-start = (f32[104,128]{1,0:T(8,128)S(1)}, f32[104,128]{1,0:T(8,128)S(1)}, u32[]{:S(2)}, u32[]{:S(2)}) collective-permute-start(f32[104,128]{1,0:T(8,128)S(1)} %get-tuple-element.64), channel_id=1, source_target_pairs={{8,16},{24,32},{40,48},{56,64},{72,80},{88,96},{104,112},{120,128}... | collective-permute-start | bytes 159752 | tf_op jit(solution)/shard_map/ppermute | solution.py:577
  16.6 3.1 %collective-permute-start.1 = (f32[104,128]{1,0:T(8,128)S(1)}, f32[104,128]{1,0:T(8,128)S(1)}, u32[]{:S(2)}, u32[]{:S(2)}) collective-permute-start(f32[104,128]{1,0:T(8,128)S(1)} %get-tuple-element.65), channel_id=1, source_target_pairs={{0,8},{8,0},{16,24},{24,16},{32,40},{40,32},{48,56},{56,48},{64,72... | collective-permute-start | bytes 159752 | tf_op jit(solution)/shard_map/ppermute | solution.py:576
  19.8 16.3 %copy-start.3 = (f32[8,1024]{1,0:T(8,128)S(1)}, f32[8,1024]{1,0:T(8,128)}, u32[]{:S(2)}) copy-start(f32[8,1024]{1,0:T(8,128)} %refs_2_.3) | copy-start | bytes 98308
  37.6 7.2 %collective-permute-start.2 = (f32[40,128]{1,0:T(8,128)S(1)}, f32[40,128]{1,0:T(8,128)S(1)}, u32[]{:S(2)}, u32[]{:S(2)}) collective-permute-start(f32[40,128]{1,0:T(8,128)S(1)} %get-tuple-element.85), channel_id=1, source_target_pairs={{8,16},{24,32},{40,48},{56,64},{72,80},{88,96},{104,112},{120,128}... | collective-permute-start | bytes 61448 | tf_op jit(solution)/shard_map/ppermute | solution.py:577
  41.0 3.8 %collective-permute-start.3 = (f32[40,128]{1,0:T(8,128)S(1)}, f32[40,128]{1,0:T(8,128)S(1)}, u32[]{:S(2)}, u32[]{:S(2)}) collective-permute-start(f32[40,128]{1,0:T(8,128)S(1)} %get-tuple-element.86), channel_id=1, source_target_pairs={{0,8},{8,0},{16,24},{24,16},{32,40},{40,32},{48,56},{56,48},{64,72... | collective-permute-start | bytes 61448 | tf_op jit(solution)/shard_map/ppermute | solution.py:576
  56.6 7.2 %collective-permute-start.4 = (f32[40,128]{1,0:T(8,128)S(1)}, f32[40,128]{1,0:T(8,128)S(1)}, u32[]{:S(2)}, u32[]{:S(2)}) collective-permute-start(f32[40,128]{1,0:T(8,128)S(1)} %get-tuple-element.99), channel_id=1, source_target_pairs={{8,16},{24,32},{40,48},{56,64},{72,80},{88,96},{104,112},{120,128}... | collective-permute-start | bytes 61448 | tf_op jit(solution)/shard_map/ppermute | solution.py:577
  59.1 4.8 %collective-permute-start.5 = (f32[40,128]{1,0:T(8,128)S(1)}, f32[40,128]{1,0:T(8,128)S(1)}, u32[]{:S(2)}, u32[]{:S(2)}) collective-permute-start(f32[40,128]{1,0:T(8,128)S(1)} %get-tuple-element.100), channel_id=1, source_target_pairs={{0,8},{8,0},{16,24},{24,16},{32,40},{40,32},{48,56},{56,48},{64,72... | collective-permute-start | bytes 61448 | tf_op jit(solution)/shard_map/ppermute | solution.py:576
  75.7 7.2 %collective-permute-start.6 = (f32[40,128]{1,0:T(8,128)S(1)}, f32[40,128]{1,0:T(8,128)S(1)}, u32[]{:S(2)}, u32[]{:S(2)}) collective-permute-start(f32[40,128]{1,0:T(8,128)S(1)} %get-tuple-element.111), channel_id=1, source_target_pairs={{8,16},{24,32},{40,48},{56,64},{72,80},{88,96},{104,112},{120,128}... | collective-permute-start | bytes 61448 | tf_op jit(solution)/shard_map/ppermute | solution.py:577
  78.1 4.8 %collective-permute-start.7 = (f32[40,128]{1,0:T(8,128)S(1)}, f32[40,128]{1,0:T(8,128)S(1)}, u32[]{:S(2)}, u32[]{:S(2)}) collective-permute-start(f32[40,128]{1,0:T(8,128)S(1)} %get-tuple-element.112), channel_id=1, source_target_pairs={{0,8},{8,0},{16,24},{24,16},{32,40},{40,32},{48,56},{56,48},{64,72... | collective-permute-start | bytes 61448 | tf_op jit(solution)/shard_map/ppermute | solution.py:576

commit v8 on v7

--- a/solution.py
+++ b/solution.py
@@ -148,6 +148,40 @@
     return total[:count] + total[count:]
 
 
+def repeated(row, count):
+    tile = jnp.broadcast_to(row, (16, LANES)).astype(jnp.bfloat16)
+    return jnp.concatenate([tile] * (count // 16), axis=0)
+
+
+def spread_cells(rates, major, minor):
+    high, low = halves(rates)
+    major = major.astype(jnp.float32)
+    minor = minor.astype(jnp.float32)
+    row = iota((LANES, LANES), 0).astype(jnp.float32).astype(jnp.bfloat16)
+    zero = jnp.zeros((), jnp.bfloat16)
+    one = jnp.ones((), jnp.bfloat16)
+    total = None
+    group = 4
+    for start in range(0, rates.shape[0], group):
+        left, right = [], []
+        for r in range(start, start + group):
+            at = row == repeated(major[r : r + 1], LANES)
+            left.append(
+                jnp.concatenate(
+                    [jnp.where(at, repeated(part[r : r + 1], LANES), zero) for part in (high, low)], axis=0
+                )
+            )
+            right.append(jnp.where(row == repeated(minor[r : r + 1], LANES), one, zero))
+        part = lax.dot_general(
+            jnp.concatenate(left, axis=1),
+            jnp.concatenate(right, axis=1),
+            (((1,), (1,)), ((), ())),
+            preferred_element_type=jnp.float32,
+        )
+        total = part if total is None else total + part
+    return total[:LANES] + total[LANES:]
+
+
 def cell_parts(cell):
     col = cell & (COLS - 1)
     return (col >> 7) * ROWS + (cell >> 9), col & (LANES - 1)
@@ -274,12 +308,11 @@
     ]
     for copy in copies:
         copy.start()
-    for copy in copies:
-        copy.wait()
-    first_body(*held, *refs[6 : count - 6])
+    first_body(copies, *held, *refs[6 : count - 6])
 
 
 def first_body(
+    copies,
     depth,
     discharge,
     cell_in,
@@ -300,15 +333,19 @@
         low, own, high = ref[0:8], ref[8:16], ref[16:24]
         return jnp.concatenate([own, jnp.where(even, high, low), jnp.where(even, low, high)], axis=0)
 
-    cell = arranged(cell_in)
+    copies[0].wait()
+    copies[2].wait()
+    bank = arranged(cell_in)
+    cell = jnp.maximum(bank, 0)
+    cell_ref[...] = cell
+    slots = depth_at_slots(depth, (), cell)
+    slots_ref[...] = slots
+    for i in (1, 3, 4, 5):
+        copies[i].wait()
     site = arranged(site_in)
-    coeff = jnp.where(cell >= 0, arranged(coeff_in), 0.0)
-    cell = jnp.maximum(cell, 0)
-    cell_ref[...] = cell
+    coeff = jnp.where(bank >= 0, arranged(coeff_in), 0.0)
     site_ref[...] = site
     coeff_ref[...] = coeff
-    slots = depth_at_slots(depth, (), cell)
-    slots_ref[...] = slots
     for at, value in enumerate((slots, site.astype(jnp.float32), coeff)):
         for v, ref in enumerate((mine_ref, beside_ref, across_ref)):
             ref[8 * at : 8 * at + 8] = value[8 * v : 8 * v + 8]
@@ -382,7 +419,7 @@
 def advance_cells(base, edges, cell, coeff, segment, slots):
     major, minor = cell_parts(cell)
     rates = coeff * (segment - slots)
-    blocks = spread(rates, major, minor, QUADS * ROWS)
+    blocks = spread_cells(rates, major, minor)
     source = jnp.concatenate([blocks[q * ROWS : (q + 1) * ROWS] for q in range(QUADS)], axis=1)
     return flood_finish([base[0], base[1], base[2]], edges, source)
 
@@ -408,7 +445,7 @@
 
 
 def last_kernel(
-    state, got, near, over, base, cell_ref, coeff_ref, slots_ref, got_first, terms, state_out, reach_out, held_state, sent
+    state, got, near, over, base, cell_ref, coeff_ref, slots_ref, got_first, terms, state_out, reach_out
 ):
     cells = [state[0], state[1], state[2]]
     edges = get_edges(got, near, over, cells, place(), EDGE, 6)
@@ -416,9 +453,7 @@
         base, edges, cell_ref[...], coeff_ref[...], gathered(got, 3), slots_ref[...]
     )
     for k in range(3):
-        held_state[k] = new[k]
-    copy = pltpu.make_async_copy(held_state, state_out, sent)
-    copy.start()
+        state_out[k] = new[k]
     outlets = got[:, 7, :]
     lane = iota((FIELDS, LANES), 1)
     for b in range(BASINS):
@@ -431,7 +466,6 @@
         level = got[b, 32:40, :] + entering + (DT * RATIO) * drawn
         for f in range(FIELDS):
             reach_out[b : b + 1, f * LANES : (f + 1) * LANES] = level[f : f + 1]
-    copy.wait()
 
 
 def step_kernel(first, tail, *refs):
@@ -645,16 +679,11 @@
         got, near, over, base = exchange(
             last_pack if tail else pack, 40 if tail else BASINS, beside, across, mine, base
         )
-    inputs = [state, got, near, over, base, cell, coeff, slots, got_first, terms]
-    state, reach = pl.pallas_call(
+    state, reach = call(
         last_kernel,
-        out_shape=[f32(3, ROWS, COLS), f32(BASINS, FIELDS * LANES)],
-        in_specs=[pl.BlockSpec(memory_space=pltpu.VMEM) for _ in inputs],
-        out_specs=[pl.BlockSpec(memory_space=pl.ANY), pl.BlockSpec(memory_space=pltpu.VMEM)],
-        scratch_shapes=[pltpu.VMEM((3, ROWS, COLS), jnp.float32), pltpu.SemaphoreType.DMA],
-        compiler_params=None if INTERPRET else pltpu.CompilerParams(vmem_limit_bytes=16 << 20),
-        interpret=pltpu.InterpretParams() if INTERPRET else False,
-    )(*inputs)
+        [f32(3, ROWS, COLS), f32(BASINS, FIELDS * LANES)],
+        [state, got, near, over, base, cell, coeff, slots, got_first, terms],
+    )
     return state, reach
 
 

time: 98.7 us -> 97.9 us (level)
    pallas_call x1 -> x0, Pallas kernels: 3.42 us -> none  [per_device(): pl.pallas_call(last_kernel, out_shape=[f32(3, ROWS, COLS), f32(BASINS, FI...]
    pallas_call x11 -> x12, Pallas kernels: 5.69 us -> 8.33 us  [call(): pl.pallas_call(kernel, out_shape=outs, in_specs=[pl.BlockSpec(memory_spac...]
where the time goes in v8:
time: 97.9 us; the launch traced here: 97.4 us
  blocking collectives  48.9 us (50%)
  starting transfers between devices  30.2 us (31%)
  Pallas kernels  9.9 us (10%)
  waiting for transfers between devices  7.5 us (8%)
    all_to_all x4, blocking collectives, exchange(): return (lax.all_to_all(send, 'gy', 0, 0), near, over, ready)  48.9 us
    ppermute x4, starting transfers between devices, exchange(): over = lax.ppermute(across, 'gx', border)  22.5 us
    pallas_call x12, Pallas kernels, call(): pl.pallas_call(kernel, out_shape=outs, in_specs=[pl.BlockSpec(memory_spac...  8.33 us
    ppermute x4, starting transfers between devices, exchange(): near = lax.ppermute(beside, 'gx', chip)  7.68 us
    ppermute x4, waiting for transfers between devices, exchange(): over = lax.ppermute(across, 'gx', border)  6.72 us
  transfers between devices with their start and end apart: 8, of which 4 were waited for; matrix products, arithmetic and copies ran while one was open for 0% of the time, Pallas kernels for 1%

profile of v8, /device:TPU:6, one launch (start us, length us, event | category | flops | bytes accessed | tf_op | source)
XLA Modules:
  0.0 97.4 jit_solution(6223123387972517695)
XLA Ops:
  0.7 1.6 %shard_map.113 = (f32[104,128]{1,0:T(8,128)S(1)}, f32[104,128]{1,0:T(8,128)S(1)}, f32[32,128]{1,0:T(8,128)S(1)}, s32[24,128]{1,0:T(8,128)S(1)}, s32[24,128]{1,0:...) custom-call(f32[32,512]{1,0:T(8,128)} %refs_0_.3, f32[2,32,512]{2,1,0:T(8,128)} %refs_1_.3, ...), custom_call_target="tpu_custom_call" | custom-call | tf_op jit(solution)/shard_map/pallas_call | solution.py:629
  2.2 0.0 copy-start.4
  2.3 0.0 copy-start.5
  2.3 14.3 %collective-permute-start = (f32[104,128]{1,0:T(8,128)S(1)}, f32[104,128]{1,0:T(8,128)S(1)}, u32[]{:S(2)}, u32[]{:S(2)}) collective-permute-start(f32[104,128]{1,0:T(8,128)S(1)} %get-tuple-element.64), channel_id=1, source_target_pairs={{8,16},{24,32},{40,48},{56,64},{72,80},{88,96},{104,112},{120,128}... | collective-permute-start | bytes 159752 | tf_op jit(solution)/shard_map/ppermute | solution.py:611
  16.6 1.9 %collective-permute-start.1 = (f32[104,128]{1,0:T(8,128)S(1)}, f32[104,128]{1,0:T(8,128)S(1)}, u32[]{:S(2)}, u32[]{:S(2)}) collective-permute-start(f32[104,128]{1,0:T(8,128)S(1)} %get-tuple-element.65), channel_id=1, source_target_pairs={{0,8},{8,0},{16,24},{24,16},{32,40},{40,32},{48,56},{56,48},{64,72... | collective-permute-start | bytes 159752 | tf_op jit(solution)/shard_map/ppermute | solution.py:610
  18.5 0.1 copy.12.upstream
  18.6 0.3 shard_map.115
  18.9 0.0 collective-permute-done.over.refs_7_
  18.9 0.8 collective-permute-done.1.near.refs_6_
  19.7 0.0 copy-start.3
  19.8 16.3 %all_to_all.20.refs_5_.got_first = f32[8,32,128]{2,1,0:T(8,128)S(1)} all-to-all(f32[8,32,128]{2,1,0:T(8,128)S(1)} %shard_map.114), channel_id=1, replica_groups=mesh['gx'=96,'gy'=8] {'gy'}, dimensions={0} | all-to-all | bytes 262144 | tf_op jit(solution)/shard_map/all_to_all | solution.py:615
  36.0 1.5 %shard_map.116 = (f32[3,32,512]{2,1,0:T(8,128)S(1)}, f32[24,128]{1,0:T(8,128)S(1)}, f32[40,128]{1,0:T(8,128)S(1)}, f32[40,128]{1,0:T(8,128)S(1)}, f32[32,128]{1,...) custom-call(f32[32,512]{1,0:T(8,128)S(1)} %copy-done.2, ...), custom_call_target="tpu_custom_call" | custom-call | tf_op jit(solution)/shard_map/pallas_call | solution.py:573
  37.5 3.4 %collective-permute-start.2 = (f32[40,128]{1,0:T(8,128)S(1)}, f32[40,128]{1,0:T(8,128)S(1)}, u32[]{:S(2)}, u32[]{:S(2)}) collective-permute-start(f32[40,128]{1,0:T(8,128)S(1)} %get-tuple-element.85), channel_id=1, source_target_pairs={{8,16},{24,32},{40,48},{56,64},{72,80},{88,96},{104,112},{120,128}... | collective-permute-start | bytes 61448 | tf_op jit(solution)/shard_map/ppermute | solution.py:611
  40.9 1.9 %collective-permute-start.3 = (f32[40,128]{1,0:T(8,128)S(1)}, f32[40,128]{1,0:T(8,128)S(1)}, u32[]{:S(2)}, u32[]{:S(2)}) collective-permute-start(f32[40,128]{1,0:T(8,128)S(1)} %get-tuple-element.86), channel_id=1, source_target_pairs={{0,8},{8,0},{16,24},{24,16},{32,40},{40,32},{48,56},{56,48},{64,72... | collective-permute-start | bytes 61448 | tf_op jit(solution)/shard_map/ppermute | solution.py:610
  42.8 0.4 shard_map.118
  43.3 1.5 %collective-permute-done.2.over.refs_8_ = f32[40,128]{1,0:T(8,128)S(1)} collective-permute-done((f32[40,128]{1,0:T(8,128)S(1)}, f32[40,128]{1,0:T(8,128)S(1)}, u32[]{:S(2)}, u32[]{:S(2)}) %collective-permute-start.2) | collective-permute-done | bytes 20512 | tf_op jit(solution)/shard_map/ppermute | solution.py:611
  44.7 0.0 collective-permute-done.3.near.refs_7_
  44.8 10.4 %all_to_all.21.refs_6_ = f32[8,8,128]{2,1,0:T(8,128)S(1)} all-to-all(f32[8,8,128]{2,1,0:T(8,128)S(1)} %shard_map.117), channel_id=1, replica_groups=mesh['gx'=96,'gy'=8] {'gy'}, dimensions={0} | all-to-all | bytes 65536 | tf_op jit(solution)/shard_map/all_to_all | solution.py:615
  55.2 1.4 %shard_map.119 = (f32[3,32,512]{2,1,0:T(8,128)S(1)}, f32[24,128]{1,0:T(8,128)S(1)}, f32[40,128]{1,0:T(8,128)S(1)}, f32[40,128]{1,0:T(8,128)S(1)}, f32[32,128]{1,...) custom-call(f32[3,32,512]{2,1,0:T(8,128)S(1)} %get-tuple-element.76.state.refs_0_, ...), custom_call_target="tpu_custom_call" | custom-call | tf_op jit(solution)/shard_map/pallas_call | solution.py:573
  56.5 2.4 %collective-permute-start.4 = (f32[40,128]{1,0:T(8,128)S(1)}, f32[40,128]{1,0:T(8,128)S(1)}, u32[]{:S(2)}, u32[]{:S(2)}) collective-permute-start(f32[40,128]{1,0:T(8,128)S(1)} %get-tuple-element.99), channel_id=1, source_target_pairs={{8,16},{24,32},{40,48},{56,64},{72,80},{88,96},{104,112},{120,128}... | collective-permute-start | bytes 61448 | tf_op jit(solution)/shard_map/ppermute | solution.py:611
  58.9 1.9 %collective-permute-start.5 = (f32[40,128]{1,0:T(8,128)S(1)}, f32[40,128]{1,0:T(8,128)S(1)}, u32[]{:S(2)}, u32[]{:S(2)}) collective-permute-start(f32[40,128]{1,0:T(8,128)S(1)} %get-tuple-element.100), channel_id=1, source_target_pairs={{0,8},{8,0},{16,24},{24,16},{32,40},{40,32},{48,56},{56,48},{64,72... | collective-permute-start | bytes 61448 | tf_op jit(solution)/shard_map/ppermute | solution.py:610
  60.8 0.2 shard_map.121.refs_9_
  61.1 2.6 %collective-permute-done.4.over.refs_8_ = f32[40,128]{1,0:T(8,128)S(1)} collective-permute-done((f32[40,128]{1,0:T(8,128)S(1)}, f32[40,128]{1,0:T(8,128)S(1)}, u32[]{:S(2)}, u32[]{:S(2)}) %collective-permute-start.4) | collective-permute-done | bytes 20512 | tf_op jit(solution)/shard_map/ppermute | solution.py:611
  63.7 0.0 collective-permute-done.5.near.refs_7_
  63.8 10.4 %all_to_all.22.refs_6_ = f32[8,8,128]{2,1,0:T(8,128)S(1)} all-to-all(f32[8,8,128]{2,1,0:T(8,128)S(1)} %shard_map.120), channel_id=1, replica_groups=mesh['gx'=96,'gy'=8] {'gy'}, dimensions={0} | all-to-all | bytes 65536 | tf_op jit(solution)/shard_map/all_to_all | solution.py:615
  74.2 1.3 %shard_map.122 = (f32[3,32,512]{2,1,0:T(8,128)S(1)}, f32[24,128]{1,0:T(8,128)S(1)}, f32[40,128]{1,0:T(8,128)S(1)}, f32[40,128]{1,0:T(8,128)S(1)}, f32[32,128]{1,0:T(8,128)S(1)}) custom-call(f32[3,32,512]{2,1,0:T(8,128)S(1)} %get-tuple-element.93.state.refs_0_, f32[8,128]{1,0:T(8,128)S(1)} %get-tuple-element.94.refs_1_, ...), custom_call_target="tpu_custom_call" | custom-call | tf_op jit(solution)/shard_map/pallas_call | solution.py:573
  75.5 2.4 %collective-permute-start.6 = (f32[40,128]{1,0:T(8,128)S(1)}, f32[40,128]{1,0:T(8,128)S(1)}, u32[]{:S(2)}, u32[]{:S(2)}) collective-permute-start(f32[40,128]{1,0:T(8,128)S(1)} %get-tuple-element.111), channel_id=1, source_target_pairs={{8,16},{24,32},{40,48},{56,64},{72,80},{88,96},{104,112},{120,128}... | collective-permute-start | bytes 61448 | tf_op jit(solution)/shard_map/ppermute | solution.py:611
  77.9 1.9 %collective-permute-start.7 = (f32[40,128]{1,0:T(8,128)S(1)}, f32[40,128]{1,0:T(8,128)S(1)}, u32[]{:S(2)}, u32[]{:S(2)}) collective-permute-start(f32[40,128]{1,0:T(8,128)S(1)} %get-tuple-element.112), channel_id=1, source_target_pairs={{0,8},{8,0},{16,24},{24,16},{32,40},{40,32},{48,56},{56,48},{64,72... | collective-permute-start | bytes 61448 | tf_op jit(solution)/shard_map/ppermute | solution.py:610
  79.9 0.2 shard_map.124.base
  80.1 2.6 %collective-permute-done.6.over = f32[40,128]{1,0:T(8,128)S(1)} collective-permute-done((f32[40,128]{1,0:T(8,128)S(1)}, f32[40,128]{1,0:T(8,128)S(1)}, u32[]{:S(2)}, u32[]{:S(2)}) %collective-permute-start.6) | collective-permute-done | bytes 20512 | tf_op jit(solution)/shard_map/ppermute | solution.py:611
  82.8 11.8 %all_to_all.23.got = f32[8,40,128]{2,1,0:T(8,128)S(1)} all-to-all(f32[8,40,128]{2,1,0:T(8,128)S(1)} %shard_map.123), channel_id=1, replica_groups=mesh['gx'=96,'gy'=8] {'gy'}, dimensions={0} | all-to-all | bytes 327680 | tf_op jit(solution)/shard_map/all_to_all | solution.py:615
  94.6 2.8 %shard_map.125 = (f32[3,32,512]{2,1,0:T(8,128)}, f32[8,1024]{1,0:T(8,128)}) custom-call(f32[3,32,512]{2,1,0:T(8,128)S(1)} %get-tuple-element.107.state, f32[8,40,128]{2,1,0:T(8,128)S(1)} %all_to_all.23.got, f32[40,128]{1,0:T(8,128)S(1)} %collective-permute-done.7.near, f32[40,128]{1,0:T(8,128)S(1)} %collective-permute-done.6.over, ...), custom_call_target="tpu_custom_call" | custom-call | tf_op jit(solution)/shard_map/pallas_call | solution.py:573
  (16 shorter events, 0.2 us)
Async XLA Ops:
  0.6 18.0 %copy-start = (f32[2,32,512]{2,1,0:T(8,128)S(1)}, f32[2,32,512]{2,1,0:T(8,128)}, u32[]{:S(2)}) copy-start(f32[2,32,512]{2,1,0:T(8,128)} %refs_1_.3) | copy-start | bytes 393220
  0.6 18.0 %copy-start.2 = (f32[32,512]{1,0:T(8,128)S(1)}, f32[32,512]{1,0:T(8,128)}, u32[]{:S(2)}) copy-start(f32[32,512]{1,0:T(8,128)} %refs_0_.3) | copy-start | bytes 196612
  0.7 17.9 %copy-start.1 = (f32[32,512]{1,0:T(8,128)S(1)}, f32[32,512]{1,0:T(8,128)}, u32[]{:S(2)}) copy-start(f32[32,512]{1,0:T(8,128)} %rough.7) | copy-start | bytes 196612
  0.7 17.8 %copy-start.6 = (s32[8,2]{0,1:T(2,128)S(1)}, s32[8,2]{0,1:T(2,128)}, u32[]{:S(2)}) copy-start(s32[8,2]{0,1:T(2,128)} %param.16) | copy-start | bytes 196
  2.2 16.4 %copy-start.4 = (f32[8,8]{1,0:T(8,128)S(1)}, f32[8,8]{1,0:T(8,128)}, u32[]{:S(2)}) copy-start(f32[8,8]{1,0:T(8,128)} %celerity.1) | copy-start | bytes 772
  2.3 16.3 %copy-start.5 = (f32[8,8]{1,0:T(8,128)S(1)}, f32[8,8]{1,0:T(8,128)}, u32[]{:S(2)}) copy-start(f32[8,8]{1,0:T(8,128)} %base_inflow.1) | copy-start | bytes 772
  2.3 16.7 %collective-permute-start = (f32[104,128]{1,0:T(8,128)S(1)}, f32[104,128]{1,0:T(8,128)S(1)}, u32[]{:S(2)}, u32[]{:S(2)}) collective-permute-start(f32[104,128]{1,0:T(8,128)S(1)} %get-tuple-element.64), channel_id=1, source_target_pairs={{8,16},{24,32},{40,48},{56,64},{72,80},{88,96},{104,112},{120,128}... | collective-permute-start | bytes 159752 | tf_op jit(solution)/shard_map/ppermute | solution.py:611
  16.6 3.1 %collective-permute-start.1 = (f32[104,128]{1,0:T(8,128)S(1)}, f32[104,128]{1,0:T(8,128)S(1)}, u32[]{:S(2)}, u32[]{:S(2)}) collective-permute-start(f32[104,128]{1,0:T(8,128)S(1)} %get-tuple-element.65), channel_id=1, source_target_pairs={{0,8},{8,0},{16,24},{24,16},{32,40},{40,32},{48,56},{56,48},{64,72... | collective-permute-start | bytes 159752 | tf_op jit(solution)/shard_map/ppermute | solution.py:610
  19.7 16.3 %copy-start.3 = (f32[8,1024]{1,0:T(8,128)S(1)}, f32[8,1024]{1,0:T(8,128)}, u32[]{:S(2)}) copy-start(f32[8,1024]{1,0:T(8,128)} %refs_2_.3) | copy-start | bytes 98308
  37.5 7.2 %collective-permute-start.2 = (f32[40,128]{1,0:T(8,128)S(1)}, f32[40,128]{1,0:T(8,128)S(1)}, u32[]{:S(2)}, u32[]{:S(2)}) collective-permute-start(f32[40,128]{1,0:T(8,128)S(1)} %get-tuple-element.85), channel_id=1, source_target_pairs={{8,16},{24,32},{40,48},{56,64},{72,80},{88,96},{104,112},{120,128}... | collective-permute-start | bytes 61448 | tf_op jit(solution)/shard_map/ppermute | solution.py:611
  40.9 3.8 %collective-permute-start.3 = (f32[40,128]{1,0:T(8,128)S(1)}, f32[40,128]{1,0:T(8,128)S(1)}, u32[]{:S(2)}, u32[]{:S(2)}) collective-permute-start(f32[40,128]{1,0:T(8,128)S(1)} %get-tuple-element.86), channel_id=1, source_target_pairs={{0,8},{8,0},{16,24},{24,16},{32,40},{40,32},{48,56},{56,48},{64,72... | collective-permute-start | bytes 61448 | tf_op jit(solution)/shard_map/ppermute | solution.py:610
  56.5 7.2 %collective-permute-start.4 = (f32[40,128]{1,0:T(8,128)S(1)}, f32[40,128]{1,0:T(8,128)S(1)}, u32[]{:S(2)}, u32[]{:S(2)}) collective-permute-start(f32[40,128]{1,0:T(8,128)S(1)} %get-tuple-element.99), channel_id=1, source_target_pairs={{8,16},{24,32},{40,48},{56,64},{72,80},{88,96},{104,112},{120,128}... | collective-permute-start | bytes 61448 | tf_op jit(solution)/shard_map/ppermute | solution.py:611
  58.9 4.8 %collective-permute-start.5 = (f32[40,128]{1,0:T(8,128)S(1)}, f32[40,128]{1,0:T(8,128)S(1)}, u32[]{:S(2)}, u32[]{:S(2)}) collective-permute-start(f32[40,128]{1,0:T(8,128)S(1)} %get-tuple-element.100), channel_id=1, source_target_pairs={{0,8},{8,0},{16,24},{24,16},{32,40},{40,32},{48,56},{56,48},{64,72... | collective-permute-start | bytes 61448 | tf_op jit(solution)/shard_map/ppermute | solution.py:610
  75.5 7.2 %collective-permute-start.6 = (f32[40,128]{1,0:T(8,128)S(1)}, f32[40,128]{1,0:T(8,128)S(1)}, u32[]{:S(2)}, u32[]{:S(2)}) collective-permute-start(f32[40,128]{1,0:T(8,128)S(1)} %get-tuple-element.111), channel_id=1, source_target_pairs={{8,16},{24,32},{40,48},{56,64},{72,80},{88,96},{104,112},{120,128}... | collective-permute-start | bytes 61448 | tf_op jit(solution)/shard_map/ppermute | solution.py:611
  77.9 4.8 %collective-permute-start.7 = (f32[40,128]{1,0:T(8,128)S(1)}, f32[40,128]{1,0:T(8,128)S(1)}, u32[]{:S(2)}, u32[]{:S(2)}) collective-permute-start(f32[40,128]{1,0:T(8,128)S(1)} %get-tuple-element.112), channel_id=1, source_target_pairs={{0,8},{8,0},{16,24},{24,16},{32,40},{40,32},{48,56},{56,48},{64,72... | collective-permute-start | bytes 61448 | tf_op jit(solution)/shard_map/ppermute | solution.py:610

commit v9 on v8

--- a/solution.py
+++ b/solution.py
@@ -607,9 +607,9 @@
 
     def exchange(kernel, rows, beside, across, mine, ready):
         across, beside = lax.optimization_barrier((across, beside))
+        over = lax.ppermute(across, "gx", border)
         near = lax.ppermute(beside, "gx", chip)
-        over = lax.ppermute(across, "gx", border)
-        over, near = lax.optimization_barrier((over, near))
+        near, over = lax.optimization_barrier((near, over))
         send = call(kernel, [f32(BASINS, rows, LANES)], [mine, near, over])[0]
         send, ready = lax.optimization_barrier((send, ready))
         return lax.all_to_all(send, "gy", 0, 0), near, over, ready

time: 97.9 us -> 105 us (1.073)
  waiting for transfers between devices: 7.5 us -> 12.4 us
  starting transfers between devices: 30.2 us -> 32.3 us
    ppermute x4, waiting for transfers between devices: 6.72 us -> 12.4 us  [exchange(): over = lax.ppermute(across, 'gx', border)]
    ppermute x4, starting transfers between devices: 22.5 us -> 24.6 us  [exchange(): over = lax.ppermute(across, 'gx', border)]
where the time goes in v9:
time: 105 us; the launch traced here: 104 us
  blocking collectives  48.6 us (46%)
  starting transfers between devices  32.3 us (31%)
  waiting for transfers between devices  12.4 us (12%)
  Pallas kernels  9.89 us (9%)
    all_to_all x4, blocking collectives, exchange(): return (lax.all_to_all(send, 'gy', 0, 0), near, over, ready)  48.6 us
    ppermute x4, starting transfers between devices, exchange(): over = lax.ppermute(across, 'gx', border)  24.6 us
    ppermute x4, waiting for transfers between devices, exchange(): over = lax.ppermute(across, 'gx', border)  12.4 us
    pallas_call x12, Pallas kernels, call(): pl.pallas_call(kernel, out_shape=outs, in_specs=[pl.BlockSpec(memory_spac...  8.33 us
    ppermute x4, starting transfers between devices, exchange(): near = lax.ppermute(beside, 'gx', chip)  7.68 us
  transfers between devices with their start and end apart: 8, of which 4 were waited for; matrix products, arithmetic and copies ran while one was open for 0% of the time, Pallas kernels for 1%

profile of v9, /device:TPU:6, one launch (start us, length us, event | category | flops | bytes accessed | tf_op | source)
XLA Modules:
  0.0 104.1 jit_solution(6827548877058555366)
XLA Ops:
  0.7 1.6 %shard_map.113 = (f32[104,128]{1,0:T(8,128)S(1)}, f32[104,128]{1,0:T(8,128)S(1)}, f32[32,128]{1,0:T(8,128)S(1)}, s32[24,128]{1,0:T(8,128)S(1)}, s32[24,128]{1,0:...) custom-call(f32[32,512]{1,0:T(8,128)} %refs_0_.3, f32[2,32,512]{2,1,0:T(8,128)} %refs_1_.3, ...), custom_call_target="tpu_custom_call" | custom-call | tf_op jit(solution)/shard_map/pallas_call | solution.py:629
  2.2 0.0 copy-start.4
  2.3 0.0 copy-start.5
  2.3 1.9 %collective-permute-start = (f32[104,128]{1,0:T(8,128)S(1)}, f32[104,128]{1,0:T(8,128)S(1)}, u32[]{:S(2)}, u32[]{:S(2)}) collective-permute-start(f32[104,128]{1,0:T(8,128)S(1)} %get-tuple-element.64), channel_id=1, source_target_pairs={{0,8},{8,0},{16,24},{24,16},{32,40},{40,32},{48,56},{56,48},{64,72... | collective-permute-start | bytes 159752 | tf_op jit(solution)/shard_map/ppermute | solution.py:611
  4.2 15.0 %collective-permute-start.1 = (f32[104,128]{1,0:T(8,128)S(1)}, f32[104,128]{1,0:T(8,128)S(1)}, u32[]{:S(2)}, u32[]{:S(2)}) collective-permute-start(f32[104,128]{1,0:T(8,128)S(1)} %get-tuple-element.65), channel_id=1, source_target_pairs={{8,16},{24,32},{40,48},{56,64},{72,80},{88,96},{104,112},{120,128}... | collective-permute-start | bytes 159752 | tf_op jit(solution)/shard_map/ppermute | solution.py:610
  19.2 0.1 copy.12.upstream
  19.3 0.3 shard_map.115
  19.6 0.0 collective-permute-done.near.refs_6_
  19.6 1.4 %collective-permute-done.1.over.refs_7_ = f32[104,128]{1,0:T(8,128)S(1)} collective-permute-done((f32[104,128]{1,0:T(8,128)S(1)}, f32[104,128]{1,0:T(8,128)S(1)}, u32[]{:S(2)}, u32[]{:S(2)}) %collective-permute-start.1) | collective-permute-done | bytes 53280 | tf_op jit(solution)/shard_map/ppermute | solution.py:610
  21.0 0.0 copy-start.3
  21.0 16.0 %all_to_all.20.refs_5_.got_first = f32[8,32,128]{2,1,0:T(8,128)S(1)} all-to-all(f32[8,32,128]{2,1,0:T(8,128)S(1)} %shard_map.114), channel_id=1, replica_groups=mesh['gx'=96,'gy'=8] {'gy'}, dimensions={0} | all-to-all | bytes 262144 | tf_op jit(solution)/shard_map/all_to_all | solution.py:615
  37.0 1.5 %shard_map.116 = (f32[3,32,512]{2,1,0:T(8,128)S(1)}, f32[24,128]{1,0:T(8,128)S(1)}, f32[40,128]{1,0:T(8,128)S(1)}, f32[40,128]{1,0:T(8,128)S(1)}, f32[32,128]{1,...) custom-call(f32[32,512]{1,0:T(8,128)S(1)} %copy-done.2, ...), custom_call_target="tpu_custom_call" | custom-call | tf_op jit(solution)/shard_map/pallas_call | solution.py:573
  38.5 1.9 %collective-permute-start.2 = (f32[40,128]{1,0:T(8,128)S(1)}, f32[40,128]{1,0:T(8,128)S(1)}, u32[]{:S(2)}, u32[]{:S(2)}) collective-permute-start(f32[40,128]{1,0:T(8,128)S(1)} %get-tuple-element.85), channel_id=1, source_target_pairs={{0,8},{8,0},{16,24},{24,16},{32,40},{40,32},{48,56},{56,48},{64,72... | collective-permute-start | bytes 61448 | tf_op jit(solution)/shard_map/ppermute | solution.py:611
  40.4 4.4 %collective-permute-start.3 = (f32[40,128]{1,0:T(8,128)S(1)}, f32[40,128]{1,0:T(8,128)S(1)}, u32[]{:S(2)}, u32[]{:S(2)}) collective-permute-start(f32[40,128]{1,0:T(8,128)S(1)} %get-tuple-element.86), channel_id=1, source_target_pairs={{8,16},{24,32},{40,48},{56,64},{72,80},{88,96},{104,112},{120,128}... | collective-permute-start | bytes 61448 | tf_op jit(solution)/shard_map/ppermute | solution.py:610
  44.8 0.4 shard_map.118
  45.2 0.0 collective-permute-done.2.near.refs_7_
  45.2 2.4 %collective-permute-done.3.over.refs_8_ = f32[40,128]{1,0:T(8,128)S(1)} collective-permute-done((f32[40,128]{1,0:T(8,128)S(1)}, f32[40,128]{1,0:T(8,128)S(1)}, u32[]{:S(2)}, u32[]{:S(2)}) %collective-permute-start.3) | collective-permute-done | bytes 20512 | tf_op jit(solution)/shard_map/ppermute | solution.py:610
  47.6 10.4 %all_to_all.21.refs_6_ = f32[8,8,128]{2,1,0:T(8,128)S(1)} all-to-all(f32[8,8,128]{2,1,0:T(8,128)S(1)} %shard_map.117), channel_id=1, replica_groups=mesh['gx'=96,'gy'=8] {'gy'}, dimensions={0} | all-to-all | bytes 65536 | tf_op jit(solution)/shard_map/all_to_all | solution.py:615
  58.0 1.4 %shard_map.119 = (f32[3,32,512]{2,1,0:T(8,128)S(1)}, f32[24,128]{1,0:T(8,128)S(1)}, f32[40,128]{1,0:T(8,128)S(1)}, f32[40,128]{1,0:T(8,128)S(1)}, f32[32,128]{1,...) custom-call(f32[3,32,512]{2,1,0:T(8,128)S(1)} %get-tuple-element.76.state.refs_0_, ...), custom_call_target="tpu_custom_call" | custom-call | tf_op jit(solution)/shard_map/pallas_call | solution.py:573
  59.4 1.9 %collective-permute-start.4 = (f32[40,128]{1,0:T(8,128)S(1)}, f32[40,128]{1,0:T(8,128)S(1)}, u32[]{:S(2)}, u32[]{:S(2)}) collective-permute-start(f32[40,128]{1,0:T(8,128)S(1)} %get-tuple-element.99), channel_id=1, source_target_pairs={{0,8},{8,0},{16,24},{24,16},{32,40},{40,32},{48,56},{56,48},{64,72... | collective-permute-start | bytes 61448 | tf_op jit(solution)/shard_map/ppermute | solution.py:611
  61.3 3.2 %collective-permute-start.5 = (f32[40,128]{1,0:T(8,128)S(1)}, f32[40,128]{1,0:T(8,128)S(1)}, u32[]{:S(2)}, u32[]{:S(2)}) collective-permute-start(f32[40,128]{1,0:T(8,128)S(1)} %get-tuple-element.100), channel_id=1, source_target_pairs={{8,16},{24,32},{40,48},{56,64},{72,80},{88,96},{104,112},{120,128}... | collective-permute-start | bytes 61448 | tf_op jit(solution)/shard_map/ppermute | solution.py:610
  64.5 0.2 shard_map.121.refs_9_
  64.8 3.7 %collective-permute-done.5.over.refs_8_ = f32[40,128]{1,0:T(8,128)S(1)} collective-permute-done((f32[40,128]{1,0:T(8,128)S(1)}, f32[40,128]{1,0:T(8,128)S(1)}, u32[]{:S(2)}, u32[]{:S(2)}) %collective-permute-start.5) | collective-permute-done | bytes 20512 | tf_op jit(solution)/shard_map/ppermute | solution.py:610
  68.6 10.4 %all_to_all.22.refs_6_ = f32[8,8,128]{2,1,0:T(8,128)S(1)} all-to-all(f32[8,8,128]{2,1,0:T(8,128)S(1)} %shard_map.120), channel_id=1, replica_groups=mesh['gx'=96,'gy'=8] {'gy'}, dimensions={0} | all-to-all | bytes 65536 | tf_op jit(solution)/shard_map/all_to_all | solution.py:615
  79.0 1.3 %shard_map.122 = (f32[3,32,512]{2,1,0:T(8,128)S(1)}, f32[24,128]{1,0:T(8,128)S(1)}, f32[40,128]{1,0:T(8,128)S(1)}, f32[40,128]{1,0:T(8,128)S(1)}, f32[32,128]{1,0:T(8,128)S(1)}) custom-call(f32[3,32,512]{2,1,0:T(8,128)S(1)} %get-tuple-element.93.state.refs_0_, f32[8,128]{1,0:T(8,128)S(1)} %get-tuple-element.94.refs_1_, ...), custom_call_target="tpu_custom_call" | custom-call | tf_op jit(solution)/shard_map/pallas_call | solution.py:573
  80.3 1.9 %collective-permute-start.6 = (f32[40,128]{1,0:T(8,128)S(1)}, f32[40,128]{1,0:T(8,128)S(1)}, u32[]{:S(2)}, u32[]{:S(2)}) collective-permute-start(f32[40,128]{1,0:T(8,128)S(1)} %get-tuple-element.111), channel_id=1, source_target_pairs={{0,8},{8,0},{16,24},{24,16},{32,40},{40,32},{48,56},{56,48},{64,72... | collective-permute-start | bytes 61448 | tf_op jit(solution)/shard_map/ppermute | solution.py:611
  82.2 2.1 %collective-permute-start.7 = (f32[40,128]{1,0:T(8,128)S(1)}, f32[40,128]{1,0:T(8,128)S(1)}, u32[]{:S(2)}, u32[]{:S(2)}) collective-permute-start(f32[40,128]{1,0:T(8,128)S(1)} %get-tuple-element.112), channel_id=1, source_target_pairs={{8,16},{24,32},{40,48},{56,64},{72,80},{88,96},{104,112},{120,128}... | collective-permute-start | bytes 61448 | tf_op jit(solution)/shard_map/ppermute | solution.py:610
  84.3 0.2 shard_map.124.base
  84.6 0.0 collective-permute-done.6.near
  84.6 4.9 %collective-permute-done.7.over = f32[40,128]{1,0:T(8,128)S(1)} collective-permute-done((f32[40,128]{1,0:T(8,128)S(1)}, f32[40,128]{1,0:T(8,128)S(1)}, u32[]{:S(2)}, u32[]{:S(2)}) %collective-permute-start.7) | collective-permute-done | bytes 20512 | tf_op jit(solution)/shard_map/ppermute | solution.py:610
  89.5 11.8 %all_to_all.23.got = f32[8,40,128]{2,1,0:T(8,128)S(1)} all-to-all(f32[8,40,128]{2,1,0:T(8,128)S(1)} %shard_map.123), channel_id=1, replica_groups=mesh['gx'=96,'gy'=8] {'gy'}, dimensions={0} | all-to-all | bytes 327680 | tf_op jit(solution)/shard_map/all_to_all | solution.py:615
  101.3 2.8 %shard_map.125 = (f32[3,32,512]{2,1,0:T(8,128)}, f32[8,1024]{1,0:T(8,128)}) custom-call(f32[3,32,512]{2,1,0:T(8,128)S(1)} %get-tuple-element.107.state, f32[8,40,128]{2,1,0:T(8,128)S(1)} %all_to_all.23.got, f32[40,128]{1,0:T(8,128)S(1)} %collective-permute-done.6.near, f32[40,128]{1,0:T(8,128)S(1)} %collective-permute-done.7.over, ...), custom_call_target="tpu_custom_call" | custom-call | tf_op jit(solution)/shard_map/pallas_call | solution.py:573
  (16 shorter events, 0.2 us)
Async XLA Ops:
  0.6 18.6 %copy-start = (f32[2,32,512]{2,1,0:T(8,128)S(1)}, f32[2,32,512]{2,1,0:T(8,128)}, u32[]{:S(2)}) copy-start(f32[2,32,512]{2,1,0:T(8,128)} %refs_1_.3) | copy-start | bytes 393220
  0.6 18.6 %copy-start.2 = (f32[32,512]{1,0:T(8,128)S(1)}, f32[32,512]{1,0:T(8,128)}, u32[]{:S(2)}) copy-start(f32[32,512]{1,0:T(8,128)} %refs_0_.3) | copy-start | bytes 196612
  0.7 18.6 %copy-start.1 = (f32[32,512]{1,0:T(8,128)S(1)}, f32[32,512]{1,0:T(8,128)}, u32[]{:S(2)}) copy-start(f32[32,512]{1,0:T(8,128)} %rough.7) | copy-start | bytes 196612
  0.7 18.5 %copy-start.6 = (s32[8,2]{0,1:T(2,128)S(1)}, s32[8,2]{0,1:T(2,128)}, u32[]{:S(2)}) copy-start(s32[8,2]{0,1:T(2,128)} %param.16) | copy-start | bytes 196
  2.2 17.0 %copy-start.4 = (f32[8,8]{1,0:T(8,128)S(1)}, f32[8,8]{1,0:T(8,128)}, u32[]{:S(2)}) copy-start(f32[8,8]{1,0:T(8,128)} %celerity.1) | copy-start | bytes 772
  2.3 17.0 %copy-start.5 = (f32[8,8]{1,0:T(8,128)S(1)}, f32[8,8]{1,0:T(8,128)}, u32[]{:S(2)}) copy-start(f32[8,8]{1,0:T(8,128)} %base_inflow.1) | copy-start | bytes 772
  2.3 17.3 %collective-permute-start = (f32[104,128]{1,0:T(8,128)S(1)}, f32[104,128]{1,0:T(8,128)S(1)}, u32[]{:S(2)}, u32[]{:S(2)}) collective-permute-start(f32[104,128]{1,0:T(8,128)S(1)} %get-tuple-element.64), channel_id=1, source_target_pairs={{0,8},{8,0},{16,24},{24,16},{32,40},{40,32},{48,56},{56,48},{64,72... | collective-permute-start | bytes 159752 | tf_op jit(solution)/shard_map/ppermute | solution.py:611
  4.2 16.8 %collective-permute-start.1 = (f32[104,128]{1,0:T(8,128)S(1)}, f32[104,128]{1,0:T(8,128)S(1)}, u32[]{:S(2)}, u32[]{:S(2)}) collective-permute-start(f32[104,128]{1,0:T(8,128)S(1)} %get-tuple-element.65), channel_id=1, source_target_pairs={{8,16},{24,32},{40,48},{56,64},{72,80},{88,96},{104,112},{120,128}... | collective-permute-start | bytes 159752 | tf_op jit(solution)/shard_map/ppermute | solution.py:610
  21.0 16.0 %copy-start.3 = (f32[8,1024]{1,0:T(8,128)S(1)}, f32[8,1024]{1,0:T(8,128)}, u32[]{:S(2)}) copy-start(f32[8,1024]{1,0:T(8,128)} %refs_2_.3) | copy-start | bytes 98308
  38.5 6.7 %collective-permute-start.2 = (f32[40,128]{1,0:T(8,128)S(1)}, f32[40,128]{1,0:T(8,128)S(1)}, u32[]{:S(2)}, u32[]{:S(2)}) collective-permute-start(f32[40,128]{1,0:T(8,128)S(1)} %get-tuple-element.85), channel_id=1, source_target_pairs={{0,8},{8,0},{16,24},{24,16},{32,40},{40,32},{48,56},{56,48},{64,72... | collective-permute-start | bytes 61448 | tf_op jit(solution)/shard_map/ppermute | solution.py:611
  40.4 7.2 %collective-permute-start.3 = (f32[40,128]{1,0:T(8,128)S(1)}, f32[40,128]{1,0:T(8,128)S(1)}, u32[]{:S(2)}, u32[]{:S(2)}) collective-permute-start(f32[40,128]{1,0:T(8,128)S(1)} %get-tuple-element.86), channel_id=1, source_target_pairs={{8,16},{24,32},{40,48},{56,64},{72,80},{88,96},{104,112},{120,128}... | collective-permute-start | bytes 61448 | tf_op jit(solution)/shard_map/ppermute | solution.py:610
  59.4 5.4 %collective-permute-start.4 = (f32[40,128]{1,0:T(8,128)S(1)}, f32[40,128]{1,0:T(8,128)S(1)}, u32[]{:S(2)}, u32[]{:S(2)}) collective-permute-start(f32[40,128]{1,0:T(8,128)S(1)} %get-tuple-element.99), channel_id=1, source_target_pairs={{0,8},{8,0},{16,24},{24,16},{32,40},{40,32},{48,56},{56,48},{64,72... | collective-permute-start | bytes 61448 | tf_op jit(solution)/shard_map/ppermute | solution.py:611
  61.3 7.2 %collective-permute-start.5 = (f32[40,128]{1,0:T(8,128)S(1)}, f32[40,128]{1,0:T(8,128)S(1)}, u32[]{:S(2)}, u32[]{:S(2)}) collective-permute-start(f32[40,128]{1,0:T(8,128)S(1)} %get-tuple-element.100), channel_id=1, source_target_pairs={{8,16},{24,32},{40,48},{56,64},{72,80},{88,96},{104,112},{120,128}... | collective-permute-start | bytes 61448 | tf_op jit(solution)/shard_map/ppermute | solution.py:610
  80.3 4.3 %collective-permute-start.6 = (f32[40,128]{1,0:T(8,128)S(1)}, f32[40,128]{1,0:T(8,128)S(1)}, u32[]{:S(2)}, u32[]{:S(2)}) collective-permute-start(f32[40,128]{1,0:T(8,128)S(1)} %get-tuple-element.111), channel_id=1, source_target_pairs={{0,8},{8,0},{16,24},{24,16},{32,40},{40,32},{48,56},{56,48},{64,72... | collective-permute-start | bytes 61448 | tf_op jit(solution)/shard_map/ppermute | solution.py:611
  82.2 7.2 %collective-permute-start.7 = (f32[40,128]{1,0:T(8,128)S(1)}, f32[40,128]{1,0:T(8,128)S(1)}, u32[]{:S(2)}, u32[]{:S(2)}) collective-permute-start(f32[40,128]{1,0:T(8,128)S(1)} %get-tuple-element.112), channel_id=1, source_target_pairs={{8,16},{24,32},{40,48},{56,64},{72,80},{88,96},{104,112},{120,128}... | collective-permute-start | bytes 61448 | tf_op jit(solution)/shard_map/ppermute | solution.py:610

commit v10 on v8

--- a/solution.py
+++ b/solution.py
@@ -607,6 +607,7 @@
 
     def exchange(kernel, rows, beside, across, mine, ready):
         across, beside = lax.optimization_barrier((across, beside))
+        beside, ready = lax.optimization_barrier((beside, ready))
         near = lax.ppermute(beside, "gx", chip)
         over = lax.ppermute(across, "gx", border)
         over, near = lax.optimization_barrier((over, near))

time: 97.9 us -> 98.4 us (level)
  no operation moved by 1% of the time
where the time goes in v10:
time: 98.4 us; the launch traced here: 97.8 us
  blocking collectives  48.9 us (50%)
  starting transfers between devices  30.4 us (31%)
  Pallas kernels  9.9 us (10%)
  waiting for transfers between devices  7.66 us (8%)
    all_to_all x4, blocking collectives, exchange(): return (lax.all_to_all(send, 'gy', 0, 0), near, over, ready)  48.9 us
    ppermute x4, starting transfers between devices, exchange(): over = lax.ppermute(across, 'gx', border)  22.8 us
    pallas_call x12, Pallas kernels, call(): pl.pallas_call(kernel, out_shape=outs, in_specs=[pl.BlockSpec(memory_spac...  8.33 us
    ppermute x4, starting transfers between devices, exchange(): near = lax.ppermute(beside, 'gx', chip)  7.67 us
    ppermute x4, waiting for transfers between devices, exchange(): over = lax.ppermute(across, 'gx', border)  6.46 us
  transfers between devices with their start and end apart: 8, of which 4 were waited for; matrix products, arithmetic and copies ran while one was open for 0% of the time, Pallas kernels for 1%

profile of v10, /device:TPU:6, one launch (start us, length us, event | category | flops | bytes accessed | tf_op | source)
XLA Modules:
  0.0 97.8 jit_solution(13596620056061148337)
XLA Ops:
  0.7 1.6 %shard_map.113 = (f32[104,128]{1,0:T(8,128)S(1)}, f32[104,128]{1,0:T(8,128)S(1)}, f32[32,128]{1,0:T(8,128)S(1)}, s32[24,128]{1,0:T(8,128)S(1)}, s32[24,128]{1,0:...) custom-call(f32[32,512]{1,0:T(8,128)} %refs_0_.3, f32[2,32,512]{2,1,0:T(8,128)} %refs_1_.3, ...), custom_call_target="tpu_custom_call" | custom-call | tf_op jit(solution)/shard_map/pallas_call | solution.py:630
  2.2 0.0 copy-start.4
  2.3 0.0 copy-start.5
  2.3 14.3 %collective-permute-start = (f32[104,128]{1,0:T(8,128)S(1)}, f32[104,128]{1,0:T(8,128)S(1)}, u32[]{:S(2)}, u32[]{:S(2)}) collective-permute-start(f32[104,128]{1,0:T(8,128)S(1)} %get-tuple-element.73), channel_id=1, source_target_pairs={{8,16},{24,32},{40,48},{56,64},{72,80},{88,96},{104,112},{120,128}... | collective-permute-start | bytes 159752 | tf_op jit(solution)/shard_map/ppermute | solution.py:612
  16.6 0.1 copy.12.upstream
  16.7 0.3 shard_map.114
  17.0 1.9 %collective-permute-start.1 = (f32[104,128]{1,0:T(8,128)S(1)}, f32[104,128]{1,0:T(8,128)S(1)}, u32[]{:S(2)}, u32[]{:S(2)}) collective-permute-start(f32[104,128]{1,0:T(8,128)S(1)} %get-tuple-element.77), channel_id=1, source_target_pairs={{0,8},{8,0},{16,24},{24,16},{32,40},{40,32},{48,56},{56,48},{64,72... | collective-permute-start | bytes 159752 | tf_op jit(solution)/shard_map/ppermute | solution.py:611
  18.9 0.0 collective-permute-done.over.refs_7_
  18.9 1.2 %collective-permute-done.1.near.refs_6_ = f32[104,128]{1,0:T(8,128)S(1)} collective-permute-done((f32[104,128]{1,0:T(8,128)S(1)}, f32[104,128]{1,0:T(8,128)S(1)}, u32[]{:S(2)}, u32[]{:S(2)}) %collective-permute-start.1) | collective-permute-done | bytes 53280 | tf_op jit(solution)/shard_map/ppermute | solution.py:611
  20.2 0.0 copy-start.3
  20.2 16.3 %all_to_all.20.refs_5_.got_first = f32[8,32,128]{2,1,0:T(8,128)S(1)} all-to-all(f32[8,32,128]{2,1,0:T(8,128)S(1)} %shard_map.115), channel_id=1, replica_groups=mesh['gx'=96,'gy'=8] {'gy'}, dimensions={0} | all-to-all | bytes 262144 | tf_op jit(solution)/shard_map/all_to_all | solution.py:616
  36.5 1.5 %shard_map.116 = (f32[3,32,512]{2,1,0:T(8,128)S(1)}, f32[24,128]{1,0:T(8,128)S(1)}, f32[40,128]{1,0:T(8,128)S(1)}, f32[40,128]{1,0:T(8,128)S(1)}, f32[32,128]{1,...) custom-call(f32[32,512]{1,0:T(8,128)S(1)} %copy-done.2, ...), custom_call_target="tpu_custom_call" | custom-call | tf_op jit(solution)/shard_map/pallas_call | solution.py:573
  37.9 3.0 %collective-permute-start.2 = (f32[40,128]{1,0:T(8,128)S(1)}, f32[40,128]{1,0:T(8,128)S(1)}, u32[]{:S(2)}, u32[]{:S(2)}) collective-permute-start(f32[40,128]{1,0:T(8,128)S(1)} %get-tuple-element.97), channel_id=1, source_target_pairs={{8,16},{24,32},{40,48},{56,64},{72,80},{88,96},{104,112},{120,128}... | collective-permute-start | bytes 61448 | tf_op jit(solution)/shard_map/ppermute | solution.py:612
  40.9 0.4 shard_map.117
  41.4 1.9 %collective-permute-start.3 = (f32[40,128]{1,0:T(8,128)S(1)}, f32[40,128]{1,0:T(8,128)S(1)}, u32[]{:S(2)}, u32[]{:S(2)}) collective-permute-start(f32[40,128]{1,0:T(8,128)S(1)} %get-tuple-element.100), channel_id=1, source_target_pairs={{0,8},{8,0},{16,24},{24,16},{32,40},{40,32},{48,56},{56,48},{64,72... | collective-permute-start | bytes 61448 | tf_op jit(solution)/shard_map/ppermute | solution.py:611
  43.3 1.9 %collective-permute-done.2.over.refs_8_ = f32[40,128]{1,0:T(8,128)S(1)} collective-permute-done((f32[40,128]{1,0:T(8,128)S(1)}, f32[40,128]{1,0:T(8,128)S(1)}, u32[]{:S(2)}, u32[]{:S(2)}) %collective-permute-start.2) | collective-permute-done | bytes 20512 | tf_op jit(solution)/shard_map/ppermute | solution.py:612
  45.1 0.0 collective-permute-done.3.near.refs_7_
  45.2 10.4 %all_to_all.21.refs_6_ = f32[8,8,128]{2,1,0:T(8,128)S(1)} all-to-all(f32[8,8,128]{2,1,0:T(8,128)S(1)} %shard_map.118), channel_id=1, replica_groups=mesh['gx'=96,'gy'=8] {'gy'}, dimensions={0} | all-to-all | bytes 65536 | tf_op jit(solution)/shard_map/all_to_all | solution.py:616
  55.6 1.4 %shard_map.119 = (f32[3,32,512]{2,1,0:T(8,128)S(1)}, f32[24,128]{1,0:T(8,128)S(1)}, f32[40,128]{1,0:T(8,128)S(1)}, f32[40,128]{1,0:T(8,128)S(1)}, f32[32,128]{1,...) custom-call(f32[3,32,512]{2,1,0:T(8,128)S(1)} %get-tuple-element.88.state.refs_0_, ...), custom_call_target="tpu_custom_call" | custom-call | tf_op jit(solution)/shard_map/pallas_call | solution.py:573
  56.9 2.8 %collective-permute-start.4 = (f32[40,128]{1,0:T(8,128)S(1)}, f32[40,128]{1,0:T(8,128)S(1)}, u32[]{:S(2)}, u32[]{:S(2)}) collective-permute-start(f32[40,128]{1,0:T(8,128)S(1)} %get-tuple-element.113), channel_id=1, source_target_pairs={{8,16},{24,32},{40,48},{56,64},{72,80},{88,96},{104,112},{120,128}... | collective-permute-start | bytes 61448 | tf_op jit(solution)/shard_map/ppermute | solution.py:612
  59.8 0.2 shard_map.120.refs_9_
  60.0 1.9 %collective-permute-start.5 = (f32[40,128]{1,0:T(8,128)S(1)}, f32[40,128]{1,0:T(8,128)S(1)}, u32[]{:S(2)}, u32[]{:S(2)}) collective-permute-start(f32[40,128]{1,0:T(8,128)S(1)} %get-tuple-element.115), channel_id=1, source_target_pairs={{0,8},{8,0},{16,24},{24,16},{32,40},{40,32},{48,56},{56,48},{64,72... | collective-permute-start | bytes 61448 | tf_op jit(solution)/shard_map/ppermute | solution.py:611
  61.9 2.2 %collective-permute-done.4.over.refs_8_ = f32[40,128]{1,0:T(8,128)S(1)} collective-permute-done((f32[40,128]{1,0:T(8,128)S(1)}, f32[40,128]{1,0:T(8,128)S(1)}, u32[]{:S(2)}, u32[]{:S(2)}) %collective-permute-start.4) | collective-permute-done | bytes 20512 | tf_op jit(solution)/shard_map/ppermute | solution.py:612
  64.2 10.4 %all_to_all.22.refs_6_ = f32[8,8,128]{2,1,0:T(8,128)S(1)} all-to-all(f32[8,8,128]{2,1,0:T(8,128)S(1)} %shard_map.121), channel_id=1, replica_groups=mesh['gx'=96,'gy'=8] {'gy'}, dimensions={0} | all-to-all | bytes 65536 | tf_op jit(solution)/shard_map/all_to_all | solution.py:616
  74.6 1.3 %shard_map.122 = (f32[3,32,512]{2,1,0:T(8,128)S(1)}, f32[24,128]{1,0:T(8,128)S(1)}, f32[40,128]{1,0:T(8,128)S(1)}, f32[40,128]{1,0:T(8,128)S(1)}, f32[32,128]{1,0:T(8,128)S(1)}) custom-call(f32[3,32,512]{2,1,0:T(8,128)S(1)} %get-tuple-element.107.state.refs_0_, f32[8,128]{1,0:T(8,128)S(1)} %get-tuple-element.108.refs_1_, ...), custom_call_target="tpu_custom_call" | custom-call | tf_op jit(solution)/shard_map/pallas_call | solution.py:573
  75.9 2.6 %collective-permute-start.6 = (f32[40,128]{1,0:T(8,128)S(1)}, f32[40,128]{1,0:T(8,128)S(1)}, u32[]{:S(2)}, u32[]{:S(2)}) collective-permute-start(f32[40,128]{1,0:T(8,128)S(1)} %get-tuple-element.127), channel_id=1, source_target_pairs={{8,16},{24,32},{40,48},{56,64},{72,80},{88,96},{104,112},{120,128}... | collective-permute-start | bytes 61448 | tf_op jit(solution)/shard_map/ppermute | solution.py:612
  78.6 0.2 shard_map.123.base
  78.8 1.9 %collective-permute-start.7 = (f32[40,128]{1,0:T(8,128)S(1)}, f32[40,128]{1,0:T(8,128)S(1)}, u32[]{:S(2)}, u32[]{:S(2)}) collective-permute-start(f32[40,128]{1,0:T(8,128)S(1)} %get-tuple-element.129), channel_id=1, source_target_pairs={{0,8},{8,0},{16,24},{24,16},{32,40},{40,32},{48,56},{56,48},{64,72... | collective-permute-start | bytes 61448 | tf_op jit(solution)/shard_map/ppermute | solution.py:611
  80.8 2.4 %collective-permute-done.6.over = f32[40,128]{1,0:T(8,128)S(1)} collective-permute-done((f32[40,128]{1,0:T(8,128)S(1)}, f32[40,128]{1,0:T(8,128)S(1)}, u32[]{:S(2)}, u32[]{:S(2)}) %collective-permute-start.6) | collective-permute-done | bytes 20512 | tf_op jit(solution)/shard_map/ppermute | solution.py:612
  83.2 0.0 collective-permute-done.7.near
  83.2 11.8 %all_to_all.23.got = f32[8,40,128]{2,1,0:T(8,128)S(1)} all-to-all(f32[8,40,128]{2,1,0:T(8,128)S(1)} %shard_map.124), channel_id=1, replica_groups=mesh['gx'=96,'gy'=8] {'gy'}, dimensions={0} | all-to-all | bytes 327680 | tf_op jit(solution)/shard_map/all_to_all | solution.py:616
  95.0 2.8 %shard_map.125 = (f32[3,32,512]{2,1,0:T(8,128)}, f32[8,1024]{1,0:T(8,128)}) custom-call(f32[3,32,512]{2,1,0:T(8,128)S(1)} %get-tuple-element.123.state, f32[8,40,128]{2,1,0:T(8,128)S(1)} %all_to_all.23.got, f32[40,128]{1,0:T(8,128)S(1)} %collective-permute-done.7.near, f32[40,128]{1,0:T(8,128)S(1)} %collective-permute-done.6.over, ...), custom_call_target="tpu_custom_call" | custom-call | tf_op jit(solution)/shard_map/pallas_call | solution.py:573
  (16 shorter events, 0.2 us)
Async XLA Ops:
  0.6 16.0 %copy-start = (f32[2,32,512]{2,1,0:T(8,128)S(1)}, f32[2,32,512]{2,1,0:T(8,128)}, u32[]{:S(2)}) copy-start(f32[2,32,512]{2,1,0:T(8,128)} %refs_1_.3) | copy-start | bytes 393220
  0.6 16.0 %copy-start.2 = (f32[32,512]{1,0:T(8,128)S(1)}, f32[32,512]{1,0:T(8,128)}, u32[]{:S(2)}) copy-start(f32[32,512]{1,0:T(8,128)} %refs_0_.3) | copy-start | bytes 196612
  0.7 16.0 %copy-start.1 = (f32[32,512]{1,0:T(8,128)S(1)}, f32[32,512]{1,0:T(8,128)}, u32[]{:S(2)}) copy-start(f32[32,512]{1,0:T(8,128)} %rough.7) | copy-start | bytes 196612
  0.7 15.9 %copy-start.6 = (s32[8,2]{0,1:T(2,128)S(1)}, s32[8,2]{0,1:T(2,128)}, u32[]{:S(2)}) copy-start(s32[8,2]{0,1:T(2,128)} %param.16) | copy-start | bytes 196
  2.2 14.4 %copy-start.4 = (f32[8,8]{1,0:T(8,128)S(1)}, f32[8,8]{1,0:T(8,128)}, u32[]{:S(2)}) copy-start(f32[8,8]{1,0:T(8,128)} %celerity.1) | copy-start | bytes 772
  2.3 14.4 %copy-start.5 = (f32[8,8]{1,0:T(8,128)S(1)}, f32[8,8]{1,0:T(8,128)}, u32[]{:S(2)}) copy-start(f32[8,8]{1,0:T(8,128)} %base_inflow.1) | copy-start | bytes 772
  2.3 16.7 %collective-permute-start = (f32[104,128]{1,0:T(8,128)S(1)}, f32[104,128]{1,0:T(8,128)S(1)}, u32[]{:S(2)}, u32[]{:S(2)}) collective-permute-start(f32[104,128]{1,0:T(8,128)S(1)} %get-tuple-element.73), channel_id=1, source_target_pairs={{8,16},{24,32},{40,48},{56,64},{72,80},{88,96},{104,112},{120,128}... | collective-permute-start | bytes 159752 | tf_op jit(solution)/shard_map/ppermute | solution.py:612
  17.0 3.1 %collective-permute-start.1 = (f32[104,128]{1,0:T(8,128)S(1)}, f32[104,128]{1,0:T(8,128)S(1)}, u32[]{:S(2)}, u32[]{:S(2)}) collective-permute-start(f32[104,128]{1,0:T(8,128)S(1)} %get-tuple-element.77), channel_id=1, source_target_pairs={{0,8},{8,0},{16,24},{24,16},{32,40},{40,32},{48,56},{56,48},{64,72... | collective-permute-start | bytes 159752 | tf_op jit(solution)/shard_map/ppermute | solution.py:611
  20.2 16.3 %copy-start.3 = (f32[8,1024]{1,0:T(8,128)S(1)}, f32[8,1024]{1,0:T(8,128)}, u32[]{:S(2)}) copy-start(f32[8,1024]{1,0:T(8,128)} %refs_2_.3) | copy-start | bytes 98308
  37.9 7.2 %collective-permute-start.2 = (f32[40,128]{1,0:T(8,128)S(1)}, f32[40,128]{1,0:T(8,128)S(1)}, u32[]{:S(2)}, u32[]{:S(2)}) collective-permute-start(f32[40,128]{1,0:T(8,128)S(1)} %get-tuple-element.97), channel_id=1, source_target_pairs={{8,16},{24,32},{40,48},{56,64},{72,80},{88,96},{104,112},{120,128}... | collective-permute-start | bytes 61448 | tf_op jit(solution)/shard_map/ppermute | solution.py:612
  41.4 3.8 %collective-permute-start.3 = (f32[40,128]{1,0:T(8,128)S(1)}, f32[40,128]{1,0:T(8,128)S(1)}, u32[]{:S(2)}, u32[]{:S(2)}) collective-permute-start(f32[40,128]{1,0:T(8,128)S(1)} %get-tuple-element.100), channel_id=1, source_target_pairs={{0,8},{8,0},{16,24},{24,16},{32,40},{40,32},{48,56},{56,48},{64,72... | collective-permute-start | bytes 61448 | tf_op jit(solution)/shard_map/ppermute | solution.py:611
  56.9 7.2 %collective-permute-start.4 = (f32[40,128]{1,0:T(8,128)S(1)}, f32[40,128]{1,0:T(8,128)S(1)}, u32[]{:S(2)}, u32[]{:S(2)}) collective-permute-start(f32[40,128]{1,0:T(8,128)S(1)} %get-tuple-element.113), channel_id=1, source_target_pairs={{8,16},{24,32},{40,48},{56,64},{72,80},{88,96},{104,112},{120,128}... | collective-permute-start | bytes 61448 | tf_op jit(solution)/shard_map/ppermute | solution.py:612
  60.0 4.1 %collective-permute-start.5 = (f32[40,128]{1,0:T(8,128)S(1)}, f32[40,128]{1,0:T(8,128)S(1)}, u32[]{:S(2)}, u32[]{:S(2)}) collective-permute-start(f32[40,128]{1,0:T(8,128)S(1)} %get-tuple-element.115), channel_id=1, source_target_pairs={{0,8},{8,0},{16,24},{24,16},{32,40},{40,32},{48,56},{56,48},{64,72... | collective-permute-start | bytes 61448 | tf_op jit(solution)/shard_map/ppermute | solution.py:611
  75.9 7.2 %collective-permute-start.6 = (f32[40,128]{1,0:T(8,128)S(1)}, f32[40,128]{1,0:T(8,128)S(1)}, u32[]{:S(2)}, u32[]{:S(2)}) collective-permute-start(f32[40,128]{1,0:T(8,128)S(1)} %get-tuple-element.127), channel_id=1, source_target_pairs={{8,16},{24,32},{40,48},{56,64},{72,80},{88,96},{104,112},{120,128}... | collective-permute-start | bytes 61448 | tf_op jit(solution)/shard_map/ppermute | solution.py:612
  78.8 4.3 %collective-permute-start.7 = (f32[40,128]{1,0:T(8,128)S(1)}, f32[40,128]{1,0:T(8,128)S(1)}, u32[]{:S(2)}, u32[]{:S(2)}) collective-permute-start(f32[40,128]{1,0:T(8,128)S(1)} %get-tuple-element.129), channel_id=1, source_target_pairs={{0,8},{8,0},{16,24},{24,16},{32,40},{40,32},{48,56},{56,48},{64,72... | collective-permute-start | bytes 61448 | tf_op jit(solution)/shard_map/ppermute | solution.py:611

commit v11 on v8

--- a/solution.py
+++ b/solution.py
@@ -444,8 +444,15 @@
     total[...] = spread(owner_coeff[...], site >> 7, site & (LANES - 1), FIELDS)
 
 
+def flow_and_sites(state, rough, got_first, base, sites):
+    flow(state, rough, base)
+    for b in range(BASINS):
+        site = jnp.concatenate([got_first[:, 8 + 8 * v + b, :] for v in range(3)], axis=0)
+        sites[b] = site.astype(jnp.int32)
+
+
 def last_kernel(
-    state, got, near, over, base, cell_ref, coeff_ref, slots_ref, got_first, terms, state_out, reach_out
+    state, got, near, over, base, cell_ref, coeff_ref, slots_ref, sites, terms, state_out, reach_out
 ):
     cells = [state[0], state[1], state[2]]
     edges = get_edges(got, near, over, cells, place(), EDGE, 6)
@@ -458,8 +465,7 @@
     lane = iota((FIELDS, LANES), 1)
     for b in range(BASINS):
         own = terms[b]
-        site = jnp.concatenate([got_first[:, 8 + 8 * v + b, :] for v in range(3)], axis=0)
-        site = site.astype(jnp.int32)
+        site = sites[b]
         held = jnp.concatenate([got[:, 8 + 8 * v + b, :] for v in range(3)], axis=0)
         drawn = spread(held, site >> 7, site & (LANES - 1), FIELDS)
         entering = jnp.where(lane == 0, own[0:8] * inflow_of(own, outlets), 0.0)
@@ -674,15 +680,25 @@
                 [f32(3, ROWS, COLS), f32(FIELDS, LANES)],
                 [state, roughness, owner_coeff, owner_site],
             )
+        elif tail:
+            base, sites = call(
+                flow_and_sites,
+                [f32(3, ROWS, COLS), i32(BASINS, SLOT_ROWS, LANES)],
+                [state, roughness, got_first],
+            )
         else:
             base = call(flow, [f32(3, ROWS, COLS)], [state, roughness])[0]
-        got, near, over, base = exchange(
-            last_pack if tail else pack, 40 if tail else BASINS, beside, across, mine, base
+        ready = (base, sites) if tail else (base,)
+        got, near, over, ready = exchange(
+            last_pack if tail else pack, 40 if tail else BASINS, beside, across, mine, ready
         )
+        base = ready[0]
+        if tail:
+            sites = ready[1]
     state, reach = call(
         last_kernel,
         [f32(3, ROWS, COLS), f32(BASINS, FIELDS * LANES)],
-        [state, got, near, over, base, cell, coeff, slots, got_first, terms],
+        [state, got, near, over, base, cell, coeff, slots, sites, terms],
     )
     return state, reach
 

time: 97.9 us -> 97.9 us (level)
  no operation moved by 1% of the time
where the time goes in v11:
time: 97.9 us; the launch traced here: 97.4 us
  blocking collectives  48.9 us (50%)
  starting transfers between devices  30.2 us (31%)
  Pallas kernels  9.91 us (10%)
  waiting for transfers between devices  7.44 us (8%)
    all_to_all x4, blocking collectives, exchange(): return (lax.all_to_all(send, 'gy', 0, 0), near, over, ready)  48.9 us
    ppermute x4, starting transfers between devices, exchange(): over = lax.ppermute(across, 'gx', border)  22.5 us
    pallas_call x12, Pallas kernels, call(): pl.pallas_call(kernel, out_shape=outs, in_specs=[pl.BlockSpec(memory_spac...  8.35 us
    ppermute x4, starting transfers between devices, exchange(): near = lax.ppermute(beside, 'gx', chip)  7.68 us
    ppermute x4, waiting for transfers between devices, exchange(): over = lax.ppermute(across, 'gx', border)  6.67 us
  transfers between devices with their start and end apart: 8, of which 4 were waited for; matrix products, arithmetic and copies ran while one was open for 0% of the time, Pallas kernels for 1%

profile of v11, /device:TPU:6, one launch (start us, length us, event | category | flops | bytes accessed | tf_op | source)
XLA Modules:
  0.0 97.4 jit_solution(16947996754315544379)
XLA Ops:
  0.7 1.6 %shard_map.113 = (f32[104,128]{1,0:T(8,128)S(1)}, f32[104,128]{1,0:T(8,128)S(1)}, f32[32,128]{1,0:T(8,128)S(1)}, s32[24,128]{1,0:T(8,128)S(1)}, s32[24,128]{1,0:...) custom-call(f32[32,512]{1,0:T(8,128)} %refs_0_.3, f32[2,32,512]{2,1,0:T(8,128)} %refs_1_.3, ...), custom_call_target="tpu_custom_call" | custom-call | tf_op jit(solution)/shard_map/pallas_call | solution.py:635
  2.2 0.0 copy-start.4
  2.3 0.0 copy-start.5
  2.3 14.3 %collective-permute-start = (f32[104,128]{1,0:T(8,128)S(1)}, f32[104,128]{1,0:T(8,128)S(1)}, u32[]{:S(2)}, u32[]{:S(2)}) collective-permute-start(f32[104,128]{1,0:T(8,128)S(1)} %get-tuple-element.67), channel_id=1, source_target_pairs={{8,16},{24,32},{40,48},{56,64},{72,80},{88,96},{104,112},{120,128}... | collective-permute-start | bytes 159752 | tf_op jit(solution)/shard_map/ppermute | solution.py:617
  16.6 1.9 %collective-permute-start.1 = (f32[104,128]{1,0:T(8,128)S(1)}, f32[104,128]{1,0:T(8,128)S(1)}, u32[]{:S(2)}, u32[]{:S(2)}) collective-permute-start(f32[104,128]{1,0:T(8,128)S(1)} %get-tuple-element.68), channel_id=1, source_target_pairs={{0,8},{8,0},{16,24},{24,16},{32,40},{40,32},{48,56},{56,48},{64,72... | collective-permute-start | bytes 159752 | tf_op jit(solution)/shard_map/ppermute | solution.py:616
  18.5 0.1 copy.12.upstream
  18.6 0.3 shard_map.115
  18.9 0.0 collective-permute-done.over.refs_7_
  18.9 0.8 collective-permute-done.1.near.refs_6_
  19.7 0.0 copy-start.3
  19.8 16.3 %all_to_all.20.refs_5_.got_first = f32[8,32,128]{2,1,0:T(8,128)S(1)} all-to-all(f32[8,32,128]{2,1,0:T(8,128)S(1)} %shard_map.114), channel_id=1, replica_groups=mesh['gx'=96,'gy'=8] {'gy'}, dimensions={0} | all-to-all | bytes 262144 | tf_op jit(solution)/shard_map/all_to_all | solution.py:621
  36.0 1.5 %shard_map.116 = (f32[3,32,512]{2,1,0:T(8,128)S(1)}, f32[24,128]{1,0:T(8,128)S(1)}, f32[40,128]{1,0:T(8,128)S(1)}, f32[40,128]{1,0:T(8,128)S(1)}, f32[32,128]{1,...) custom-call(f32[32,512]{1,0:T(8,128)S(1)} %copy-done.2, ...), custom_call_target="tpu_custom_call" | custom-call | tf_op jit(solution)/shard_map/pallas_call | solution.py:579
  37.5 3.4 %collective-permute-start.2 = (f32[40,128]{1,0:T(8,128)S(1)}, f32[40,128]{1,0:T(8,128)S(1)}, u32[]{:S(2)}, u32[]{:S(2)}) collective-permute-start(f32[40,128]{1,0:T(8,128)S(1)} %get-tuple-element.88), channel_id=1, source_target_pairs={{8,16},{24,32},{40,48},{56,64},{72,80},{88,96},{104,112},{120,128}... | collective-permute-start | bytes 61448 | tf_op jit(solution)/shard_map/ppermute | solution.py:617
  40.9 1.9 %collective-permute-start.3 = (f32[40,128]{1,0:T(8,128)S(1)}, f32[40,128]{1,0:T(8,128)S(1)}, u32[]{:S(2)}, u32[]{:S(2)}) collective-permute-start(f32[40,128]{1,0:T(8,128)S(1)} %get-tuple-element.89), channel_id=1, source_target_pairs={{0,8},{8,0},{16,24},{24,16},{32,40},{40,32},{48,56},{56,48},{64,72... | collective-permute-start | bytes 61448 | tf_op jit(solution)/shard_map/ppermute | solution.py:616
  42.8 0.4 shard_map.118
  43.3 1.5 %collective-permute-done.2.over.refs_8_ = f32[40,128]{1,0:T(8,128)S(1)} collective-permute-done((f32[40,128]{1,0:T(8,128)S(1)}, f32[40,128]{1,0:T(8,128)S(1)}, u32[]{:S(2)}, u32[]{:S(2)}) %collective-permute-start.2) | collective-permute-done | bytes 20512 | tf_op jit(solution)/shard_map/ppermute | solution.py:617
  44.7 0.0 collective-permute-done.3.near.refs_7_
  44.8 10.4 %all_to_all.21.refs_6_ = f32[8,8,128]{2,1,0:T(8,128)S(1)} all-to-all(f32[8,8,128]{2,1,0:T(8,128)S(1)} %shard_map.117), channel_id=1, replica_groups=mesh['gx'=96,'gy'=8] {'gy'}, dimensions={0} | all-to-all | bytes 65536 | tf_op jit(solution)/shard_map/all_to_all | solution.py:621
  55.2 1.4 %shard_map.119 = (f32[3,32,512]{2,1,0:T(8,128)S(1)}, f32[24,128]{1,0:T(8,128)S(1)}, f32[40,128]{1,0:T(8,128)S(1)}, f32[40,128]{1,0:T(8,128)S(1)}, f32[32,128]{1,...) custom-call(f32[3,32,512]{2,1,0:T(8,128)S(1)} %get-tuple-element.79.state.refs_0_, ...), custom_call_target="tpu_custom_call" | custom-call | tf_op jit(solution)/shard_map/pallas_call | solution.py:579
  56.5 2.4 %collective-permute-start.4 = (f32[40,128]{1,0:T(8,128)S(1)}, f32[40,128]{1,0:T(8,128)S(1)}, u32[]{:S(2)}, u32[]{:S(2)}) collective-permute-start(f32[40,128]{1,0:T(8,128)S(1)} %get-tuple-element.102), channel_id=1, source_target_pairs={{8,16},{24,32},{40,48},{56,64},{72,80},{88,96},{104,112},{120,128}... | collective-permute-start | bytes 61448 | tf_op jit(solution)/shard_map/ppermute | solution.py:617
  58.9 1.9 %collective-permute-start.5 = (f32[40,128]{1,0:T(8,128)S(1)}, f32[40,128]{1,0:T(8,128)S(1)}, u32[]{:S(2)}, u32[]{:S(2)}) collective-permute-start(f32[40,128]{1,0:T(8,128)S(1)} %get-tuple-element.103), channel_id=1, source_target_pairs={{0,8},{8,0},{16,24},{24,16},{32,40},{40,32},{48,56},{56,48},{64,72... | collective-permute-start | bytes 61448 | tf_op jit(solution)/shard_map/ppermute | solution.py:616
  60.9 0.2 shard_map.121.refs_9_
  61.1 2.6 %collective-permute-done.4.over.refs_8_ = f32[40,128]{1,0:T(8,128)S(1)} collective-permute-done((f32[40,128]{1,0:T(8,128)S(1)}, f32[40,128]{1,0:T(8,128)S(1)}, u32[]{:S(2)}, u32[]{:S(2)}) %collective-permute-start.4) | collective-permute-done | bytes 20512 | tf_op jit(solution)/shard_map/ppermute | solution.py:617
  63.8 10.4 %all_to_all.22.refs_6_ = f32[8,8,128]{2,1,0:T(8,128)S(1)} all-to-all(f32[8,8,128]{2,1,0:T(8,128)S(1)} %shard_map.120), channel_id=1, replica_groups=mesh['gx'=96,'gy'=8] {'gy'}, dimensions={0} | all-to-all | bytes 65536 | tf_op jit(solution)/shard_map/all_to_all | solution.py:621
  74.2 1.3 %shard_map.122 = (f32[3,32,512]{2,1,0:T(8,128)S(1)}, f32[24,128]{1,0:T(8,128)S(1)}, f32[40,128]{1,0:T(8,128)S(1)}, f32[40,128]{1,0:T(8,128)S(1)}, f32[32,128]{1,0:T(8,128)S(1)}) custom-call(f32[3,32,512]{2,1,0:T(8,128)S(1)} %get-tuple-element.96.state.refs_0_, f32[8,128]{1,0:T(8,128)S(1)} %get-tuple-element.97.refs_1_, ...), custom_call_target="tpu_custom_call" | custom-call | tf_op jit(solution)/shard_map/pallas_call | solution.py:579
  75.5 2.4 %collective-permute-start.6 = (f32[40,128]{1,0:T(8,128)S(1)}, f32[40,128]{1,0:T(8,128)S(1)}, u32[]{:S(2)}, u32[]{:S(2)}) collective-permute-start(f32[40,128]{1,0:T(8,128)S(1)} %get-tuple-element.114), channel_id=1, source_target_pairs={{8,16},{24,32},{40,48},{56,64},{72,80},{88,96},{104,112},{120,128}... | collective-permute-start | bytes 61448 | tf_op jit(solution)/shard_map/ppermute | solution.py:617
  77.9 1.9 %collective-permute-start.7 = (f32[40,128]{1,0:T(8,128)S(1)}, f32[40,128]{1,0:T(8,128)S(1)}, u32[]{:S(2)}, u32[]{:S(2)}) collective-permute-start(f32[40,128]{1,0:T(8,128)S(1)} %get-tuple-element.115), channel_id=1, source_target_pairs={{0,8},{8,0},{16,24},{24,16},{32,40},{40,32},{48,56},{56,48},{64,72... | collective-permute-start | bytes 61448 | tf_op jit(solution)/shard_map/ppermute | solution.py:616
  79.9 0.3 shard_map.124
  80.2 2.6 %collective-permute-done.6.over = f32[40,128]{1,0:T(8,128)S(1)} collective-permute-done((f32[40,128]{1,0:T(8,128)S(1)}, f32[40,128]{1,0:T(8,128)S(1)}, u32[]{:S(2)}, u32[]{:S(2)}) %collective-permute-start.6) | collective-permute-done | bytes 20512 | tf_op jit(solution)/shard_map/ppermute | solution.py:617
  82.7 0.0 collective-permute-done.7.near
  82.8 11.8 %all_to_all.23.got = f32[8,40,128]{2,1,0:T(8,128)S(1)} all-to-all(f32[8,40,128]{2,1,0:T(8,128)S(1)} %shard_map.123), channel_id=1, replica_groups=mesh['gx'=96,'gy'=8] {'gy'}, dimensions={0} | all-to-all | bytes 327680 | tf_op jit(solution)/shard_map/all_to_all | solution.py:621
  94.6 2.8 %shard_map.125 = (f32[3,32,512]{2,1,0:T(8,128)}, f32[8,1024]{1,0:T(8,128)}) custom-call(f32[3,32,512]{2,1,0:T(8,128)S(1)} %get-tuple-element.110.state, f32[8,40,128]{2,1,0:T(8,128)S(1)} %all_to_all.23.got, f32[40,128]{1,0:T(8,128)S(1)} %collective-permute-done.7.near, f32[40,128]{1,0:T(8,128)S(1)} %collective-permute-done.6.over, ...), custom_call_target="tpu_custom_call" | custom-call | tf_op jit(solution)/shard_map/pallas_call | solution.py:579
  (16 shorter events, 0.2 us)
Async XLA Ops:
  0.6 18.0 %copy-start = (f32[2,32,512]{2,1,0:T(8,128)S(1)}, f32[2,32,512]{2,1,0:T(8,128)}, u32[]{:S(2)}) copy-start(f32[2,32,512]{2,1,0:T(8,128)} %refs_1_.3) | copy-start | bytes 393220
  0.6 18.0 %copy-start.2 = (f32[32,512]{1,0:T(8,128)S(1)}, f32[32,512]{1,0:T(8,128)}, u32[]{:S(2)}) copy-start(f32[32,512]{1,0:T(8,128)} %refs_0_.3) | copy-start | bytes 196612
  0.7 17.9 %copy-start.1 = (f32[32,512]{1,0:T(8,128)S(1)}, f32[32,512]{1,0:T(8,128)}, u32[]{:S(2)}) copy-start(f32[32,512]{1,0:T(8,128)} %rough.7) | copy-start | bytes 196612
  0.7 17.8 %copy-start.6 = (s32[8,2]{0,1:T(2,128)S(1)}, s32[8,2]{0,1:T(2,128)}, u32[]{:S(2)}) copy-start(s32[8,2]{0,1:T(2,128)} %param.16) | copy-start | bytes 196
  2.2 16.4 %copy-start.4 = (f32[8,8]{1,0:T(8,128)S(1)}, f32[8,8]{1,0:T(8,128)}, u32[]{:S(2)}) copy-start(f32[8,8]{1,0:T(8,128)} %celerity.1) | copy-start | bytes 772
  2.3 16.3 %copy-start.5 = (f32[8,8]{1,0:T(8,128)S(1)}, f32[8,8]{1,0:T(8,128)}, u32[]{:S(2)}) copy-start(f32[8,8]{1,0:T(8,128)} %base_inflow.1) | copy-start | bytes 772
  2.3 16.7 %collective-permute-start = (f32[104,128]{1,0:T(8,128)S(1)}, f32[104,128]{1,0:T(8,128)S(1)}, u32[]{:S(2)}, u32[]{:S(2)}) collective-permute-start(f32[104,128]{1,0:T(8,128)S(1)} %get-tuple-element.67), channel_id=1, source_target_pairs={{8,16},{24,32},{40,48},{56,64},{72,80},{88,96},{104,112},{120,128}... | collective-permute-start | bytes 159752 | tf_op jit(solution)/shard_map/ppermute | solution.py:617
  16.6 3.1 %collective-permute-start.1 = (f32[104,128]{1,0:T(8,128)S(1)}, f32[104,128]{1,0:T(8,128)S(1)}, u32[]{:S(2)}, u32[]{:S(2)}) collective-permute-start(f32[104,128]{1,0:T(8,128)S(1)} %get-tuple-element.68), channel_id=1, source_target_pairs={{0,8},{8,0},{16,24},{24,16},{32,40},{40,32},{48,56},{56,48},{64,72... | collective-permute-start | bytes 159752 | tf_op jit(solution)/shard_map/ppermute | solution.py:616
  19.7 16.3 %copy-start.3 = (f32[8,1024]{1,0:T(8,128)S(1)}, f32[8,1024]{1,0:T(8,128)}, u32[]{:S(2)}) copy-start(f32[8,1024]{1,0:T(8,128)} %refs_2_.3) | copy-start | bytes 98308
  37.5 7.2 %collective-permute-start.2 = (f32[40,128]{1,0:T(8,128)S(1)}, f32[40,128]{1,0:T(8,128)S(1)}, u32[]{:S(2)}, u32[]{:S(2)}) collective-permute-start(f32[40,128]{1,0:T(8,128)S(1)} %get-tuple-element.88), channel_id=1, source_target_pairs={{8,16},{24,32},{40,48},{56,64},{72,80},{88,96},{104,112},{120,128}... | collective-permute-start | bytes 61448 | tf_op jit(solution)/shard_map/ppermute | solution.py:617
  40.9 3.8 %collective-permute-start.3 = (f32[40,128]{1,0:T(8,128)S(1)}, f32[40,128]{1,0:T(8,128)S(1)}, u32[]{:S(2)}, u32[]{:S(2)}) collective-permute-start(f32[40,128]{1,0:T(8,128)S(1)} %get-tuple-element.89), channel_id=1, source_target_pairs={{0,8},{8,0},{16,24},{24,16},{32,40},{40,32},{48,56},{56,48},{64,72... | collective-permute-start | bytes 61448 | tf_op jit(solution)/shard_map/ppermute | solution.py:616
  56.5 7.2 %collective-permute-start.4 = (f32[40,128]{1,0:T(8,128)S(1)}, f32[40,128]{1,0:T(8,128)S(1)}, u32[]{:S(2)}, u32[]{:S(2)}) collective-permute-start(f32[40,128]{1,0:T(8,128)S(1)} %get-tuple-element.102), channel_id=1, source_target_pairs={{8,16},{24,32},{40,48},{56,64},{72,80},{88,96},{104,112},{120,128}... | collective-permute-start | bytes 61448 | tf_op jit(solution)/shard_map/ppermute | solution.py:617
  58.9 4.8 %collective-permute-start.5 = (f32[40,128]{1,0:T(8,128)S(1)}, f32[40,128]{1,0:T(8,128)S(1)}, u32[]{:S(2)}, u32[]{:S(2)}) collective-permute-start(f32[40,128]{1,0:T(8,128)S(1)} %get-tuple-element.103), channel_id=1, source_target_pairs={{0,8},{8,0},{16,24},{24,16},{32,40},{40,32},{48,56},{56,48},{64,72... | collective-permute-start | bytes 61448 | tf_op jit(solution)/shard_map/ppermute | solution.py:616
  75.5 7.2 %collective-permute-start.6 = (f32[40,128]{1,0:T(8,128)S(1)}, f32[40,128]{1,0:T(8,128)S(1)}, u32[]{:S(2)}, u32[]{:S(2)}) collective-permute-start(f32[40,128]{1,0:T(8,128)S(1)} %get-tuple-element.114), channel_id=1, source_target_pairs={{8,16},{24,32},{40,48},{56,64},{72,80},{88,96},{104,112},{120,128}... | collective-permute-start | bytes 61448 | tf_op jit(solution)/shard_map/ppermute | solution.py:617
  77.9 4.8 %collective-permute-start.7 = (f32[40,128]{1,0:T(8,128)S(1)}, f32[40,128]{1,0:T(8,128)S(1)}, u32[]{:S(2)}, u32[]{:S(2)}) collective-permute-start(f32[40,128]{1,0:T(8,128)S(1)} %get-tuple-element.115), channel_id=1, source_target_pairs={{0,8},{8,0},{16,24},{24,16},{32,40},{40,32},{48,56},{56,48},{64,72... | collective-permute-start | bytes 61448 | tf_op jit(solution)/shard_map/ppermute | solution.py:616
